TPU v7x, 256 devices: a whole 4x4x8 slice. The times are simulated.
256 devices in a mesh: dp: 4 (over y_hi, core), dap: 64 (over z, x, y_lo).
Axes of the slice: x: 4, y: 4 (y_hi: 2, y_lo: 2; y = y_hi * 2 + y_lo), z: 8, core: 2. Of those that a mesh axis runs over, the one named last changes fastest.
Arguments:
- pair_input: bfloat16 [4, 128, 128, 128], P('dp', 'dap'), may hold values from -6 to 6
- cotangent: bfloat16 [4, 128, 128, 128], P('dp', 'dap'), may hold values from -6 to 6
- residue_mask: int32 [4, 128], P('dp'), may hold values from 0 to 1, as said below
- gain_start: float32 [128], replicated, may hold values from 0.5 to 1.5
- proj_start: float32 [128, 512], replicated, may hold values from -0.5 to 0.5
- bias_start: float32 [128, 4], replicated, may hold values from -0.5 to 0.5
- output_start: float32 [128, 128], replicated, may hold values from -0.5 to 0.5
- gain_end: float32 [128], replicated, may hold values from 0.5 to 1.5
- proj_end: float32 [128, 512], replicated, may hold values from -0.5 to 0.5
- bias_end: float32 [128, 4], replicated, may hold values from -0.5 to 0.5
- output_end: float32 [128, 128], replicated, may hold values from -0.5 to 0.5
- gain_transition: float32 [128], replicated, may hold values from 0.5 to 1.5
- transition_up: float32 [128, 512], replicated, may hold values from -0.5 to 0.5
- transition_down: float32 [512, 128], replicated, may hold values from -0.25 to 0.25
Outputs:
- grad_pair: bfloat16 [4, 128, 128, 128], P('dp', 'dap')
- grad_gain_start: float32 [128], replicated
- grad_proj_start: float32 [128, 512], replicated
- grad_bias_start: float32 [128, 4], replicated
- grad_output_start: float32 [128, 128], replicated
- grad_gain_end: float32 [128], replicated
- grad_proj_end: float32 [128, 512], replicated
- grad_bias_end: float32 [128, 4], replicated
- grad_output_end: float32 [128, 128], replicated
- grad_gain_transition: float32 [128], replicated
- grad_transition_up: float32 [128, 512], replicated
- grad_transition_down: float32 [512, 128], replicated
Inputs may be any that keep to these rules, and one draw needn't show every extreme that they name: `residue_mask`: row b is 1 on the first L residues of complex b and 0 after them, with L at least half of 128 and less than 128.
All inputs are finite; a program needn't handle non-finite values.
Results may differ from a plain program's by a relative error of at most 0.03.
Values may be sent and summed in bfloat16 or wider, within the bound.
No kernel may reach another device: no remote copies, remote signals or barrier semaphores. Data moves between devices by JAX's collectives and lax.ppermute only.
A program may use at most 64 MiB of HBM per device.

v0:
```python
import jax
import jax.numpy as jnp
from jax import lax
from jax.sharding import PartitionSpec as P

HEADS = 4


EPS = 1e-05
FULL_PRECISION = lax.Precision.HIGHEST


def normalize(pair_rows, scaling):
    widened = pair_rows.astype(jnp.float32)
    centre = widened - jnp.mean(widened, -1, keepdims=True)
    spread = jnp.mean(centre * centre, -1, keepdims=True)
    return (centre * lax.rsqrt(spread + EPS) * scaling).astype(jnp.bfloat16)


def plane_rows(pair_rows, scaling, w_bias):
    normed = normalize(pair_rows, scaling).astype(jnp.float32)
    return jnp.einsum("rkc,ch->hrk", normed, w_bias, precision=FULL_PRECISION).astype(jnp.bfloat16)


def attend(pair_rows, bias_plane, kept_keys, scaling, w_proj, w_out):
    row_count, col_count, channels = pair_rows.shape
    head_size = channels // HEADS
    head_shape = (row_count, col_count, HEADS, head_size)
    normed = normalize(pair_rows, scaling).reshape(row_count * col_count, channels)
    projected = jnp.dot(normed, w_proj.astype(jnp.bfloat16), preferred_element_type=jnp.float32)
    queries = (
        (projected[:, :channels] * head_size ** (-0.5)).astype(jnp.bfloat16).reshape(head_shape)
    )
    key_vectors = projected[:, channels : 2 * channels].astype(jnp.bfloat16).reshape(head_shape)
    values = projected[:, 2 * channels : 3 * channels].astype(jnp.bfloat16).reshape(head_shape)
    gating = jax.nn.sigmoid(projected[:, 3 * channels :])
    scores = (
        jnp.einsum("rjhd,rkhd->rhjk", queries, key_vectors, preferred_element_type=jnp.float32)
        + bias_plane
    )
    weights = jnp.exp(scores) * kept_keys
    attention = (weights / jnp.sum(weights, -1, keepdims=True)).astype(jnp.bfloat16)
    mixture = jnp.einsum("rhjk,rkhd->rjhd", attention, values, preferred_element_type=jnp.float32)
    gated_mix = (gating * mixture.reshape(row_count * col_count, channels)).astype(jnp.bfloat16)
    update = jnp.dot(gated_mix, w_out.astype(jnp.bfloat16), preferred_element_type=jnp.float32)
    return update.reshape(row_count, col_count, channels)


def transition(pair_rows, scaling, w_up, w_down):
    row_count, col_count, channels = pair_rows.shape
    normed = normalize(pair_rows, scaling).reshape(row_count * col_count, channels)
    widened = jnp.dot(normed, w_up.astype(jnp.bfloat16), preferred_element_type=jnp.float32)
    hidden = jax.nn.gelu(widened, approximate=False).astype(jnp.bfloat16)
    update = jnp.dot(hidden, w_down.astype(jnp.bfloat16), preferred_element_type=jnp.float32)
    return update.reshape(row_count, col_count, channels)


def flipped(pair_block):
    return jnp.transpose(pair_block, (1, 0, 2))


def local(
    pair_input,
    cotangent,
    residue_mask,
    gain_start,
    proj_start,
    bias_start,
    output_start,
    gain_end,
    proj_end,
    bias_end,
    output_end,
    gain_transition,
    transition_up,
    transition_down,
):
    pair_rows = pair_input[0]
    kept_keys = residue_mask[0].astype(jnp.float32)

    def attend_keys(pair_block, bias_plane, scaling, w_proj, w_out):
        return attend(pair_block, bias_plane, kept_keys, scaling, w_proj, w_out)

    attend_saved = jax.checkpoint(attend_keys)
    transition_saved = jax.checkpoint(transition)
    start_local, start_plane_pull = jax.vjp(plane_rows, pair_rows, gain_start, bias_start)
    start_plane = lax.all_gather(start_local, "dap", axis=1, tiled=True).astype(jnp.float32)
    start_update, start_pull = jax.vjp(
        attend_saved, pair_rows, start_plane, gain_start, proj_start, output_start
    )
    first_pair = (pair_rows.astype(jnp.float32) + start_update).astype(jnp.bfloat16)
    pair_moved, cotangent_moved = (
        lax.all_to_all(first_pair, "dap", split_axis=1, concat_axis=0, tiled=True),
        lax.all_to_all(cotangent[0], "dap", split_axis=1, concat_axis=0, tiled=True),
    )
    first_columns = flipped(pair_moved)
    cotangent_columns = flipped(cotangent_moved)
    end_local, end_plane_pull = jax.vjp(plane_rows, first_columns, gain_end, bias_end)
    end_plane = lax.all_gather(end_local, "dap", axis=1, tiled=True).astype(jnp.float32)
    end_update, end_pull = jax.vjp(
        attend_saved, first_columns, end_plane, gain_end, proj_end, output_end
    )
    second = (first_columns.astype(jnp.float32) + end_update).astype(jnp.bfloat16)
    transit_update, transition_pull = jax.vjp(
        transition_saved, second, gain_transition, transition_up, transition_down
    )
    transit_input_grad, transit_gain_grad, transit_up_grad, transit_down_grad = transition_pull(
        cotangent_columns.astype(jnp.float32)
    )
    second_grad = cotangent_columns + transit_input_grad
    end_input_grad, end_plane_grad, end_gain_grad, end_proj_grad, end_out_grad = end_pull(
        second_grad.astype(jnp.float32)
    )
    column_grad = second_grad + end_input_grad
    end_share = lax.psum_scatter(end_plane_grad, "dap", scatter_dimension=1, tiled=True).astype(
        jnp.bfloat16
    )
    crossed_input_grad, crossed_gain_grad, crossed_bias_grad = end_plane_pull(end_share)
    column_grad = column_grad + crossed_input_grad
    first_grad = lax.all_to_all(
        flipped(column_grad), "dap", split_axis=0, concat_axis=1, tiled=True
    )
    start_input_grad, start_plane_grad, start_gain_grad, start_proj_grad, start_out_grad = (
        start_pull(first_grad.astype(jnp.float32))
    )
    start_share = lax.psum_scatter(start_plane_grad, "dap", scatter_dimension=1, tiled=True).astype(
        jnp.bfloat16
    )
    plane_input_grad, plane_gain_grad, plane_bias_grad = start_plane_pull(start_share)
    grad_rows = first_grad + start_input_grad + plane_input_grad
    partials = (
        start_gain_grad + plane_gain_grad,
        start_proj_grad,
        plane_bias_grad,
        start_out_grad,
        end_gain_grad + crossed_gain_grad,
        end_proj_grad,
        crossed_bias_grad,
        end_out_grad,
        transit_gain_grad,
        transit_up_grad,
        transit_down_grad,
    )
    totals = lax.psum(
        (
            partials[0],
            partials[1],
            partials[2],
            partials[3],
            partials[4],
            partials[5],
            partials[6],
            partials[7],
            partials[8],
            partials[9],
            partials[10],
        ),
        ("dp", "dap"),
    )
    factor = 1.0 / (pair_input.shape[0] * lax.axis_size("dp") * pair_rows.shape[1])
    return (
        grad_rows[None],
        totals[0] * factor,
        totals[1] * factor,
        totals[2] * factor,
        totals[3] * factor,
        totals[4] * factor,
        totals[5] * factor,
        totals[6] * factor,
        totals[7] * factor,
        totals[8] * factor,
        totals[9] * factor,
        totals[10] * factor,
    )


def solution(mesh):
    in_specs = (
        P("dp", "dap", None, None),
        P("dp", "dap", None, None),
        P("dp", None),
        P(),
        P(),
        P(),
        P(),
        P(),
        P(),
        P(),
        P(),
        P(),
        P(),
        P(),
    )
    out_specs = (P("dp", "dap", None, None), P(), P(), P(), P(), P(), P(), P(), P(), P(), P(), P())
    return jax.shard_map(local, mesh=mesh, in_specs=in_specs, out_specs=out_specs, check_vma=False)
```

profile of v0, /device:TPU:1, one launch (start us, length us, event | category | flops | bytes accessed | tf_op | source)
XLA Modules:
  0.0 1341.3 jit_solution(5639806371261014355)
XLA Ops:
  7.2 0.7 convert_bitcast_fusion
  7.9 0.9 copy.190
  8.9 0.6 copy-done.14
  9.8 133.0 %all_gather.6 = bf16[4,128,128]{2,0,1:T(4,128)(2,1)S(1)} all-gather(bf16[4,2,128]{2,0,1:T(4,128)(2,1)S(1)} %fusion.29), channel_id=1, replica_groups=mesh['dp'=4,'dap'=64] {'dap'}, dimensions={1}, use_global_device_ids=true | all-gather | bytes 133120 | tf_op jit(solution)/shard_map/all_gather | solution.py:87
  142.9 0.7 copy-done.3
  145.1 0.7 copy-done.17
  146.1 0.8 copy.203
  146.9 4.6 all-to-all-start.1
  151.6 0.8 copy-done.8
  152.4 0.7 copy.397
  153.1 0.7 copy-done.18
  153.7 0.6 dynamic-slice
  155.0 6.0 all-to-all-done.1
  161.0 4.6 all-to-all-start
  166.0 0.6 copy-done.11
  167.0 129.7 %all_gather.7 = bf16[4,128,128]{2,0,1:T(4,128)(2,1)S(1)} all-gather(bf16[4,2,128]{2,0,1:T(4,128)(2,1)S(1)} %fusion.30), channel_id=1, replica_groups=mesh['dp'=4,'dap'=64] {'dap'}, dimensions={1}, use_global_device_ids=true | all-gather | bytes 133120 | tf_op jit(solution)/shard_map/all_gather | solution.py:99
  297.1 0.7 copy-done.1
  299.2 0.7 copy-done.16
  300.4 0.5 copy-done.13
  301.2 1.5 fusion.31
  302.7 1.0 fusion.9
  303.7 0.3 multiply_add_fusion
  304.3 0.9 fusion.10
  307.3 0.3 multiply_reduce_fusion.3
  309.2 247.6 %all-reduce.17 = bf16[4,128,128]{2,0,1:T(4,128)(2,1)S(1)} all-reduce(f32[4,128,128]{2,0,1:T(4,128)S(1)} %copy.251), channel_id=2, replica_groups=mesh['dp'=4,'dap'=64] {'dap'}, use_global_device_ids=true, to_apply=%region_17.0.clone | all-reduce | flops 65536 | bytes 393216
  557.5 0.9 fusion.27
  559.7 0.8 copy.252
  560.5 5.0 all-to-all-start.2
  565.6 0.9 fusion.11
  566.7 8.5 all-to-all-done.2
  576.8 0.3 multiply_reduce_fusion.2
  578.7 249.5 %all-reduce.18 = bf16[4,128,128]{2,0,1:T(4,128)(2,1)S(1)} all-reduce(f32[4,128,128]{2,0,1:T(4,128)S(1)} %copy.283), channel_id=3, replica_groups=mesh['dp'=4,'dap'=64] {'dap'}, use_global_device_ids=true, to_apply=%region_27.0.clone | all-reduce | flops 65536 | bytes 393216
  829.4 0.9 fusion.28
  830.8 0.9 fusion.12
  832.2 238.1 %all-reduce.10 = (f32[128]{0:T(128)S(1)}, f32[128,4]{0,1:T(4,128)S(1)}, f32[128]{0:T(128)S(1)}, f32[128,4]{0,1:T(4,128)S(1)}, f32[128]{0:T(128)S(1)}) all-reduce(f32[128]{0:T(128)S(1)} %add.191, f32[128,4]{0,1:T(4,128)S(1)} %convolution_bitcast_fusion.5, f32[128]{0:T(128)S(1)} %add.192, ...), channel_id=1, replica_groups=mesh['dp'=4,'dap'=64] {'dp','dap'}, use_global_device_ids=true, to_apply=%region_32.0 | all-reduce | flops 1408 | bytes 11264 | tf_op jit(solution)/shard_map/psum | solution.py:144
  1070.3 0.5 broadcast_multiply_fusion.15
  1070.8 0.5 broadcast_multiply_fusion.14
  1071.5 0.7 copy.291
  1072.3 0.5 broadcast_multiply_fusion.13
  1072.8 0.6 broadcast_multiply_fusion.7
  1073.4 0.6 broadcast_multiply_fusion.6
  1073.9 254.7 %all-reduce.16.cloned.1.call-done = (f32[128,512]{1,0:T(8,128)}, f32[128,128]{1,0:T(8,128)}, f32[128,512]{1,0:T(8,128)}, f32[128,128]{1,0:T(8,128)}, f32[128,512]{1,0:T(8,128)}, /*index=5*/f32[512,128]{1,0:T(8,128)}) async-done(((f32[128,512]{1,0:T(8,128)}, f32[128,128]{1,0:T(8,128)}, f32[128,512]{1,0:T(8,128)}, f32[128,128]{1,0:T(8,128)}, f32[128,512]{1,0:T(8,128)}, /*index=5*/f32[512,128]{1,0:T(8,128)}), ...) | async-done | bytes 1179664 | tf_op jit(solution)/shard_map/psum | solution.py:144
  1328.7 1.7 broadcast_multiply_fusion.3
  1330.4 0.6 broadcast_multiply_fusion.5
  1331.0 0.6 broadcast_multiply_fusion.4
  1331.7 0.7 broadcast_multiply_fusion.2
  1332.7 0.7 broadcast_multiply_fusion.1
  1333.8 0.7 broadcast_multiply_fusion
  (212 shorter events, 17.1 us)
Async XLA Ops:
  7.2 159.5 %copy-start = (f32[128,4]{0,1:T(4,128)S(1)}, f32[128,4]{0,1:T(4,128)}, u32[]{:S(2)}) copy-start(f32[128,4]{0,1:T(4,128)} %param.23) | copy-start | bytes 6148
  8.9 0.7 copy-start.14
  8.9 0.7 copy-start.12
  9.8 133.1 %copy-start.2 = (f32[128,512]{1,0:T(8,128)S(1)}, f32[128,512]{1,0:T(8,128)}, u32[]{:S(2)}) copy-start(f32[128,512]{1,0:T(8,128)} %param.18) | copy-start | bytes 786436
  142.8 0.8 copy-start.3
  145.0 0.8 copy-start.17
  146.9 14.1 %all-to-all-start.1 = ((bf16[2,128,128]{2,0,1:T(2,128)(2,1)}), bf16[2,128,128]{2,0,1:T(2,128)(2,1)S(1)}, u32[]{:S(2)}, u32[]{:S(2)}) async-start(bf16[2,128,128]{2,0,1:T(2,128)(2,1)} %copy.203), calls=%async_computation.1 | async-start | bytes 131072 | tf_op jit(solution)/shard_map/all_to_all | solution.py:93
  151.5 0.8 copy-start.8
  153.1 0.7 copy-start.18
  161.0 135.9 %all-to-all-start = ((bf16[2,128,128]{2,0,1:T(2,128)(2,1)}), bf16[2,128,128]{2,0,1:T(2,128)(2,1)S(1)}, u32[]{:S(2)}, u32[]{:S(2)}) async-start(bf16[2,128,128]{2,0,1:T(2,128)(2,1)} %bitcast.240), calls=%async_computation | async-start | bytes 131072 | tf_op jit(solution)/shard_map/all_to_all | solution.py:94
  166.0 0.7 copy-start.11
  296.8 1.0 copy-start.1
  299.1 0.8 copy-start.16
  300.2 0.7 copy-start.13
  300.3 1.0 copy-start.4
  302.7 1.0 copy-start.15
  560.5 14.6 %all-to-all-start.2 = ((bf16[128,2,128]{2,1,0:T(2,128)(2,1)}), bf16[128,2,128]{2,1,0:T(2,128)(2,1)S(1)}, u32[]{:S(2)}, u32[]{:S(2)}) async-start(bf16[128,2,128]{2,1,0:T(2,128)(2,1)} %copy.252), calls=%async_computation.2 | async-start | bytes 131072 | tf_op jit(solution)/shard_map/all_to_all | solution.py:120
  565.6 763.1 %all-reduce.16.cloned.1.call-start = ((), (), s32[]{:S(2)}) async-start(), calls=%async_computation.3 | async-start | bytes 2359296 | tf_op jit(solution)/shard_map/psum | solution.py:144
  1328.7 1.7 copy-start.10
  1328.7 2.4 copy-start.9
  1330.4 1.3 copy-start.7
  1331.7 1.0 copy-start.6
  1332.7 1.0 copy-start.5
Sparse Core Ops, SparseCore 0:
  1072.4 256.2 all-reduce.15
where the time goes:
time: 1340 us
  blocking collectives  998 us (74%)
  waiting for transfers between devices  269 us (20%)
  local copies, waits for them, and re-layouts  17.9 us (1%)
  between operations  15.8 us (1%)
  matrix products  14.7 us (1%)
  starting transfers between devices  14.4 us (1%)
    unnamed x2, blocking collectives  497 us
    psum x1, waiting for transfers between devices, local(): lax.psum((partials[0], partials[1], partials[2], partials[3], partials[4]...  255 us
    psum x1, blocking collectives, local(): lax.psum((partials[0], partials[1], partials[2], partials[3], partials[4]...  238 us
    all_gather x1, blocking collectives, local(): lax.all_gather(start_local, 'dap', axis=1, tiled=True).astype(jnp.float32)  133 us
    all_gather x1, blocking collectives, local(): lax.all_gather(end_local, 'dap', axis=1, tiled=True).astype(jnp.float32)  130 us
  transfers between devices with their start and end apart: 4, of which 3 were waited for; matrix products, arithmetic and copies ran while one was open for 0% of the time, Pallas kernels for 0%

commit v1 on v0

v1 whole, which is shorter than its diff:
```python
import functools

import jax
import jax.numpy as jnp
from jax import lax
from jax.experimental import pallas as pl
from jax.experimental.pallas import tpu as pltpu
from jax.sharding import PartitionSpec as P

HEADS = 4
EPS = 1e-05
F32 = jnp.float32
BF16 = jnp.bfloat16
C = 128
FULL = lax.Precision.HIGHEST
VMEM_LIMIT = 48 * 1024 * 1024


def dot(a, b, contract=((1,), (0,)), precision=None):
    return lax.dot_general(a, b, (contract, ((), ())), precision=precision, preferred_element_type=F32)


NN = ((1,), (0,))
NT = ((1,), (1,))
TN = ((0,), (0,))


def ln_stats(x):
    centre = x - jnp.mean(x, -1, keepdims=True)
    spread = jnp.mean(centre * centre, -1, keepdims=True)
    rstd = lax.rsqrt(spread + EPS)
    return centre * rstd, rstd


def ln_back(dn, xhat, rstd, gain):
    t = dn * gain
    m1 = jnp.mean(t, -1, keepdims=True)
    m2 = jnp.mean(t * xhat, -1, keepdims=True)
    dx = rstd * (t - m1 - xhat * m2)
    return dx.astype(BF16).astype(F32), jnp.sum(dn * xhat, 0, keepdims=True)


def head_masks(dtype):
    lane = lax.broadcasted_iota(jnp.int32, (1, C), 1)
    size = C // HEADS
    return [((lane >= h * size) & (lane < (h + 1) * size)).astype(dtype) for h in range(HEADS)]


def stack_heads(a, masks):
    return jnp.concatenate([a * m for m in masks], 0)


def unstack_heads(a, masks):
    n = a.shape[0] // HEADS
    total = a[:n] * masks[0]
    for h in range(1, HEADS):
        total = total + a[h * n : (h + 1) * n] * masks[h]
    return total


def project(n, w_ref):
    proj = dot(n, w_ref[...].astype(BF16))
    scale = (C // HEADS) ** (-0.5)
    q = (proj[:, :C] * scale).astype(BF16)
    k = proj[:, C : 2 * C].astype(BF16)
    v = proj[:, 2 * C : 3 * C].astype(BF16)
    return q, k, v, jax.nn.sigmoid(proj[:, 3 * C :])


def plane_of(n, wt_ref):
    return dot(wt_ref[...], n.astype(F32), NT, FULL)


def rows_of(ref, start, count, stride):
    return ref[pl.ds(start, count, stride=stride), :]


def plane_local_kernel(x_ref, g_ref, wt_ref, out_ref, small):
    n_dst, rows, _ = out_ref.shape
    xhat, _ = ln_stats(x_ref[...].astype(F32))
    n = (xhat * g_ref[...]).astype(BF16)
    plane = plane_of(n, wt_ref)
    small[0:HEADS, :] = plane[:, :C]
    small[HEADS : 2 * HEADS, :] = plane[:, C:]
    out_ref[...] = jnp.broadcast_to(small[...].astype(BF16)[None], (n_dst, rows, C))


def start_forward_kernel(
    recv_ref, x_ref, cot_ref, mask_ref, g_ref, w_ref, wo_ref, ge_ref, wte_ref,
    send_ref, qkv_ref, gating_ref, mix_ref, prob_ref, first_ref,
    fscr, plane, sscr, small,
):
    n_dst = recv_ref.shape[0]
    N = 2 * n_dst
    rows = send_ref.shape[1]
    fscr[...] = recv_ref[...].astype(F32).reshape(n_dst * 8, C)
    for r in range(2):
        for h in range(HEADS):
            plane[pl.ds(h * N + r, n_dst, stride=2), :] = rows_of(fscr, r * 4 + h, n_dst, 8)
    masks = head_masks(BF16)
    kept = mask_ref[...].astype(F32)
    x = x_ref[...].astype(F32)
    xhat, _ = ln_stats(x)
    n = (xhat * g_ref[...]).astype(BF16)
    q, k, v, gating = project(n, w_ref)
    qkv_ref[:, :C] = q
    qkv_ref[:, C : 2 * C] = k
    qkv_ref[:, 2 * C :] = v
    gating_ref[...] = gating
    mixes = []
    for r in range(2):
        part = slice(r * N, (r + 1) * N)
        s = dot(q[part], stack_heads(k[part], masks), NT)
        probs = []
        for h in range(HEADS):
            w = jnp.exp(s[:, h * N : (h + 1) * N] + plane[h * N : (h + 1) * N, :]) * kept
            probs.append(w / jnp.sum(w, -1, keepdims=True))
        prob = jnp.concatenate(probs, 1)
        prob_ref[part, :] = prob
        mixes.append(dot(prob.astype(BF16), stack_heads(v[part], masks)))
    mix = jnp.concatenate(mixes, 0)
    mix_ref[...] = mix
    update = dot((gating * mix).astype(BF16), wo_ref[...].astype(BF16))
    first = (x + update).astype(BF16)
    first_ref[...] = first
    first = first.astype(F32)
    xhat_e, _ = ln_stats(first)
    plane_e = plane_of((xhat_e * ge_ref[...]).astype(BF16), wte_ref)
    small[0:HEADS, :] = plane_e[:, :N]
    small[HEADS : 2 * HEADS, :] = plane_e[:, N:]
    fscr[0 : 2 * N, :] = first
    for r in range(2):
        for a in range(2):
            sscr[pl.ds(r * 2 + a, n_dst, stride=rows), :] = rows_of(fscr, r * N + a, n_dst, 2)
    fscr[0 : 2 * N, :] = cot_ref[...].astype(F32)
    for r in range(2):
        for a in range(2):
            sscr[pl.ds(4 + r * 2 + a, n_dst, stride=rows), :] = rows_of(fscr, r * N + a, n_dst, 2)
    for i in range(8):
        sscr[pl.ds(8 + i, n_dst, stride=rows), :] = jnp.broadcast_to(small[i : i + 1, :], (n_dst, C))
    send_ref[...] = sscr[...].reshape(n_dst, rows, C).astype(BF16)


def put_wide(scr, src, value, row, n_dst, rows):
    for t in range(4):
        src[...] = value[:, t * C : (t + 1) * C]
        for i in range(2):
            scr[pl.ds(row + i * 4 + t, n_dst, stride=rows), :] = rows_of(src, i, n_dst, 2)


def put_narrow(scr, src, row, n_dst, rows, each):
    for i in range(each):
        scr[pl.ds(row + i, n_dst, stride=rows), :] = rows_of(src, i, n_dst, each)


def put_small(scr, row, values, n_dst, rows):
    scr[pl.ds(row, n_dst, stride=rows), :] = jnp.zeros((n_dst, C), F32)
    for e, value in enumerate(values):
        scr[e * rows + row : e * rows + row + 1, :] = value


def end_kernel(
    recv_ref, mask_ref, g_ref, w_ref, wo_ref, gt_ref, wu_ref, wd_ref,
    send_ref,
    fscr, zscr, cscr, plane, down, narrow, sscr,
):
    n_dst, in_rows, _ = recv_ref.shape
    N = 2 * n_dst
    rows = send_ref.shape[1]
    fscr[...] = recv_ref[...].astype(F32).reshape(n_dst * in_rows, C)
    for r in range(2):
        for a in range(2):
            zscr[pl.ds(a * N + r, n_dst, stride=2), :] = rows_of(fscr, r * 2 + a, n_dst, in_rows)
            cscr[pl.ds(a * N + r, n_dst, stride=2), :] = rows_of(fscr, 4 + r * 2 + a, n_dst, in_rows)
        for h in range(HEADS):
            plane[pl.ds(h * N + r, n_dst, stride=2), :] = rows_of(fscr, 8 + r * 4 + h, n_dst, in_rows)
    masks = head_masks(BF16)
    masks_f = head_masks(F32)
    length = jnp.sum(mask_ref[...].astype(F32), -1, keepdims=True)
    kept = (lax.broadcasted_iota(jnp.int32, (N, 1), 0).astype(F32) < length).astype(F32)
    x = zscr[...]
    cot = cscr[...]
    xhat, rstd = ln_stats(x)
    n = (xhat * g_ref[...]).astype(BF16)
    q, k, v, gating = project(n, w_ref)
    saved = []
    mixes = []
    for a in range(2):
        part = slice(a * N, (a + 1) * N)
        ks = stack_heads(k[part], masks)
        vs = stack_heads(v[part], masks)
        s = dot(ks, q[part], NT) + plane[...]
        probs = []
        for h in range(HEADS):
            w = jnp.exp(s[h * N : (h + 1) * N]) * kept
            probs.append(w / jnp.sum(w, 0, keepdims=True))
        prob = jnp.concatenate(probs, 0)
        prob_b = prob.astype(BF16)
        mixes.append(dot(prob_b, vs, TN))
        saved.append((ks, vs, prob, prob_b))
    mix = jnp.concatenate(mixes, 0)
    gated = (gating * mix).astype(BF16)
    wo = wo_ref[...].astype(BF16)
    second = (x + dot(gated, wo)).astype(BF16).astype(F32)
    xhat2, rstd2 = ln_stats(second)
    n2 = (xhat2 * gt_ref[...]).astype(BF16)
    wu = wu_ref[...].astype(BF16)
    wd = wd_ref[...].astype(BF16)
    cot_b = cot.astype(BF16)
    up = dot(n2, wu)
    cdf = 0.5 * (1.0 + lax.erf(up * (0.5**0.5)))
    hidden = (up * cdf).astype(BF16)
    dhidden = dot(cot_b, wd, NT).astype(BF16).astype(F32)
    slope = cdf + up * (jnp.exp(-0.5 * up * up) * 0.3989422804014327)
    dup = (dhidden * slope).astype(BF16)
    down[...] = dot(hidden, cot_b, TN)
    put_narrow(sscr, down, 28, n_dst, rows, 8)
    put_wide(sscr, narrow, dot(n2, dup, TN), 20, n_dst, rows)
    dn2 = dot(dup, wu, NT).astype(BF16).astype(F32)
    dx2, dgain_t = ln_back(dn2, xhat2, rstd2, gt_ref[...])
    dsecond = (cot + dx2).astype(BF16)
    narrow[...] = dot(gated, dsecond, TN)
    put_narrow(sscr, narrow, 36, n_dst, rows, 2)
    dgated = dot(dsecond, wo, NT).astype(BF16).astype(F32)
    dgating = dgated * mix
    dmix = (dgated * gating).astype(BF16)
    dq, dk, dv = [], [], []
    for a in range(2):
        part = slice(a * N, (a + 1) * N)
        ks, vs, prob, prob_b = saved[a]
        dprob = dot(vs, dmix[part], NT).astype(BF16).astype(F32)
        dv.append(unstack_heads(dot(prob_b, dmix[part]), masks_f))
        ds = []
        for h in range(HEADS):
            p = prob[h * N : (h + 1) * N]
            d = dprob[h * N : (h + 1) * N]
            ds.append(p * (d - jnp.sum(p * d, 0, keepdims=True)))
        ds = jnp.concatenate(ds, 0)
        if a == 0:
            plane[...] = ds
        else:
            plane[...] += ds
        ds = ds.astype(BF16)
        dq.append(dot(ds, ks, TN))
        dk.append(unstack_heads(dot(ds, q[part]), masks_f))
    for r in range(2):
        for h in range(HEADS):
            sscr[pl.ds(r * 4 + h, n_dst, stride=rows), :] = rows_of(plane, h * N + r, n_dst, 2)
    dproj = project_cotangent(dq, dk, dv, gating, dgating)
    put_wide(sscr, narrow, dot(n, dproj, TN), 12, n_dst, rows)
    dn = dot(dproj, w_ref[...].astype(BF16), NT).astype(BF16).astype(F32)
    dx, dgain = ln_back(dn, xhat, rstd, g_ref[...])
    zscr[...] = dsecond.astype(F32) + dx
    for r in range(2):
        for a in range(2):
            sscr[pl.ds(8 + r * 2 + a, n_dst, stride=rows), :] = rows_of(zscr, a * N + r, n_dst, 2)
    put_small(sscr, 38, [dgain_t, dgain], n_dst, rows)
    sscr[pl.ds(39, n_dst, stride=rows), :] = jnp.zeros((n_dst, C), F32)
    send_ref[...] = sscr[...].reshape(n_dst, rows, C).astype(BF16)


def project_cotangent(dq, dk, dv, gating, dgating):
    scale = (C // HEADS) ** (-0.5)
    dq = jnp.concatenate(dq, 0).astype(BF16).astype(F32) * scale
    dk = jnp.concatenate(dk, 0)
    dv = jnp.concatenate(dv, 0)
    dg = dgating * gating * (1.0 - gating)
    return jnp.concatenate([dq.astype(BF16), dk.astype(BF16), dv.astype(BF16), dg.astype(BF16)], 1)


def plane_back(planes, n, xhat, rstd, gain, wt8_ref, p8_ref, wt_ref):
    N = planes.shape[1]
    planes = planes.astype(BF16)
    wt8_ref[...] = jnp.zeros_like(wt8_ref)
    wt8_ref[0:HEADS, :] = wt_ref[...]
    p8_ref[...] = jnp.zeros_like(p8_ref)
    wide = planes.astype(F32)
    dns = []
    dbias = 0.0
    for r in range(2):
        p8_ref[0:HEADS, :] = wide[r * HEADS : (r + 1) * HEADS, :]
        p = p8_ref[...]
        dns.append(dot(p, wt8_ref[...], TN, FULL))
        dbias = dbias + dot(p.astype(BF16), n[r * N : (r + 1) * N])
    dn = jnp.concatenate(dns, 0).astype(BF16).astype(F32)
    dx, dgain = ln_back(dn, xhat, rstd, gain)
    return dx, dgain, dbias[0:HEADS]


def start_backward_kernel(
    recv_ref, x_ref, first_ref, qkv_ref, gating_ref, mix_ref, prob_ref, g_ref, w_ref, wo_ref, ge_ref, wte_ref,
    send_ref, sum_ref, gsum_ref,
    fscr, gscr, plane, narrow, sscr, wt8, p8,
):
    n_dst, in_rows, _ = recv_ref.shape
    N = 2 * n_dst
    rows = send_ref.shape[1]
    recv = recv_ref[...].astype(F32)
    total = jnp.sum(recv, 0)
    sum_ref[...] = total
    fscr[...] = recv.reshape(n_dst * in_rows, C)
    for r in range(2):
        for a in range(2):
            gscr[pl.ds(r * N + a, n_dst, stride=2), :] = rows_of(fscr, 8 + r * 2 + a, n_dst, in_rows)
    first = first_ref[...].astype(F32)
    xhat_e, rstd_e = ln_stats(first)
    n_e = (xhat_e * ge_ref[...]).astype(BF16)
    dxe, dgain_e, dbias_e = plane_back(total[0:8], n_e, xhat_e, rstd_e, ge_ref[...], wt8, p8, wte_ref)
    dfirst = (gscr[...] + dxe).astype(BF16)
    masks = head_masks(BF16)
    masks_f = head_masks(F32)
    xhat, rstd = ln_stats(x_ref[...].astype(F32))
    n = (xhat * g_ref[...]).astype(BF16)
    q = qkv_ref[:, :C]
    k = qkv_ref[:, C : 2 * C]
    v = qkv_ref[:, 2 * C :]
    gating = gating_ref[...]
    mix = mix_ref[...]
    gated = (gating * mix).astype(BF16)
    wo = wo_ref[...].astype(BF16)
    narrow[...] = dot(gated, dfirst, TN)
    put_narrow(sscr, narrow, 16, n_dst, rows, 2)
    dgated = dot(dfirst, wo, NT).astype(BF16).astype(F32)
    dgating = dgated * mix
    dmix = (dgated * gating).astype(BF16)
    dq, dk, dv = [], [], []
    for r in range(2):
        part = slice(r * N, (r + 1) * N)
        ks = stack_heads(k[part], masks)
        vs = stack_heads(v[part], masks)
        prob = prob_ref[part, :]
        dprob = dot(dmix[part], vs, NT).astype(BF16).astype(F32)
        dv.append(unstack_heads(dot(prob.astype(BF16), dmix[part], TN), masks_f))
        ds = []
        for h in range(HEADS):
            p = prob[:, h * N : (h + 1) * N]
            d = dprob[:, h * N : (h + 1) * N]
            ds.append(p * (d - jnp.sum(p * d, -1, keepdims=True)))
            if r == 0:
                plane[h * N : (h + 1) * N, :] = ds[h]
            else:
                plane[h * N : (h + 1) * N, :] += ds[h]
        ds = jnp.concatenate(ds, 1).astype(BF16)
        dq.append(dot(ds, ks))
        dk.append(unstack_heads(dot(ds, q[part], TN), masks_f))
    for r in range(2):
        for h in range(HEADS):
            sscr[pl.ds(r * 4 + h, n_dst, stride=rows), :] = rows_of(plane, h * N + r, n_dst, 2)
    dproj = project_cotangent(dq, dk, dv, gating, dgating)
    put_wide(sscr, narrow, dot(n, dproj, TN), 8, n_dst, rows)
    dn = dot(dproj, w_ref[...].astype(BF16), NT).astype(BF16).astype(F32)
    dx, dgain = ln_back(dn, xhat, rstd, g_ref[...])
    gsum_ref[...] = dfirst.astype(F32) + dx
    put_small(sscr, 18, [dbias_e[h : h + 1] for h in range(HEADS)] + [dgain_e, dgain], n_dst, rows)
    for i in range(19, rows):
        sscr[pl.ds(i, n_dst, stride=rows), :] = jnp.zeros((n_dst, C), F32)
    send_ref[...] = sscr[...].reshape(n_dst, rows, C).astype(BF16)


def start_plane_kernel(
    recv_ref, sum_ref, gsum_ref, x_ref, g_ref, wt_ref, grad_ref, part_ref, wt8, p8
):
    total = jnp.sum(recv_ref[...].astype(F32), 0)
    xhat, rstd = ln_stats(x_ref[...].astype(F32))
    n = (xhat * g_ref[...]).astype(BF16)
    dx, dgain, dbias = plane_back(total[0:8], n, xhat, rstd, g_ref[...], wt8, p8, wt_ref)
    grad_ref[...] = (gsum_ref[...] + dx).astype(BF16)
    part_ref[0:28, :] = sum_ref[12:40, :]
    part_ref[28:40, :] = total[8:20]
    part_ref[40:44, :] = dbias
    part_ref[44:45, :] = dgain
    part_ref[45:48, :] = jnp.zeros((3, C), F32)


def spread_kernel(a_ref, b_ref, c_ref, d_ref, out_ref):
    total = (a_ref[...] + b_ref[...]) + (c_ref[...] + d_ref[...])
    out_ref[...] = jnp.broadcast_to(total.astype(BF16)[None], out_ref.shape)


def finish_kernel(
    factor, recv_ref,
    gs_ref, ps_ref, bs_ref, os_ref, ge_ref, pe_ref, be_ref, oe_ref, gt_ref, up_ref, down_ref,
    fscr, block,
):
    n_dst, rows, _ = recv_ref.shape
    recv = recv_ref[...].astype(F32) * factor
    fscr[...] = recv.reshape(n_dst * rows, C)

    def wide(ref, row):
        for t in range(4):
            for i in range(2):
                block[pl.ds(i, n_dst, stride=2), :] = rows_of(fscr, row + i * 4 + t, n_dst, rows)
            ref[:, t * C : (t + 1) * C] = block[...]

    def narrow(ref, row, each):
        for i in range(each):
            ref[pl.ds(i, n_dst, stride=each), :] = rows_of(fscr, row + i, n_dst, rows)

    wide(pe_ref, 0)
    wide(up_ref, 8)
    narrow(down_ref, 16, 8)
    narrow(oe_ref, 24, 2)
    wide(ps_ref, 28)
    narrow(os_ref, 36, 2)
    tail = jnp.sum(recv[:, 40:48, :], 0)
    bs_ref[...] = tail[0:HEADS]

    def one(e, row):
        return fscr[e * rows + row : e * rows + row + 1, :]

    gt_ref[...] = one(0, 26)
    for h in range(HEADS):
        be_ref[h : h + 1, :] = one(h, 38)
    ge_ref[...] = one(1, 26) + one(4, 38)
    gs_ref[...] = tail[HEADS : HEADS + 1] + one(5, 38)


def shape(dims, dtype=F32):
    return jax.ShapeDtypeStruct(dims, dtype)


def call(body, out_shape, scratch, *operands):
    whole = pl.BlockSpec(memory_space=pltpu.VMEM)
    many = isinstance(out_shape, (list, tuple))
    return pl.pallas_call(
        body,
        out_shape=out_shape,
        in_specs=[whole] * len(operands),
        out_specs=[whole] * len(out_shape) if many else whole,
        scratch_shapes=[pltpu.VMEM(s, F32) for s in scratch],
        compiler_params=pltpu.CompilerParams(vmem_limit_bytes=VMEM_LIMIT),
    )(*operands)


def swap(buffer):
    return lax.all_to_all(buffer, "dap", split_axis=0, concat_axis=0, tiled=True)


def local(
    pair_input, cotangent, residue_mask, gain_start, proj_start, bias_start, output_start,
    gain_end, proj_end, bias_end, output_end, gain_transition, transition_up, transition_down,
):
    _, _, N, _ = pair_input.shape
    n_dst = N // 2
    x = pair_input.reshape(2 * N, C)
    cot = cotangent.reshape(2 * N, C)
    g_s, g_e, g_t = (g.reshape(1, C) for g in (gain_start, gain_end, gain_transition))
    wt_s, wt_e = bias_start.T, bias_end.T
    tokens = (2 * N, C)
    wide = (C, 4 * C)

    send = call(plane_local_kernel, shape((n_dst, 8, C), BF16), [(8, C)], x, g_s, wt_s)
    recv = swap(send)
    send, qkv, gating, mix, prob, first = call(
        start_forward_kernel,
        [shape((n_dst, 16, C), BF16), shape((2 * N, 3 * C), BF16), shape(tokens), shape(tokens),
         shape((2 * N, HEADS * N)), shape(tokens, BF16)],
        [(n_dst * 8, C), (HEADS * N, N), (n_dst * 16, C), (8, C)],
        recv, x, cot, residue_mask, g_s, proj_start, output_start, g_e, wt_e,
    )
    recv = swap(send)
    send = call(
        end_kernel,
        shape((n_dst, 40, C), BF16),
        [(n_dst * 16, C), tokens, tokens, (HEADS * N, N), (4 * C, C), (C, C), (n_dst * 40, C)],
        recv, residue_mask, g_e, proj_end, output_end, g_t, transition_up, transition_down,
    )
    recv = swap(send)
    send, summed, gsum = call(
        start_backward_kernel,
        [shape((n_dst, 24, C), BF16), shape((40, C)), shape(tokens)],
        [(n_dst * 40, C), tokens, (HEADS * N, N), (C, C), (n_dst * 24, C), (8, C), (8, C)],
        recv, x, first, qkv, gating, mix, prob, g_s, proj_start, output_start, g_e, wt_e,
    )
    recv = swap(send)
    grad, part = call(
        start_plane_kernel,
        [shape(tokens, BF16), shape((48, C))],
        [(8, C), (8, C)],
        recv, summed, gsum, x, g_s, wt_s,
    )
    n_dp = lax.axis_size("dp")
    others = [lax.ppermute(part, "dp", [(i, i ^ d) for i in range(n_dp)]) for d in range(1, n_dp)]
    send = call(spread_kernel, shape((n_dst, 48, C), BF16), [], part, *others)
    recv = swap(send)
    factor = 1.0 / (n_dp * N)
    gs, ps, bs, os, ge, pe, be, oe, gt, up, down = call(
        functools.partial(finish_kernel, factor),
        [shape((1, C)), shape(wide), shape((HEADS, C)), shape((C, C)),
         shape((1, C)), shape(wide), shape((HEADS, C)), shape((C, C)),
         shape((1, C)), shape(wide), shape((4 * C, C))],
        [(n_dst * 48, C), (C, C)],
        recv,
    )
    return (
        grad.reshape(1, 2, N, C), gs.reshape(C), ps, bs.T, os, ge.reshape(C), pe, be.T, oe, gt.reshape(C), up, down,
    )


def solution(mesh):
    rows = P("dp", "dap", None, None)
    in_specs = (rows, rows, P("dp", None)) + (P(),) * 11
    out_specs = (rows,) + (P(),) * 11
    return jax.shard_map(local, mesh=mesh, in_specs=in_specs, out_specs=out_specs, check_vma=False)
```

time: 1340 us -> 133 us (0.10)
  blocking collectives: 998 us -> 104 us
  waiting for transfers between devices: 269 us -> 3.75 us
  between operations: 15.8 us -> 0.78 us
  matrix products: 14.7 us -> 0 us
    unnamed x2 -> x0, blocking collectives: 497 us -> none
    all_gather x2 -> x0, blocking collectives: 263 us -> none  [the longest x1 133 us: local(): lax.all_gather(start_local, 'dap', axis=1, tiled=True).astype(jnp.float32)]
    psum x1 -> x0, waiting for transfers between devices: 255 us -> none  [local(): lax.psum((partials[0], partials[1], partials[2], partials[3], partials[4]...]
    psum x1 -> x0, blocking collectives: 238 us -> none  [local(): lax.psum((partials[0], partials[1], partials[2], partials[3], partials[4]...]
    all_to_all x0 -> x5, blocking collectives: none -> 104 us  [swap(): lax.all_to_all(buffer, 'dap', split_axis=0, concat_axis=0, tiled=True)]
    dot_general x41 -> x0, matrix products: 14.7 us -> none  [the longest x8 3.2 us: attend(): jnp.dot(normed, w_proj.astype(jnp.bfloat16), preferred_element_type=jnp.f...]
    all_to_all x3 -> x0, waiting for transfers between devices: 14.5 us -> none  [the longest x1 8.46 us: local(): lax.all_to_all(flipped(column_grad), 'dap', split_axis=0, concat_axis=1,...]
    all_to_all x3 -> x0, starting transfers between devices: 14.3 us -> none  [the longest x1 5.05 us: local(): lax.all_to_all(flipped(column_grad), 'dap', split_axis=0, concat_axis=1,...]
  transfers between devices with their start and end apart: 4 -> 3, of which waited for: 3 -> 2; matrix products, arithmetic and copies ran while one was open for 0% -> 0% of each run, Pallas kernels for 0% -> 0%
where the time goes in v1:
time: 133 us
  blocking collectives  104 us (78%)
  Pallas kernels  10.2 us (8%)
  starting transfers between devices  8.85 us (7%)
  local copies, waits for them, and re-layouts  4.88 us (4%)
  waiting for transfers between devices  3.75 us (3%)
    all_to_all x5, blocking collectives, swap(): lax.all_to_all(buffer, 'dap', split_axis=0, concat_axis=0, tiled=True)  104 us
    pallas_call x7, Pallas kernels, call(): pl.pallas_call(body, out_shape=out_shape, in_specs=[whole] * len(operands...  10.2 us
    ppermute x3, starting transfers between devices, local(): lax.ppermute(part, 'dp', [(i, i ^ d) for i in range(n_dp)])  8.85 us
    unnamed x34, local copies, waits for them, and re-layouts  4.88 us
    ppermute x3, waiting for transfers between devices, local(): lax.ppermute(part, 'dp', [(i, i ^ d) for i in range(n_dp)])  3.75 us
  transfers between devices with their start and end apart: 3, of which 2 were waited for; matrix products, arithmetic and copies ran while one was open for 0% of the time, Pallas kernels for 0%

profile of v1, /device:TPU:1, one launch (start us, length us, event | category | flops | bytes accessed | tf_op | source)
XLA Modules:
  0.0 132.6 jit_solution(417805033553905966)
XLA Ops:
  0.6 0.0 copy-start
  0.7 0.0 copy-start.1
  0.7 0.9 copy-done.1
  1.5 0.0 copy-start.10
  1.5 0.7 copy-done.10
  2.2 0.0 copy-start.12
  2.2 0.7 copy-done.12
  2.9 0.4 shard_map.229
  3.3 0.0 copy-start.6
  3.3 0.0 copy-start.8
  3.3 23.3 %all_to_all.25.recv_ref = bf16[64,8,128]{2,1,0:T(8,128)(2,1)S(1)} all-to-all(bf16[64,8,128]{2,1,0:T(8,128)(2,1)S(1)} %shard_map.229), channel_id=1, replica_groups=mesh['dp'=4,'dap'=64] {'dap'}, dimensions={0} | all-to-all | bytes 262144 | tf_op jit(solution)/shard_map/all_to_all | solution.py:436
  26.6 0.0 copy-start.9
  26.6 0.0 copy-start.14
  26.6 0.0 copy-done
  26.6 0.0 copy-done.6
  26.6 0.0 copy-done.8
  26.7 0.7 copy-done.9
  27.3 0.0 copy-done.14
  27.3 0.0 copy-done.15
  27.3 0.0 copy-start.5
  27.3 0.0 copy-start.7
  27.3 1.8 %shard_map.230 = (bf16[64,16,128]{2,1,0:T(8,128)(2,1)S(1)}, bf16[256,384]{1,0:T(8,128)(2,1)S(1)}, f32[256,128]{1,0:T(8,128)S(1)}, f32[256,128]{1,0:T(8,128)S(1)}...) custom-call(bf16[64,8,128]{2,1,0:T(8,128)(2,1)S(1)} %all_to_all.25.recv_ref, bf16[256,128]{1,0:T(8,128)(2,1)S(1)} %bitcast.14, ...), custom_call_target="tpu_custom_call" | custom-call | tf_op jit(solution)/shard_map/pallas_call | solution.py:425
  29.1 0.0 copy-start.3
  29.1 0.0 copy-start.4
  29.1 14.7 %all_to_all.26.recv_ref = bf16[64,16,128]{2,1,0:T(8,128)(2,1)S(1)} all-to-all(bf16[64,16,128]{2,1,0:T(8,128)(2,1)S(1)} %get-tuple-element.34), channel_id=1, replica_groups=mesh['dp'=4,'dap'=64] {'dap'}, dimensions={0} | all-to-all | bytes 524288 | tf_op jit(solution)/shard_map/all_to_all | solution.py:436
  43.8 0.0 copy-done.5
  43.8 0.0 copy-done.7
  43.8 0.0 copy-done.3
  43.8 0.0 copy-done.4
  43.9 0.6 copy-done.16
  44.5 3.3 %shard_map.231 = bf16[64,40,128]{2,1,0:T(8,128)(2,1)S(1)} custom-call(bf16[64,16,128]{2,1,0:T(8,128)(2,1)S(1)} %all_to_all.26.recv_ref, s32[1,128]{1,0:T(1,128)S(1)} %copy-done.15, f32[1,128]{1,0:T(1,128)S(1)} %bitcast.27, f32[128,512]{1,0:T(8,128)S(1)} %copy-done.3, f32[128,128]{1,0:T(8,128)S(1)} %copy-done.7, f32[1,128]{1,0:T(1,128)S(1)} %bitcast.29, ...), custom_call_target="tpu_custom_call" | custom-call | tf_op jit(solution)/shard_map/pallas_call | solution.py:425
  47.8 0.0 copy-start.2
  47.8 20.3 %all_to_all.27.recv_ref = bf16[64,40,128]{2,1,0:T(8,128)(2,1)S(1)} all-to-all(bf16[64,40,128]{2,1,0:T(8,128)(2,1)S(1)} %shard_map.231), channel_id=1, replica_groups=mesh['dp'=4,'dap'=64] {'dap'}, dimensions={0} | all-to-all | bytes 1310720 | tf_op jit(solution)/shard_map/all_to_all | solution.py:436
  68.1 0.0 copy-done.2
  68.1 0.7 copy-done.13
  68.8 2.1 %shard_map.232 = (bf16[64,24,128]{2,1,0:T(8,128)(2,1)S(1)}, f32[40,128]{1,0:T(8,128)S(1)}, f32[256,128]{1,0:T(8,128)S(1)}) custom-call(bf16[64,40,128]{2,1,0:T(8,128)(2,1)S(1)} %all_to_all.27.recv_ref, bf16[256,128]{1,0:T(8,128)(2,1)S(1)} %bitcast.15, bf16[256,128]{1,0:T(8,128)(2,1)S(1)} %get-tuple-element.35.first_ref, ...), custom_call_target="tpu_custom_call" | custom-call | tf_op jit(solution)/shard_map/pallas_call | solution.py:425
  70.8 19.4 %all_to_all.28.recv_ref = bf16[64,24,128]{2,1,0:T(8,128)(2,1)S(1)} all-to-all(bf16[64,24,128]{2,1,0:T(8,128)(2,1)S(1)} %get-tuple-element.40), channel_id=1, replica_groups=mesh['dp'=4,'dap'=64] {'dap'}, dimensions={0} | all-to-all | bytes 786432 | tf_op jit(solution)/shard_map/all_to_all | solution.py:436
  90.2 0.7 copy-done.11
  90.9 1.2 shard_map.233
  92.1 8.4 %collective-permute-start.2 = (f32[48,128]{1,0:T(8,128)S(1)}, f32[48,128]{1,0:T(8,128)S(1)}, u32[]{:S(2)}, u32[]{:S(2)}) collective-permute-start(f32[48,128]{1,0:T(8,128)S(1)} %get-tuple-element.44.a_ref), channel_id=1, source_target_pairs={{0,192},{64,128},{128,64},{192,0},{1,193},{65,129},{129,65},{193,1... | collective-permute-start | bytes 73736 | tf_op jit(solution)/shard_map/ppermute | solution.py:483
  100.5 0.3 collective-permute-start.1
  100.9 0.1 collective-permute-start
  101.0 1.6 %collective-permute-done.2.d_ref = f32[48,128]{1,0:T(8,128)S(1)} collective-permute-done((f32[48,128]{1,0:T(8,128)S(1)}, f32[48,128]{1,0:T(8,128)S(1)}, u32[]{:S(2)}, u32[]{:S(2)}) %collective-permute-start.2) | collective-permute-done | bytes 24608 | tf_op jit(solution)/shard_map/ppermute | solution.py:483
  102.5 2.2 %collective-permute-done.1.c_ref = f32[48,128]{1,0:T(8,128)S(1)} collective-permute-done((f32[48,128]{1,0:T(8,128)S(1)}, f32[48,128]{1,0:T(8,128)S(1)}, u32[]{:S(2)}, u32[]{:S(2)}) %collective-permute-start.1) | collective-permute-done | bytes 24608 | tf_op jit(solution)/shard_map/ppermute | solution.py:483
  104.7 0.0 collective-permute-done.b_ref
  104.7 0.1 shard_map.234
  104.8 26.5 %all_to_all.29.recv_ref = bf16[64,48,128]{2,1,0:T(8,128)(2,1)S(1)} all-to-all(bf16[64,48,128]{2,1,0:T(8,128)(2,1)S(1)} %shard_map.234), channel_id=1, replica_groups=mesh['dp'=4,'dap'=64] {'dap'}, dimensions={0} | all-to-all | bytes 1572864 | tf_op jit(solution)/shard_map/all_to_all | solution.py:436
  131.2 1.4 %shard_map.235 = (f32[1,128]{1,0:T(1,128)}, f32[128,512]{1,0:T(8,128)}, f32[4,128]{1,0:T(4,128)}, f32[128,128]{1,0:T(8,128)}, f32[1,128]{1,0:T(1,128)}, /*index=...) custom-call(bf16[64,48,128]{2,1,0:T(8,128)(2,1)S(1)} %all_to_all.29., ...), custom_call_target="tpu_custom_call" | custom-call | tf_op jit(solution)/shard_map/pallas_call | solution.py:425
  (4 shorter events, 0.0 us)
Async XLA Ops:
  0.6 26.0 %copy-start = (f32[128,512]{1,0:T(8,128)S(1)}, f32[128,512]{1,0:T(8,128)}, u32[]{:S(2)}) copy-start(f32[128,512]{1,0:T(8,128)} %w_ref.5) | copy-start | bytes 786436
  0.7 0.9 copy-start.1
  1.5 0.7 copy-start.10
  2.2 0.7 copy-start.12
  3.3 23.4 %copy-start.6 = (f32[128,128]{1,0:T(8,128)S(1)}, f32[128,128]{1,0:T(8,128)}, u32[]{:S(2)}) copy-start(f32[128,128]{1,0:T(8,128)} %wo_ref.5) | copy-start | bytes 196612
  3.3 23.4 %copy-start.8 = (bf16[1,2,128,128]{3,2,1,0:T(8,128)(2,1)S(1)}, bf16[1,2,128,128]{3,2,1,0:T(8,128)(2,1)}, u32[]{:S(2)}) copy-start(bf16[1,2,128,128]{3,2,1,0:T(8,128)(2,1)} %param.15) | copy-start | bytes 196612
  26.6 0.7 copy-start.9
  26.6 0.7 copy-start.14
  26.6 0.7 copy-start.15
  27.3 16.5 %copy-start.5 = (f32[512,128]{1,0:T(8,128)S(1)}, f32[512,128]{1,0:T(8,128)}, u32[]{:S(2)}) copy-start(f32[512,128]{1,0:T(8,128)} %wd_ref.1) | copy-start | bytes 786436
  27.3 16.5 %copy-start.7 = (f32[128,128]{1,0:T(8,128)S(1)}, f32[128,128]{1,0:T(8,128)}, u32[]{:S(2)}) copy-start(f32[128,128]{1,0:T(8,128)} %wo_ref.4) | copy-start | bytes 196612
  29.1 14.7 %copy-start.3 = (f32[128,512]{1,0:T(8,128)S(1)}, f32[128,512]{1,0:T(8,128)}, u32[]{:S(2)}) copy-start(f32[128,512]{1,0:T(8,128)} %w_ref.4) | copy-start | bytes 786436
  29.1 14.7 %copy-start.4 = (f32[128,512]{1,0:T(8,128)S(1)}, f32[128,512]{1,0:T(8,128)}, u32[]{:S(2)}) copy-start(f32[128,512]{1,0:T(8,128)} %wu_ref.1) | copy-start | bytes 786436
  43.8 0.7 copy-start.16
  47.8 20.3 %copy-start.2 = (bf16[1,2,128,128]{3,2,1,0:T(8,128)(2,1)S(1)}, bf16[1,2,128,128]{3,2,1,0:T(8,128)(2,1)}, u32[]{:S(2)}) copy-start(bf16[1,2,128,128]{3,2,1,0:T(8,128)(2,1)} %param.14) | copy-start | bytes 196612
  68.1 0.7 copy-start.13
  90.2 0.7 copy-start.11
  92.1 10.4 %collective-permute-start.2 = (f32[48,128]{1,0:T(8,128)S(1)}, f32[48,128]{1,0:T(8,128)S(1)}, u32[]{:S(2)}, u32[]{:S(2)}) collective-permute-start(f32[48,128]{1,0:T(8,128)S(1)} %get-tuple-element.44.a_ref), channel_id=1, source_target_pairs={{0,192},{64,128},{128,64},{192,0},{1,193},{65,129},{129,65},{193,1... | collective-permute-start | bytes 73736 | tf_op jit(solution)/shard_map/ppermute | solution.py:483
  100.5 4.2 %collective-permute-start.1 = (f32[48,128]{1,0:T(8,128)S(1)}, f32[48,128]{1,0:T(8,128)S(1)}, u32[]{:S(2)}, u32[]{:S(2)}) collective-permute-start(f32[48,128]{1,0:T(8,128)S(1)} %get-tuple-element.44.a_ref), channel_id=1, source_target_pairs={{0,128},{64,192},{128,0},{192,64},{1,129},{65,193},{129,1},{193,65... | collective-permute-start | bytes 73736 | tf_op jit(solution)/shard_map/ppermute | solution.py:483
  100.9 3.8 %collective-permute-start = (f32[48,128]{1,0:T(8,128)S(1)}, f32[48,128]{1,0:T(8,128)S(1)}, u32[]{:S(2)}, u32[]{:S(2)}) collective-permute-start(f32[48,128]{1,0:T(8,128)S(1)} %get-tuple-element.44.a_ref), channel_id=1, source_target_pairs={{0,64},{64,0},{128,192},{192,128},{1,65},{65,1},{129,193},{193,129... | collective-permute-start | bytes 73736 | tf_op jit(solution)/shard_map/ppermute | solution.py:483

commit v2 on v1

--- a/solution.py
+++ b/solution.py
@@ -12,6 +12,7 @@
 F32 = jnp.float32
 BF16 = jnp.bfloat16
 C = 128
+HALF = 13
 FULL = lax.Precision.HIGHEST
 VMEM_LIMIT = 48 * 1024 * 1024
 
@@ -67,53 +68,97 @@
     return q, k, v, jax.nn.sigmoid(proj[:, 3 * C :])
 
 
-def plane_of(n, wt_ref):
-    return dot(wt_ref[...], n.astype(F32), NT, FULL)
+def plane_of(n, wt):
+    return dot(wt, n.astype(F32), NT, FULL)
+
+
+def core_index():
+    return lax.rem(lax.axis_index("dp"), 2)
 
 
 def rows_of(ref, start, count, stride):
     return ref[pl.ds(start, count, stride=stride), :]
 
 
-def plane_local_kernel(x_ref, g_ref, wt_ref, out_ref, small):
+WT_S, WT_E = slice(0, 4), slice(4, 8)
+G_S, G_E, G_T, KEPT = slice(8, 9), slice(9, 10), slice(10, 11), slice(11, 12)
+
+
+def plane_local_kernel(
+    x_hbm, gs_hbm, wts_hbm, ge_hbm, wte_hbm, gt_hbm, mask_hbm,
+    out_ref, args_ref,
+    x_ref, gs, wts, ge, wte, gt, mask, small, sems,
+):
     n_dst, rows, _ = out_ref.shape
+    moves = [(gs_hbm, gs), (wts_hbm, wts), (x_hbm, x_ref), (ge_hbm, ge), (wte_hbm, wte), (gt_hbm, gt), (mask_hbm, mask)]
+    copies = [pltpu.make_async_copy(src, dst, sems.at[i]) for i, (src, dst) in enumerate(moves)]
+    for copy in copies:
+        copy.start()
+    for copy in copies:
+        copy.wait()
+    args_ref[WT_S, :] = wts[...]
+    args_ref[WT_E, :] = wte[...]
+    args_ref[G_S, :] = gs[...]
+    args_ref[G_E, :] = ge[...]
+    args_ref[G_T, :] = gt[...]
+    args_ref[KEPT, :] = mask[...].astype(F32)
+    args_ref[12:16, :] = jnp.zeros((4, C), F32)
     xhat, _ = ln_stats(x_ref[...].astype(F32))
-    n = (xhat * g_ref[...]).astype(BF16)
-    plane = plane_of(n, wt_ref)
+    n = (xhat * gs[...]).astype(BF16)
+    plane = plane_of(n, wts[...])
     small[0:HEADS, :] = plane[:, :C]
     small[HEADS : 2 * HEADS, :] = plane[:, C:]
     out_ref[...] = jnp.broadcast_to(small[...].astype(BF16)[None], (n_dst, rows, C))
 
 
-def start_forward_kernel(
-    recv_ref, x_ref, cot_ref, mask_ref, g_ref, w_ref, wo_ref, ge_ref, wte_ref,
-    send_ref, qkv_ref, gating_ref, mix_ref, prob_ref, first_ref,
-    fscr, plane, sscr, small,
-):
-    n_dst = recv_ref.shape[0]
-    N = 2 * n_dst
-    rows = send_ref.shape[1]
-    fscr[...] = recv_ref[...].astype(F32).reshape(n_dst * 8, C)
-    for r in range(2):
-        for h in range(HEADS):
-            plane[pl.ds(h * N + r, n_dst, stride=2), :] = rows_of(fscr, r * 4 + h, n_dst, 8)
+def start_scores_kernel(
+    x_ref, cot_hbm, args_ref, w_ref, wo_hbm,
+    qkv_ref, gating_ref, score_ref, n_ref, cot_ref, wo_ref,
+    sems,
+):
+    copies = [pltpu.make_async_copy(cot_hbm, cot_ref, sems.at[0]), pltpu.make_async_copy(wo_hbm, wo_ref, sems.at[1])]
+    for copy in copies:
+        copy.start()
+    N = score_ref.shape[1] // HEADS
     masks = head_masks(BF16)
-    kept = mask_ref[...].astype(F32)
-    x = x_ref[...].astype(F32)
-    xhat, _ = ln_stats(x)
-    n = (xhat * g_ref[...]).astype(BF16)
+    xhat, _ = ln_stats(x_ref[...].astype(F32))
+    n = (xhat * args_ref[G_S, :]).astype(BF16)
+    n_ref[...] = n
     q, k, v, gating = project(n, w_ref)
     qkv_ref[:, :C] = q
     qkv_ref[:, C : 2 * C] = k
     qkv_ref[:, 2 * C :] = v
     gating_ref[...] = gating
+    for r in range(2):
+        part = slice(r * N, (r + 1) * N)
+        score_ref[part, :] = dot(q[part], stack_heads(k[part], masks), NT)
+    for copy in copies:
+        copy.wait()
+
+
+def start_forward_kernel(
+    recv_ref, x_ref, cot_ref, args_ref, qkv_ref, gating_ref, score_ref, wo_ref,
+    send_ref, mix_ref, prob_ref, first_ref,
+    fscr, plane, sscr, small,
+):
+    n_dst = recv_ref.shape[0]
+    N = 2 * n_dst
+    rows = send_ref.shape[1]
+    fscr[...] = recv_ref[...].astype(F32).reshape(n_dst * 8, C)
+    for r in range(2):
+        for h in range(HEADS):
+            plane[pl.ds(h * N + r, n_dst, stride=2), :] = rows_of(fscr, r * 4 + h, n_dst, 8)
+    masks = head_masks(BF16)
+    kept = args_ref[KEPT, :]
+    x = x_ref[...].astype(F32)
+    v = qkv_ref[:, 2 * C :]
+    gating = gating_ref[...]
     mixes = []
     for r in range(2):
         part = slice(r * N, (r + 1) * N)
-        s = dot(q[part], stack_heads(k[part], masks), NT)
         probs = []
         for h in range(HEADS):
-            w = jnp.exp(s[:, h * N : (h + 1) * N] + plane[h * N : (h + 1) * N, :]) * kept
+            w = jnp.exp(score_ref[part, h * N : (h + 1) * N] + plane[h * N : (h + 1) * N, :]) * kept
             probs.append(w / jnp.sum(w, -1, keepdims=True))
         prob = jnp.concatenate(probs, 1)
         prob_ref[part, :] = prob
@@ -125,7 +170,7 @@
     first_ref[...] = first
     first = first.astype(F32)
     xhat_e, _ = ln_stats(first)
-    plane_e = plane_of((xhat_e * ge_ref[...]).astype(BF16), wte_ref)
+    plane_e = plane_of((xhat_e * args_ref[G_E, :]).astype(BF16), args_ref[WT_E, :])
     small[0:HEADS, :] = plane_e[:, :N]
     small[HEADS : 2 * HEADS, :] = plane_e[:, N:]
     fscr[0 : 2 * N, :] = first
@@ -141,11 +186,11 @@
     send_ref[...] = sscr[...].reshape(n_dst, rows, C).astype(BF16)
 
 
-def put_wide(scr, src, value, row, n_dst, rows):
+def put_wide(scr, src, value, starts, n_dst, rows):
     for t in range(4):
         src[...] = value[:, t * C : (t + 1) * C]
         for i in range(2):
-            scr[pl.ds(row + i * 4 + t, n_dst, stride=rows), :] = rows_of(src, i, n_dst, 2)
+            scr[pl.ds(starts[i] + t, n_dst, stride=rows), :] = rows_of(src, i, n_dst, 2)
 
 
 def put_narrow(scr, src, row, n_dst, rows, each):
@@ -160,9 +205,9 @@
 
 
 def end_kernel(
-    recv_ref, mask_ref, g_ref, w_ref, wo_ref, gt_ref, wu_ref, wd_ref,
-    send_ref,
-    fscr, zscr, cscr, plane, down, narrow, sscr,
+    recv_ref, args_ref, w_ref, wo_ref, wu_ref, wd_ref,
+    send_ref, small_ref, hidden_ref, dup_ref, n_ref, n2_ref, cot_ref, dproj_ref, gated_ref, dsecond_ref,
+    fscr, zscr, cscr, plane, sscr,
 ):
     n_dst, in_rows, _ = recv_ref.shape
     N = 2 * n_dst
@@ -176,12 +221,13 @@
             plane[pl.ds(h * N + r, n_dst, stride=2), :] = rows_of(fscr, 8 + r * 4 + h, n_dst, in_rows)
     masks = head_masks(BF16)
     masks_f = head_masks(F32)
-    length = jnp.sum(mask_ref[...].astype(F32), -1, keepdims=True)
+    gain, gain_t = args_ref[G_E, :], args_ref[G_T, :]
+    length = jnp.sum(args_ref[KEPT, :], -1, keepdims=True)
     kept = (lax.broadcasted_iota(jnp.int32, (N, 1), 0).astype(F32) < length).astype(F32)
     x = zscr[...]
     cot = cscr[...]
     xhat, rstd = ln_stats(x)
-    n = (xhat * g_ref[...]).astype(BF16)
+    n = (xhat * gain).astype(BF16)
     q, k, v, gating = project(n, w_ref)
     saved = []
     mixes = []
@@ -203,7 +249,7 @@
     wo = wo_ref[...].astype(BF16)
     second = (x + dot(gated, wo)).astype(BF16).astype(F32)
     xhat2, rstd2 = ln_stats(second)
-    n2 = (xhat2 * gt_ref[...]).astype(BF16)
+    n2 = (xhat2 * gain_t).astype(BF16)
     wu = wu_ref[...].astype(BF16)
     wd = wd_ref[...].astype(BF16)
     cot_b = cot.astype(BF16)
@@ -213,14 +259,16 @@
     dhidden = dot(cot_b, wd, NT).astype(BF16).astype(F32)
     slope = cdf + up * (jnp.exp(-0.5 * up * up) * 0.3989422804014327)
     dup = (dhidden * slope).astype(BF16)
-    down[...] = dot(hidden, cot_b, TN)
-    put_narrow(sscr, down, 28, n_dst, rows, 8)
-    put_wide(sscr, narrow, dot(n2, dup, TN), 20, n_dst, rows)
+    hidden_ref[...] = hidden
+    dup_ref[...] = dup
+    n_ref[...] = n
+    n2_ref[...] = n2
+    cot_ref[...] = cot_b
+    gated_ref[...] = gated
     dn2 = dot(dup, wu, NT).astype(BF16).astype(F32)
-    dx2, dgain_t = ln_back(dn2, xhat2, rstd2, gt_ref[...])
+    dx2, dgain_t = ln_back(dn2, xhat2, rstd2, gain_t)
     dsecond = (cot + dx2).astype(BF16)
-    narrow[...] = dot(gated, dsecond, TN)
-    put_narrow(sscr, narrow, 36, n_dst, rows, 2)
+    dsecond_ref[...] = dsecond
     dgated = dot(dsecond, wo, NT).astype(BF16).astype(F32)
     dgating = dgated * mix
     dmix = (dgated * gating).astype(BF16)
@@ -247,16 +295,38 @@
         for h in range(HEADS):
             sscr[pl.ds(r * 4 + h, n_dst, stride=rows), :] = rows_of(plane, h * N + r, n_dst, 2)
     dproj = project_cotangent(dq, dk, dv, gating, dgating)
-    put_wide(sscr, narrow, dot(n, dproj, TN), 12, n_dst, rows)
+    dproj_ref[...] = dproj
     dn = dot(dproj, w_ref[...].astype(BF16), NT).astype(BF16).astype(F32)
-    dx, dgain = ln_back(dn, xhat, rstd, g_ref[...])
+    dx, dgain = ln_back(dn, xhat, rstd, gain)
     zscr[...] = dsecond.astype(F32) + dx
     for r in range(2):
         for a in range(2):
             sscr[pl.ds(8 + r * 2 + a, n_dst, stride=rows), :] = rows_of(zscr, a * N + r, n_dst, 2)
-    put_small(sscr, 38, [dgain_t, dgain], n_dst, rows)
-    sscr[pl.ds(39, n_dst, stride=rows), :] = jnp.zeros((n_dst, C), F32)
+    for i in range(12, rows):
+        sscr[pl.ds(i, n_dst, stride=rows), :] = jnp.zeros((n_dst, C), F32)
     send_ref[...] = sscr[...].reshape(n_dst, rows, C).astype(BF16)
+    small_ref[0:1, :] = dgain_t
+    small_ref[1:2, :] = dgain
+    small_ref[2:8, :] = jnp.zeros((6, C), F32)
+
+
+def end_weights_kernel(
+    hidden_ref, dup_ref, n_ref, n2_ref, cot_ref, dproj_ref, gated_ref, dsecond_ref,
+    keep_ref, give_ref,
+    down, narrow, wscr,
+):
+    half = keep_ref.shape[0]
+    n_dst = half // HALF
+    down[...] = dot(hidden_ref[...], cot_ref[...], TN)
+    put_narrow(wscr, down, half + 4, n_dst, HALF, 8)
+    put_wide(wscr, narrow, dot(n2_ref[...], dup_ref[...], TN), (8, half), n_dst, HALF)
+    put_wide(wscr, narrow, dot(n_ref[...], dproj_ref[...], TN), (0, 4), n_dst, HALF)
+    narrow[...] = dot(gated_ref[...], dsecond_ref[...], TN)
+    for i in range(2):
+        wscr[pl.ds(i * half + 12, n_dst, stride=HALF), :] = rows_of(narrow, i, n_dst, 2)
+    core = core_index()
+    keep_ref[...] = wscr[pl.ds(pl.multiple_of(core * half, 8), half), :]
+    give_ref[...] = wscr[pl.ds(pl.multiple_of((1 - core) * half, 8), half), :].astype(BF16)
 
 
 def project_cotangent(dq, dk, dv, gating, dgating):
@@ -268,11 +338,11 @@
     return jnp.concatenate([dq.astype(BF16), dk.astype(BF16), dv.astype(BF16), dg.astype(BF16)], 1)
 
 
-def plane_back(planes, n, xhat, rstd, gain, wt8_ref, p8_ref, wt_ref):
+def plane_back(planes, n, wt8_ref, p8_ref, wt):
     N = planes.shape[1]
     planes = planes.astype(BF16)
     wt8_ref[...] = jnp.zeros_like(wt8_ref)
-    wt8_ref[0:HEADS, :] = wt_ref[...]
+    wt8_ref[0:HEADS, :] = wt
     p8_ref[...] = jnp.zeros_like(p8_ref)
     wide = planes.astype(F32)
     dns = []
@@ -283,34 +353,33 @@
         dns.append(dot(p, wt8_ref[...], TN, FULL))
         dbias = dbias + dot(p.astype(BF16), n[r * N : (r + 1) * N])
     dn = jnp.concatenate(dns, 0).astype(BF16).astype(F32)
-    dx, dgain = ln_back(dn, xhat, rstd, gain)
-    return dx, dgain, dbias[0:HEADS]
+    return dn, dbias[0:HEADS]
 
 
 def start_backward_kernel(
-    recv_ref, x_ref, first_ref, qkv_ref, gating_ref, mix_ref, prob_ref, g_ref, w_ref, wo_ref, ge_ref, wte_ref,
-    send_ref, sum_ref, gsum_ref,
-    fscr, gscr, plane, narrow, sscr, wt8, p8,
+    recv_ref, keep_ref, got_ref, small_ref, n_ref, first_ref, qkv_ref, gating_ref, mix_ref, prob_ref, args_ref, wo_ref,
+    send_ref, dfirst_ref, dproj_ref,
+    fscr, gscr, plane, narrow, sscr, wscr, wt8, p8,
 ):
     n_dst, in_rows, _ = recv_ref.shape
     N = 2 * n_dst
     rows = send_ref.shape[1]
     recv = recv_ref[...].astype(F32)
     total = jnp.sum(recv, 0)
-    sum_ref[...] = total
     fscr[...] = recv.reshape(n_dst * in_rows, C)
     for r in range(2):
         for a in range(2):
             gscr[pl.ds(r * N + a, n_dst, stride=2), :] = rows_of(fscr, 8 + r * 2 + a, n_dst, in_rows)
     first = first_ref[...].astype(F32)
     xhat_e, rstd_e = ln_stats(first)
-    n_e = (xhat_e * ge_ref[...]).astype(BF16)
-    dxe, dgain_e, dbias_e = plane_back(total[0:8], n_e, xhat_e, rstd_e, ge_ref[...], wt8, p8, wte_ref)
+    n_e = (xhat_e * args_ref[G_E, :]).astype(BF16)
+    dn_e, dbias_e = plane_back(total[0:8], n_e, wt8, p8, args_ref[WT_E, :])
+    dxe, dgain_e = ln_back(dn_e, xhat_e, rstd_e, args_ref[G_E, :])
     dfirst = (gscr[...] + dxe).astype(BF16)
+    dfirst_ref[...] = dfirst
     masks = head_masks(BF16)
     masks_f = head_masks(F32)
-    xhat, rstd = ln_stats(x_ref[...].astype(F32))
-    n = (xhat * g_ref[...]).astype(BF16)
+    n = n_ref[...]
     q = qkv_ref[:, :C]
     k = qkv_ref[:, C : 2 * C]
     v = qkv_ref[:, 2 * C :]
@@ -347,87 +416,103 @@
         for h in range(HEADS):
             sscr[pl.ds(r * 4 + h, n_dst, stride=rows), :] = rows_of(plane, h * N + r, n_dst, 2)
     dproj = project_cotangent(dq, dk, dv, gating, dgating)
-    put_wide(sscr, narrow, dot(n, dproj, TN), 8, n_dst, rows)
-    dn = dot(dproj, w_ref[...].astype(BF16), NT).astype(BF16).astype(F32)
-    dx, dgain = ln_back(dn, xhat, rstd, g_ref[...])
-    gsum_ref[...] = dfirst.astype(F32) + dx
-    put_small(sscr, 18, [dbias_e[h : h + 1] for h in range(HEADS)] + [dgain_e, dgain], n_dst, rows)
-    for i in range(19, rows):
-        sscr[pl.ds(i, n_dst, stride=rows), :] = jnp.zeros((n_dst, C), F32)
+    put_wide(sscr, narrow, dot(n, dproj, TN), (8, 12), n_dst, rows)
+    dproj_ref[...] = dproj
+    smalls = [small_ref[0:1, :], small_ref[1:2, :], dgain_e] + [dbias_e[h : h + 1] for h in range(HEADS)]
+    put_small(sscr, 18, smalls, n_dst, rows)
+    wscr[...] = keep_ref[...] + got_ref[...].astype(F32)
+    for i in range(HALF):
+        sscr[pl.ds(19 + i, n_dst, stride=rows), :] = rows_of(wscr, i, n_dst, HALF)
     send_ref[...] = sscr[...].reshape(n_dst, rows, C).astype(BF16)
 
 
-def start_plane_kernel(
-    recv_ref, sum_ref, gsum_ref, x_ref, g_ref, wt_ref, grad_ref, part_ref, wt8, p8
-):
+def start_plane_kernel(recv_ref, dproj_ref, x_ref, w_ref, args_ref, dn_ref, dn_plane_ref, part_ref, wt8, p8):
     total = jnp.sum(recv_ref[...].astype(F32), 0)
+    xhat, _ = ln_stats(x_ref[...].astype(F32))
+    n = (xhat * args_ref[G_S, :]).astype(BF16)
+    dn = dot(dproj_ref[...], w_ref[...].astype(BF16), NT).astype(BF16)
+    dn_ref[...] = dn
+    dn_plane, dbias = plane_back(total[0:8], n, wt8, p8, args_ref[WT_S, :])
+    dn_plane_ref[...] = dn_plane.astype(BF16)
+    part_ref[0:11, :] = total[8:19]
+    part_ref[11:15, :] = dbias
+    part_ref[15:16, :] = jnp.sum((dn_plane + dn.astype(F32)) * xhat, 0, keepdims=True)
+    part_ref[16 : 16 + HALF, :] = total[19 : 19 + HALF]
+    part_ref[16 + HALF : 32, :] = jnp.zeros((16 - HALF, C), F32)
+
+
+def grad_kernel(dn_ref, dn_plane_ref, dfirst_ref, x_ref, args_ref, grad_ref):
     xhat, rstd = ln_stats(x_ref[...].astype(F32))
-    n = (xhat * g_ref[...]).astype(BF16)
-    dx, dgain, dbias = plane_back(total[0:8], n, xhat, rstd, g_ref[...], wt8, p8, wt_ref)
-    grad_ref[...] = (gsum_ref[...] + dx).astype(BF16)
-    part_ref[0:28, :] = sum_ref[12:40, :]
-    part_ref[28:40, :] = total[8:20]
-    part_ref[40:44, :] = dbias
-    part_ref[44:45, :] = dgain
-    part_ref[45:48, :] = jnp.zeros((3, C), F32)
-
-
-def spread_kernel(a_ref, b_ref, c_ref, d_ref, out_ref):
-    total = (a_ref[...] + b_ref[...]) + (c_ref[...] + d_ref[...])
-    out_ref[...] = jnp.broadcast_to(total.astype(BF16)[None], out_ref.shape)
+    dx, _ = ln_back(dn_ref[...].astype(F32), xhat, rstd, args_ref[G_S, :])
+    dx_plane, _ = ln_back(dn_plane_ref[...].astype(F32), xhat, rstd, args_ref[G_S, :])
+    grad_ref[...] = (dfirst_ref[...].astype(F32) + dx + dx_plane).astype(BF16)
+
+
+def spread_kernel(a_ref, b_ref, c_ref, d_ref, out_ref, scr):
+    near = a_ref[...] + c_ref[...]
+    total = near + (b_ref[...] + d_ref[...])
+    scr[0:8, :] = jnp.where(core_index() == 0, total[0:8], total[8:16])
+    scr[8:24, :] = near[16:32]
+    out_ref[...] = jnp.broadcast_to(scr[...].astype(BF16)[None], out_ref.shape)
 
 
 def finish_kernel(
-    factor, recv_ref,
+    factor, recv_ref, other_ref,
     gs_ref, ps_ref, bs_ref, os_ref, ge_ref, pe_ref, be_ref, oe_ref, gt_ref, up_ref, down_ref,
     fscr, block,
 ):
-    n_dst, rows, _ = recv_ref.shape
-    recv = recv_ref[...].astype(F32) * factor
-    fscr[...] = recv.reshape(n_dst * rows, C)
-
-    def wide(ref, row):
+    n_dst, half, _ = recv_ref.shape
+    size = n_dst * half
+    core = core_index()
+    for index, ref in ((core, recv_ref), (1 - core, other_ref)):
+        fscr[pl.ds(pl.multiple_of(index * size, 8), size), :] = ref[...].astype(F32).reshape(size, C) * factor
+
+    def rows(row):
+        return rows_of(fscr, row, n_dst, half)
+
+    def wide(ref, starts):
         for t in range(4):
             for i in range(2):
-                block[pl.ds(i, n_dst, stride=2), :] = rows_of(fscr, row + i * 4 + t, n_dst, rows)
+                block[pl.ds(i, n_dst, stride=2), :] = rows(starts[i] + t)
             ref[:, t * C : (t + 1) * C] = block[...]
 
-    def narrow(ref, row, each):
-        for i in range(each):
-            ref[pl.ds(i, n_dst, stride=each), :] = rows_of(fscr, row + i, n_dst, rows)
-
-    wide(pe_ref, 0)
-    wide(up_ref, 8)
-    narrow(down_ref, 16, 8)
-    narrow(oe_ref, 24, 2)
-    wide(ps_ref, 28)
-    narrow(os_ref, 36, 2)
-    tail = jnp.sum(recv[:, 40:48, :], 0)
-    bs_ref[...] = tail[0:HEADS]
+    def narrow(ref, starts):
+        for i, start in enumerate(starts):
+            ref[pl.ds(i, n_dst, stride=len(starts)), :] = rows(start)
 
     def one(e, row):
-        return fscr[e * rows + row : e * rows + row + 1, :]
-
-    gt_ref[...] = one(0, 26)
+        start = e * half + row
+        return fscr[start : start + 1, :]
+
+    wide(ps_ref, (0, 4))
+    wide(pe_ref, (8, 12))
+    wide(up_ref, (16, size + 8))
+    narrow(down_ref, range(size + 12, size + 20))
+    narrow(os_ref, (size, size + 1))
+    narrow(oe_ref, (20, size + 20))
     for h in range(HEADS):
-        be_ref[h : h + 1, :] = one(h, 38)
-    ge_ref[...] = one(1, 26) + one(4, 38)
-    gs_ref[...] = tail[HEADS : HEADS + 1] + one(5, 38)
+        bs_ref[h : h + 1, :] = jnp.sum(rows(size + 3 + h), 0, keepdims=True)
+        be_ref[h : h + 1, :] = one(3 + h, size + 2)
+    gt_ref[...] = one(0, size + 2)
+    ge_ref[...] = one(1, size + 2) + one(2, size + 2)
+    gs_ref[...] = jnp.sum(rows(size + 7), 0, keepdims=True)
 
 
 def shape(dims, dtype=F32):
     return jax.ShapeDtypeStruct(dims, dtype)
 
 
-def call(body, out_shape, scratch, *operands):
+def call(body, out_shape, scratch, *operands, in_hbm=()):
+    many = isinstance(out_shape, (list, tuple))
     whole = pl.BlockSpec(memory_space=pltpu.VMEM)
-    many = isinstance(out_shape, (list, tuple))
+    spaces = [pltpu.HBM if i in in_hbm else pltpu.VMEM for i in range(len(operands))]
+    operands = [pltpu.with_memory_space_constraint(a, m) if m is pltpu.HBM else a for a, m in zip(operands, spaces)]
     return pl.pallas_call(
         body,
         out_shape=out_shape,
-        in_specs=[whole] * len(operands),
+        in_specs=[pl.BlockSpec(memory_space=m) for m in spaces],
         out_specs=[whole] * len(out_shape) if many else whole,
-        scratch_shapes=[pltpu.VMEM(s, F32) for s in scratch],
+        scratch_shapes=[pltpu.VMEM(s, F32) if isinstance(s, tuple) else s for s in scratch],
         compiler_params=pltpu.CompilerParams(vmem_limit_bytes=VMEM_LIMIT),
     )(*operands)
 
@@ -449,40 +534,67 @@
     tokens = (2 * N, C)
     wide = (C, 4 * C)
 
-    send = call(plane_local_kernel, shape((n_dst, 8, C), BF16), [(8, C)], x, g_s, wt_s)
+    send, args = call(
+        plane_local_kernel,
+        [shape((n_dst, 8, C), BF16), shape((16, C))],
+        [pltpu.VMEM(tokens, BF16), (1, C), (HEADS, C), (1, C), (HEADS, C), (1, C),
+         pltpu.VMEM((1, C), jnp.int32), (8, C), pltpu.SemaphoreType.DMA((7,))],
+        x, g_s, wt_s, g_e, wt_e, g_t, residue_mask,
+        in_hbm=range(7),
+    )
     recv = swap(send)
-    send, qkv, gating, mix, prob, first = call(
+    qkv, gating, score, n, cot, wo = call(
+        start_scores_kernel,
+        [shape((2 * N, 3 * C), BF16), shape(tokens), shape((2 * N, HEADS * N)), shape(tokens, BF16),
+         shape(tokens, BF16), shape((C, C))],
+        [pltpu.SemaphoreType.DMA((2,))],
+        x, cot, args, proj_start, output_start,
+        in_hbm=(1, 4),
+    )
+    send, mix, prob, first = call(
         start_forward_kernel,
-        [shape((n_dst, 16, C), BF16), shape((2 * N, 3 * C), BF16), shape(tokens), shape(tokens),
-         shape((2 * N, HEADS * N)), shape(tokens, BF16)],
+        [shape((n_dst, 16, C), BF16), shape(tokens), shape((2 * N, HEADS * N)), shape(tokens, BF16)],
         [(n_dst * 8, C), (HEADS * N, N), (n_dst * 16, C), (8, C)],
-        recv, x, cot, residue_mask, g_s, proj_start, output_start, g_e, wt_e,
+        recv, x, cot, args, qkv, gating, score, wo,
     )
     recv = swap(send)
-    send = call(
+    n_dp = lax.axis_size("dp")
+    to_core = [(i, i ^ 1) for i in range(n_dp)]
+    half = (n_dst * HALF, C)
+    hidden = (2 * N, 4 * C)
+    send, small, *saved = call(
         end_kernel,
-        shape((n_dst, 40, C), BF16),
-        [(n_dst * 16, C), tokens, tokens, (HEADS * N, N), (4 * C, C), (C, C), (n_dst * 40, C)],
-        recv, residue_mask, g_e, proj_end, output_end, g_t, transition_up, transition_down,
+        [shape((n_dst, 16, C), BF16), shape((8, C)), shape(hidden, BF16), shape(hidden, BF16), shape(tokens, BF16),
+         shape(tokens, BF16), shape(tokens, BF16), shape(hidden, BF16), shape(tokens, BF16), shape(tokens, BF16)],
+        [(n_dst * 16, C), tokens, tokens, (HEADS * N, N), (n_dst * 16, C)],
+        recv, args, proj_end, output_end, transition_up, transition_down,
     )
     recv = swap(send)
-    send, summed, gsum = call(
+    keep, give = call(
+        end_weights_kernel,
+        [shape(half), shape(half, BF16)],
+        [(4 * C, C), (C, C), (n_dst * 2 * HALF, C)],
+        *saved,
+    )
+    got = lax.ppermute(give, "dp", to_core)
+    send, dfirst, dproj = call(
         start_backward_kernel,
-        [shape((n_dst, 24, C), BF16), shape((40, C)), shape(tokens)],
-        [(n_dst * 40, C), tokens, (HEADS * N, N), (C, C), (n_dst * 24, C), (8, C), (8, C)],
-        recv, x, first, qkv, gating, mix, prob, g_s, proj_start, output_start, g_e, wt_e,
+        [shape((n_dst, 32, C), BF16), shape(tokens, BF16), shape(hidden, BF16)],
+        [(n_dst * 16, C), tokens, (HEADS * N, N), (C, C), (n_dst * 32, C), half, (8, C), (8, C)],
+        recv, keep, got, small, n, first, qkv, gating, mix, prob, args, wo,
     )
     recv = swap(send)
-    grad, part = call(
+    dn, dn_plane, part = call(
         start_plane_kernel,
-        [shape(tokens, BF16), shape((48, C))],
+        [shape(tokens, BF16), shape(tokens, BF16), shape((32, C))],
         [(8, C), (8, C)],
-        recv, summed, gsum, x, g_s, wt_s,
-    )
-    n_dp = lax.axis_size("dp")
+        recv, dproj, x, proj_start, args,
+    )
     others = [lax.ppermute(part, "dp", [(i, i ^ d) for i in range(n_dp)]) for d in range(1, n_dp)]
-    send = call(spread_kernel, shape((n_dst, 48, C), BF16), [], part, *others)
+    grad = call(grad_kernel, shape(tokens, BF16), [], dn, dn_plane, dfirst, x, args)
+    send = call(spread_kernel, shape((n_dst, 24, C), BF16), [(24, C)], part, *others)
     recv = swap(send)
+    other = lax.ppermute(recv, "dp", to_core)
     factor = 1.0 / (n_dp * N)
     gs, ps, bs, os, ge, pe, be, oe, gt, up, down = call(
         functools.partial(finish_kernel, factor),
@@ -490,7 +602,7 @@
          shape((1, C)), shape(wide), shape((HEADS, C)), shape((C, C)),
          shape((1, C)), shape(wide), shape((4 * C, C))],
         [(n_dst * 48, C), (C, C)],
-        recv,
+        recv, other,
     )
     return (
         grad.reshape(1, 2, N, C), gs.reshape(C), ps, bs.T, os, ge.reshape(C), pe, be.T, oe, gt.reshape(C), up, down,

time: 133 us -> 118 us (0.89)
  blocking collectives: 104 us -> 52.4 us
  starting transfers between devices: 8.85 us -> 31.5 us
  waiting for transfers between devices: 3.75 us -> 19.5 us
  local copies, waits for them, and re-layouts: 4.88 us -> 0.03 us
  Pallas kernels: 10.2 us -> 13.7 us
    all_to_all x5 -> x3, blocking collectives: 104 us -> 52.4 us  [swap(): lax.all_to_all(buffer, 'dap', split_axis=0, concat_axis=0, tiled=True)]
    all_to_all x0 -> x2, starting transfers between devices: none -> 18.5 us  [swap(): lax.all_to_all(buffer, 'dap', split_axis=0, concat_axis=0, tiled=True)]
    all_to_all x0 -> x2, waiting for transfers between devices: none -> 14.1 us  [swap(): lax.all_to_all(buffer, 'dap', split_axis=0, concat_axis=0, tiled=True)]
    unnamed x34 -> x12, local copies, waits for them, and re-layouts: 4.88 us -> 0.03 us
    ppermute x0 -> x2, starting transfers between devices: none -> 3.57 us  [the longest x1 3.56 us: local(): got = lax.ppermute(give, 'dp', to_core)]
    pallas_call x7 -> x10, Pallas kernels: 10.2 us -> 13.7 us  [call(): pl.pallas_call(body, out_shape=out_shape, in_specs=[pl.BlockSpec(memory_s...]
    ppermute x0 -> x2, waiting for transfers between devices: none -> 1.86 us  [the longest x1 1.09 us: local(): got = lax.ppermute(give, 'dp', to_core)]
  transfers between devices with their start and end apart: 3 -> 7, of which waited for: 2 -> 6; matrix products, arithmetic and copies ran while one was open for 0% -> 0% of each run, Pallas kernels for 0% -> 2%
where the time goes in v2:
time: 118 us
  blocking collectives  52.4 us (44%)
  starting transfers between devices  31.5 us (27%)
  waiting for transfers between devices  19.5 us (17%)
  Pallas kernels  13.7 us (12%)
    all_to_all x3, blocking collectives, swap(): lax.all_to_all(buffer, 'dap', split_axis=0, concat_axis=0, tiled=True)  52.4 us
    all_to_all x2, starting transfers between devices, swap(): lax.all_to_all(buffer, 'dap', split_axis=0, concat_axis=0, tiled=True)  18.5 us
    all_to_all x2, waiting for transfers between devices, swap(): lax.all_to_all(buffer, 'dap', split_axis=0, concat_axis=0, tiled=True)  14.1 us
    pallas_call x10, Pallas kernels, call(): pl.pallas_call(body, out_shape=out_shape, in_specs=[pl.BlockSpec(memory_s...  13.7 us
    ppermute x3, starting transfers between devices, local(): lax.ppermute(part, 'dp', [(i, i ^ d) for i in range(n_dp)])  9.38 us
    ppermute x3, waiting for transfers between devices, local(): lax.ppermute(part, 'dp', [(i, i ^ d) for i in range(n_dp)])  3.6 us
    ppermute x1, starting transfers between devices, local(): got = lax.ppermute(give, 'dp', to_core)  3.56 us
  transfers between devices with their start and end apart: 7, of which 6 were waited for; matrix products, arithmetic and copies ran while one was open for 0% of the time, Pallas kernels for 2%

profile of v2, /device:TPU:1, one launch (start us, length us, event | category | flops | bytes accessed | tf_op | source)
XLA Modules:
  0.0 117.9 jit_solution(553744895385574036)
XLA Ops:
  0.6 0.0 copy-start.1
  0.7 2.0 %shard_map.229 = (bf16[64,8,128]{2,1,0:T(8,128)(2,1)}, f32[16,128]{1,0:T(8,128)S(1)}) custom-call(bf16[256,128]{1,0:T(8,128)(2,1)} %bitcast.13, f32[1,128]{1,0:T(1,128)} %bitcast.22, f32[4,128]{1,0:T(4,128)} %bitcast.20, f32[1,128]{1,0:T(1,128)} %bitcast.23, f32[4,128]{1,0:T(4,128)} %bitcast.21, f32[1,128]{1,0:T(1,128)} %bitcast.24, s32[1,128]{1,0:T(1,128)} %mask_hbm.1), custom_call_target="tpu_custom_call" | custom-call | tf_op jit(solution)/shard_map/pallas_call | solution.py:510
  2.7 0.0 copy-start
  2.7 13.6 %all-to-all-start = ((bf16[64,8,128]{2,1,0:T(8,128)(2,1)}), bf16[64,8,128]{2,1,0:T(8,128)(2,1)S(1)}, u32[]{:S(2)}, u32[]{:S(2)}) async-start(bf16[64,8,128]{2,1,0:T(8,128)(2,1)} %get-tuple-element.53), calls=%async_computation | async-start | bytes 262144 | tf_op jit(solution)/shard_map/all_to_all | solution.py:521
  16.4 0.0 copy-done.1
  16.4 0.0 copy-done
  16.4 1.3 %shard_map.230 = (bf16[256,384]{1,0:T(8,128)(2,1)S(1)}, f32[256,128]{1,0:T(8,128)S(1)}, f32[256,512]{1,0:T(8,128)S(1)}, bf16[256,128]{1,0:T(8,128)(2,1)S(1)}, bf...) custom-call(bf16[256,128]{1,0:T(8,128)(2,1)S(1)} %bitcast.14, bf16[256,128]{1,0:T(8,128)(2,1)} %bitcast.18, ...), custom_call_target="tpu_custom_call" | custom-call | tf_op jit(solution)/shard_map/pallas_call | solution.py:510
  17.7 8.6 %all-to-all-done.recv_ref = bf16[64,8,128]{2,1,0:T(8,128)(2,1)S(1)} async-done(((bf16[64,8,128]{2,1,0:T(8,128)(2,1)}), bf16[64,8,128]{2,1,0:T(8,128)(2,1)S(1)}, u32[]{:S(2)}, u32[]{:S(2)}) %all-to-all-start) | async-done | bytes 131104 | tf_op jit(solution)/shard_map/all_to_all | solution.py:521
  26.3 0.0 copy-start.4
  26.3 0.0 copy-start.5
  26.3 1.1 shard_map.231
  27.4 0.0 copy-start.2
  27.4 0.0 copy-start.3
  27.4 14.7 %all_to_all.25.recv_ref = bf16[64,16,128]{2,1,0:T(8,128)(2,1)S(1)} all-to-all(bf16[64,16,128]{2,1,0:T(8,128)(2,1)S(1)} %get-tuple-element.60), channel_id=1, replica_groups=mesh['dp'=4,'dap'=64] {'dap'}, dimensions={0} | all-to-all | bytes 524288 | tf_op jit(solution)/shard_map/all_to_all | solution.py:521
  42.1 0.0 copy-done.4
  42.1 0.0 copy-done.5
  42.1 0.0 copy-done.2
  42.1 0.0 copy-done.3
  42.2 3.7 %shard_map.232 = (bf16[64,16,128]{2,1,0:T(8,128)(2,1)}, f32[8,128]{1,0:T(8,128)S(1)}, bf16[256,512]{1,0:T(8,128)(2,1)S(1)}, bf16[256,512]{1,0:T(8,128)(2,1)S(1)}...) custom-call(bf16[64,16,128]{2,1,0:T(8,128)(2,1)S(1)} %all_to_all.25., ...), custom_call_target="tpu_custom_call" | custom-call | tf_op jit(solution)/shard_map/pallas_call | solution.py:510
  45.8 4.9 %all-to-all-start.2 = ((bf16[64,16,128]{2,1,0:T(8,128)(2,1)}), bf16[64,16,128]{2,1,0:T(8,128)(2,1)S(1)}, u32[]{:S(2)}, u32[]{:S(2)}) async-start(bf16[64,16,128]{2,1,0:T(8,128)(2,1)} %get-tuple-element.61), calls=%async_computation.2 | async-start | bytes 524288 | tf_op jit(solution)/shard_map/all_to_all | solution.py:521
  50.7 0.5 shard_map.233
  51.2 3.6 %collective-permute-start = (bf16[832,128]{1,0:T(8,128)(2,1)S(1)}, bf16[832,128]{1,0:T(8,128)(2,1)S(1)}, u32[]{:S(2)}, u32[]{:S(2)}) collective-permute-start(bf16[832,128]{1,0:T(8,128)(2,1)S(1)} %get-tuple-element.71), channel_id=1, source_target_pairs={{0,64},{64,0},{128,192},{192,128},{1,65},{65,1},{129,193},{193,129... | collective-permute-start | bytes 638984 | tf_op jit(solution)/shard_map/ppermute | solution.py:579
  54.7 1.1 collective-permute-done.got_ref
  55.8 5.5 %all-to-all-done.2.recv_ref = bf16[64,16,128]{2,1,0:T(8,128)(2,1)S(1)} async-done(((bf16[64,16,128]{2,1,0:T(8,128)(2,1)}), bf16[64,16,128]{2,1,0:T(8,128)(2,1)S(1)}, u32[]{:S(2)}, u32[]{:S(2)}) %all-to-all-start.2) | async-done | bytes 262176 | tf_op jit(solution)/shard_map/all_to_all | solution.py:521
  61.3 2.3 %shard_map.234 = (bf16[64,32,128]{2,1,0:T(8,128)(2,1)S(1)}, bf16[256,128]{1,0:T(8,128)(2,1)S(1)}, bf16[256,512]{1,0:T(8,128)(2,1)S(1)}) custom-call(bf16[64,16,128]{2,1,0:T(8,128)(2,1)S(1)} %all-to-all-done.2.recv_ref, f32[832,128]{1,0:T(8,128)S(1)} %get-tuple-element.70.keep_ref, bf16[832,128]{1,0:T(8,128)(2,1)S(1)} %collective-permute-done.got_ref, ...), custom_call_target="tpu_custom_call" | custom-call | tf_op jit(solution)/shard_map/pallas_call | solution.py:510
  63.6 17.9 %all_to_all.26.recv_ref = bf16[64,32,128]{2,1,0:T(8,128)(2,1)S(1)} all-to-all(bf16[64,32,128]{2,1,0:T(8,128)(2,1)S(1)} %get-tuple-element.77), channel_id=1, replica_groups=mesh['dp'=4,'dap'=64] {'dap'}, dimensions={0} | all-to-all | bytes 1048576 | tf_op jit(solution)/shard_map/all_to_all | solution.py:521
  81.5 0.5 shard_map.235
  82.0 8.9 %collective-permute-start.3 = (f32[32,128]{1,0:T(8,128)S(1)}, f32[32,128]{1,0:T(8,128)S(1)}, u32[]{:S(2)}, u32[]{:S(2)}) collective-permute-start(f32[32,128]{1,0:T(8,128)S(1)} %get-tuple-element.82.a_ref), channel_id=1, source_target_pairs={{0,192},{64,128},{128,64},{192,0},{1,193},{65,129},{129,65},{193,1... | collective-permute-start | bytes 49160 | tf_op jit(solution)/shard_map/ppermute | solution.py:593
  90.9 0.3 collective-permute-start.2
  91.3 0.1 collective-permute-start.1
  91.4 1.3 %collective-permute-done.3.d_ref = f32[32,128]{1,0:T(8,128)S(1)} collective-permute-done((f32[32,128]{1,0:T(8,128)S(1)}, f32[32,128]{1,0:T(8,128)S(1)}, u32[]{:S(2)}, u32[]{:S(2)}) %collective-permute-start.3) | collective-permute-done | bytes 16416 | tf_op jit(solution)/shard_map/ppermute | solution.py:593
  92.8 2.2 %collective-permute-done.2.c_ref = f32[32,128]{1,0:T(8,128)S(1)} collective-permute-done((f32[32,128]{1,0:T(8,128)S(1)}, f32[32,128]{1,0:T(8,128)S(1)}, u32[]{:S(2)}, u32[]{:S(2)}) %collective-permute-start.2) | collective-permute-done | bytes 16416 | tf_op jit(solution)/shard_map/ppermute | solution.py:593
  95.0 0.0 collective-permute-done.1.b_ref
  95.1 19.8 %all_to_all.27.recv_ref = bf16[64,24,128]{2,1,0:T(8,128)(2,1)S(1)} all-to-all(bf16[64,24,128]{2,1,0:T(8,128)(2,1)S(1)} %shard_map.237), channel_id=1, replica_groups=mesh['dp'=4,'dap'=64] {'dap'}, dimensions={0} | all-to-all | bytes 786432 | tf_op jit(solution)/shard_map/all_to_all | solution.py:521
  114.8 0.0 collective-permute-start.4
  114.8 1.0 shard_map.236
  115.8 0.8 collective-permute-done.4.other_ref
  116.6 1.3 %shard_map.238 = (f32[1,128]{1,0:T(1,128)}, f32[128,512]{1,0:T(8,128)}, f32[4,128]{1,0:T(4,128)}, f32[128,128]{1,0:T(8,128)}, f32[1,128]{1,0:T(1,128)}, /*index=...) custom-call(bf16[64,24,128]{2,1,0:T(8,128)(2,1)S(1)} %all_to_all.27., ...), custom_call_target="tpu_custom_call" | custom-call | tf_op jit(solution)/shard_map/pallas_call | solution.py:510
  (1 shorter events, 0.0 us)
Async XLA Ops:
  0.6 15.7 %copy-start.1 = (f32[128,512]{1,0:T(8,128)S(1)}, f32[128,512]{1,0:T(8,128)}, u32[]{:S(2)}) copy-start(f32[128,512]{1,0:T(8,128)} %w_ref.5) | copy-start | bytes 786436
  2.7 13.7 %copy-start = (bf16[1,2,128,128]{3,2,1,0:T(8,128)(2,1)S(1)}, bf16[1,2,128,128]{3,2,1,0:T(8,128)(2,1)}, u32[]{:S(2)}) copy-start(bf16[1,2,128,128]{3,2,1,0:T(8,128)(2,1)} %param.14) | copy-start | bytes 196612
  2.7 23.5 %all-to-all-start = ((bf16[64,8,128]{2,1,0:T(8,128)(2,1)}), bf16[64,8,128]{2,1,0:T(8,128)(2,1)S(1)}, u32[]{:S(2)}, u32[]{:S(2)}) async-start(bf16[64,8,128]{2,1,0:T(8,128)(2,1)} %get-tuple-element.53), calls=%async_computation | async-start | bytes 262144 | tf_op jit(solution)/shard_map/all_to_all | solution.py:521
  26.3 15.9 %copy-start.4 = (f32[512,128]{1,0:T(8,128)S(1)}, f32[512,128]{1,0:T(8,128)}, u32[]{:S(2)}) copy-start(f32[512,128]{1,0:T(8,128)} %wd_ref.1) | copy-start | bytes 786436
  26.3 15.9 %copy-start.5 = (f32[128,128]{1,0:T(8,128)S(1)}, f32[128,128]{1,0:T(8,128)}, u32[]{:S(2)}) copy-start(f32[128,128]{1,0:T(8,128)} %wo_ref.1) | copy-start | bytes 196612
  27.4 14.7 %copy-start.2 = (f32[128,512]{1,0:T(8,128)S(1)}, f32[128,512]{1,0:T(8,128)}, u32[]{:S(2)}) copy-start(f32[128,512]{1,0:T(8,128)} %w_ref.4) | copy-start | bytes 786436
  27.4 14.7 %copy-start.3 = (f32[128,512]{1,0:T(8,128)S(1)}, f32[128,512]{1,0:T(8,128)}, u32[]{:S(2)}) copy-start(f32[128,512]{1,0:T(8,128)} %wu_ref.1) | copy-start | bytes 786436
  45.8 15.5 %all-to-all-start.2 = ((bf16[64,16,128]{2,1,0:T(8,128)(2,1)}), bf16[64,16,128]{2,1,0:T(8,128)(2,1)S(1)}, u32[]{:S(2)}, u32[]{:S(2)}) async-start(bf16[64,16,128]{2,1,0:T(8,128)(2,1)} %get-tuple-element.61), calls=%async_computation.2 | async-start | bytes 524288 | tf_op jit(solution)/shard_map/all_to_all | solution.py:521
  51.2 4.7 %collective-permute-start = (bf16[832,128]{1,0:T(8,128)(2,1)S(1)}, bf16[832,128]{1,0:T(8,128)(2,1)S(1)}, u32[]{:S(2)}, u32[]{:S(2)}) collective-permute-start(bf16[832,128]{1,0:T(8,128)(2,1)S(1)} %get-tuple-element.71), channel_id=1, source_target_pairs={{0,64},{64,0},{128,192},{192,128},{1,65},{65,1},{129,193},{193,129... | collective-permute-start | bytes 638984 | tf_op jit(solution)/shard_map/ppermute | solution.py:579
  82.0 10.7 %collective-permute-start.3 = (f32[32,128]{1,0:T(8,128)S(1)}, f32[32,128]{1,0:T(8,128)S(1)}, u32[]{:S(2)}, u32[]{:S(2)}) collective-permute-start(f32[32,128]{1,0:T(8,128)S(1)} %get-tuple-element.82.a_ref), channel_id=1, source_target_pairs={{0,192},{64,128},{128,64},{192,0},{1,193},{65,129},{129,65},{193,1... | collective-permute-start | bytes 49160 | tf_op jit(solution)/shard_map/ppermute | solution.py:593
  90.9 4.1 %collective-permute-start.2 = (f32[32,128]{1,0:T(8,128)S(1)}, f32[32,128]{1,0:T(8,128)S(1)}, u32[]{:S(2)}, u32[]{:S(2)}) collective-permute-start(f32[32,128]{1,0:T(8,128)S(1)} %get-tuple-element.82.a_ref), channel_id=1, source_target_pairs={{0,128},{64,192},{128,0},{192,64},{1,129},{65,193},{129,1},{193,65... | collective-permute-start | bytes 49160 | tf_op jit(solution)/shard_map/ppermute | solution.py:593
  91.3 3.7 %collective-permute-start.1 = (f32[32,128]{1,0:T(8,128)S(1)}, f32[32,128]{1,0:T(8,128)S(1)}, u32[]{:S(2)}, u32[]{:S(2)}) collective-permute-start(f32[32,128]{1,0:T(8,128)S(1)} %get-tuple-element.82.a_ref), channel_id=1, source_target_pairs={{0,64},{64,0},{128,192},{192,128},{1,65},{65,1},{129,193},{193,129... | collective-permute-start | bytes 49160 | tf_op jit(solution)/shard_map/ppermute | solution.py:593
  114.8 1.7 %collective-permute-start.4 = (bf16[64,24,128]{2,1,0:T(8,128)(2,1)S(1)}, bf16[64,24,128]{2,1,0:T(8,128)(2,1)S(1)}, u32[]{:S(2)}, u32[]{:S(2)}) collective-permute-start(bf16[64,24,128]{2,1,0:T(8,128)(2,1)S(1)} %all_to_all.27.recv_ref), channel_id=1, source_target_pairs={{0,64},{64,0},{128,192},{192,128},{1,65},{65,1},{129,193},{193,129... | collective-permute-start | bytes 1179656 | tf_op jit(solution)/shard_map/ppermute | solution.py:597

commit v3 on v2

--- a/solution.py
+++ b/solution.py
@@ -13,12 +13,11 @@
 BF16 = jnp.bfloat16
 C = 128
 HALF = 13
-FULL = lax.Precision.HIGHEST
 VMEM_LIMIT = 48 * 1024 * 1024
 
 
-def dot(a, b, contract=((1,), (0,)), precision=None):
-    return lax.dot_general(a, b, (contract, ((), ())), precision=precision, preferred_element_type=F32)
+def dot(a, b, contract=((1,), (0,))):
+    return lax.dot_general(a, b, (contract, ((), ())), preferred_element_type=F32)
 
 
 NN = ((1,), (0,))
@@ -68,8 +67,18 @@
     return q, k, v, jax.nn.sigmoid(proj[:, 3 * C :])
 
 
-def plane_of(n, wt):
-    return dot(wt, n.astype(F32), NT, FULL)
+def split(scr, wt):
+    for i in range(3):
+        part = wt.astype(BF16).astype(F32)
+        scr[i * HEADS : (i + 1) * HEADS, :] = part
+        wt = wt - part
+    scr[3 * HEADS : 16, :] = jnp.zeros((16 - 3 * HEADS, C), F32)
+    return scr[...].astype(BF16)
+
+
+def plane_of(n, parts):
+    out = dot(parts, n, NT)
+    return out[0:4] + out[4:8] + out[8:12]
 
 
 def core_index():
@@ -80,14 +89,14 @@
     return ref[pl.ds(start, count, stride=stride), :]
 
 
-WT_S, WT_E = slice(0, 4), slice(4, 8)
-G_S, G_E, G_T, KEPT = slice(8, 9), slice(9, 10), slice(10, 11), slice(11, 12)
+WT_S, WT_E = slice(0, 16), slice(16, 32)
+G_S, G_E, G_T, KEPT = slice(0, 1), slice(1, 2), slice(2, 3), slice(3, 4)
 
 
 def plane_local_kernel(
     x_hbm, gs_hbm, wts_hbm, ge_hbm, wte_hbm, gt_hbm, mask_hbm,
-    out_ref, args_ref,
-    x_ref, gs, wts, ge, wte, gt, mask, small, sems,
+    out_ref, args_ref, parts_ref,
+    x_ref, gs, wts, ge, wte, gt, mask, small, scr, sems,
 ):
     n_dst, rows, _ = out_ref.shape
     moves = [(gs_hbm, gs), (wts_hbm, wts), (x_hbm, x_ref), (ge_hbm, ge), (wte_hbm, wte), (gt_hbm, gt), (mask_hbm, mask)]
@@ -96,16 +105,16 @@
         copy.start()
     for copy in copies:
         copy.wait()
-    args_ref[WT_S, :] = wts[...]
-    args_ref[WT_E, :] = wte[...]
+    parts_ref[WT_S, :] = split(scr, wts[...])
+    parts_ref[WT_E, :] = split(scr, wte[...])
     args_ref[G_S, :] = gs[...]
     args_ref[G_E, :] = ge[...]
     args_ref[G_T, :] = gt[...]
     args_ref[KEPT, :] = mask[...].astype(F32)
-    args_ref[12:16, :] = jnp.zeros((4, C), F32)
+    args_ref[4:8, :] = jnp.zeros((4, C), F32)
     xhat, _ = ln_stats(x_ref[...].astype(F32))
     n = (xhat * gs[...]).astype(BF16)
-    plane = plane_of(n, wts[...])
+    plane = plane_of(n, parts_ref[WT_S, :])
     small[0:HEADS, :] = plane[:, :C]
     small[HEADS : 2 * HEADS, :] = plane[:, C:]
     out_ref[...] = jnp.broadcast_to(small[...].astype(BF16)[None], (n_dst, rows, C))
@@ -137,7 +146,7 @@
 
 
 def start_forward_kernel(
-    recv_ref, x_ref, cot_ref, args_ref, qkv_ref, gating_ref, score_ref, wo_ref,
+    recv_ref, x_ref, cot_ref, args_ref, parts_ref, qkv_ref, gating_ref, score_ref, wo_ref,
     send_ref, mix_ref, prob_ref, first_ref,
     fscr, plane, sscr, small,
 ):
@@ -170,7 +179,7 @@
     first_ref[...] = first
     first = first.astype(F32)
     xhat_e, _ = ln_stats(first)
-    plane_e = plane_of((xhat_e * args_ref[G_E, :]).astype(BF16), args_ref[WT_E, :])
+    plane_e = plane_of((xhat_e * args_ref[G_E, :]).astype(BF16), parts_ref[WT_E, :])
     small[0:HEADS, :] = plane_e[:, :N]
     small[HEADS : 2 * HEADS, :] = plane_e[:, N:]
     fscr[0 : 2 * N, :] = first
@@ -338,28 +347,24 @@
     return jnp.concatenate([dq.astype(BF16), dk.astype(BF16), dv.astype(BF16), dg.astype(BF16)], 1)
 
 
-def plane_back(planes, n, wt8_ref, p8_ref, wt):
+def plane_back(planes, n, p_ref, parts):
     N = planes.shape[1]
-    planes = planes.astype(BF16)
-    wt8_ref[...] = jnp.zeros_like(wt8_ref)
-    wt8_ref[0:HEADS, :] = wt
-    p8_ref[...] = jnp.zeros_like(p8_ref)
-    wide = planes.astype(F32)
+    p_ref[...] = jnp.zeros_like(p_ref)
     dns = []
     dbias = 0.0
     for r in range(2):
-        p8_ref[0:HEADS, :] = wide[r * HEADS : (r + 1) * HEADS, :]
-        p = p8_ref[...]
-        dns.append(dot(p, wt8_ref[...], TN, FULL))
-        dbias = dbias + dot(p.astype(BF16), n[r * N : (r + 1) * N])
-    dn = jnp.concatenate(dns, 0).astype(BF16).astype(F32)
-    return dn, dbias[0:HEADS]
+        for i in range(3):
+            p_ref[i * HEADS : (i + 1) * HEADS, :] = planes[r * HEADS : (r + 1) * HEADS]
+        p = p_ref[...].astype(BF16)
+        dns.append(dot(p, parts, TN))
+        dbias = dbias + dot(p, n[r * N : (r + 1) * N])
+    return jnp.concatenate(dns, 0).astype(BF16).astype(F32), dbias[0:HEADS]
 
 
 def start_backward_kernel(
-    recv_ref, keep_ref, got_ref, small_ref, n_ref, first_ref, qkv_ref, gating_ref, mix_ref, prob_ref, args_ref, wo_ref,
+    recv_ref, keep_ref, got_ref, small_ref, n_ref, first_ref, qkv_ref, gating_ref, mix_ref, prob_ref, args_ref, parts_ref, wo_ref,
     send_ref, dfirst_ref, dproj_ref,
-    fscr, gscr, plane, narrow, sscr, wscr, wt8, p8,
+    fscr, gscr, plane, narrow, sscr, wscr, p_ref,
 ):
     n_dst, in_rows, _ = recv_ref.shape
     N = 2 * n_dst
@@ -373,7 +378,7 @@
     first = first_ref[...].astype(F32)
     xhat_e, rstd_e = ln_stats(first)
     n_e = (xhat_e * args_ref[G_E, :]).astype(BF16)
-    dn_e, dbias_e = plane_back(total[0:8], n_e, wt8, p8, args_ref[WT_E, :])
+    dn_e, dbias_e = plane_back(total[0:8], n_e, p_ref, parts_ref[WT_E, :])
     dxe, dgain_e = ln_back(dn_e, xhat_e, rstd_e, args_ref[G_E, :])
     dfirst = (gscr[...] + dxe).astype(BF16)
     dfirst_ref[...] = dfirst
@@ -426,13 +431,13 @@
     send_ref[...] = sscr[...].reshape(n_dst, rows, C).astype(BF16)
 
 
-def start_plane_kernel(recv_ref, dproj_ref, x_ref, w_ref, args_ref, dn_ref, dn_plane_ref, part_ref, wt8, p8):
+def start_plane_kernel(recv_ref, dproj_ref, x_ref, w_ref, args_ref, parts_ref, dn_ref, dn_plane_ref, part_ref, p_ref):
     total = jnp.sum(recv_ref[...].astype(F32), 0)
     xhat, _ = ln_stats(x_ref[...].astype(F32))
     n = (xhat * args_ref[G_S, :]).astype(BF16)
     dn = dot(dproj_ref[...], w_ref[...].astype(BF16), NT).astype(BF16)
     dn_ref[...] = dn
-    dn_plane, dbias = plane_back(total[0:8], n, wt8, p8, args_ref[WT_S, :])
+    dn_plane, dbias = plane_back(total[0:8], n, p_ref, parts_ref[WT_S, :])
     dn_plane_ref[...] = dn_plane.astype(BF16)
     part_ref[0:11, :] = total[8:19]
     part_ref[11:15, :] = dbias
@@ -458,9 +463,16 @@
 
 def finish_kernel(
     factor, recv_ref, other_ref,
+    gs_out, ps_out, bs_out, os_out, ge_out, pe_out, be_out, oe_out, gt_out, up_out, down_out,
     gs_ref, ps_ref, bs_ref, os_ref, ge_ref, pe_ref, be_ref, oe_ref, gt_ref, up_ref, down_ref,
-    fscr, block,
-):
+    fscr, block, sems,
+):
+    copies = []
+
+    def leave(ref, out):
+        copies.append(pltpu.make_async_copy(ref, out, sems.at[len(copies)]))
+        copies[-1].start()
+
     n_dst, half, _ = recv_ref.shape
     size = n_dst * half
     core = core_index()
@@ -485,26 +497,36 @@
         return fscr[start : start + 1, :]
 
     wide(ps_ref, (0, 4))
+    leave(ps_ref, ps_out)
     wide(pe_ref, (8, 12))
+    leave(pe_ref, pe_out)
     wide(up_ref, (16, size + 8))
+    leave(up_ref, up_out)
     narrow(down_ref, range(size + 12, size + 20))
+    leave(down_ref, down_out)
     narrow(os_ref, (size, size + 1))
+    leave(os_ref, os_out)
     narrow(oe_ref, (20, size + 20))
+    leave(oe_ref, oe_out)
     for h in range(HEADS):
         bs_ref[h : h + 1, :] = jnp.sum(rows(size + 3 + h), 0, keepdims=True)
         be_ref[h : h + 1, :] = one(3 + h, size + 2)
     gt_ref[...] = one(0, size + 2)
     ge_ref[...] = one(1, size + 2) + one(2, size + 2)
     gs_ref[...] = jnp.sum(rows(size + 7), 0, keepdims=True)
+    for ref, out in ((bs_ref, bs_out), (be_ref, be_out), (gt_ref, gt_out), (ge_ref, ge_out), (gs_ref, gs_out)):
+        leave(ref, out)
+    for copy in copies:
+        copy.wait()
 
 
 def shape(dims, dtype=F32):
     return jax.ShapeDtypeStruct(dims, dtype)
 
 
-def call(body, out_shape, scratch, *operands, in_hbm=()):
+def call(body, out_shape, scratch, *operands, in_hbm=(), out=pltpu.VMEM):
     many = isinstance(out_shape, (list, tuple))
-    whole = pl.BlockSpec(memory_space=pltpu.VMEM)
+    whole = pl.BlockSpec(memory_space=out)
     spaces = [pltpu.HBM if i in in_hbm else pltpu.VMEM for i in range(len(operands))]
     operands = [pltpu.with_memory_space_constraint(a, m) if m is pltpu.HBM else a for a, m in zip(operands, spaces)]
     return pl.pallas_call(
@@ -534,11 +556,11 @@
     tokens = (2 * N, C)
     wide = (C, 4 * C)
 
-    send, args = call(
+    send, args, parts = call(
         plane_local_kernel,
-        [shape((n_dst, 8, C), BF16), shape((16, C))],
+        [shape((n_dst, 8, C), BF16), shape((8, C)), shape((32, C), BF16)],
         [pltpu.VMEM(tokens, BF16), (1, C), (HEADS, C), (1, C), (HEADS, C), (1, C),
-         pltpu.VMEM((1, C), jnp.int32), (8, C), pltpu.SemaphoreType.DMA((7,))],
+         pltpu.VMEM((1, C), jnp.int32), (8, C), (16, C), pltpu.SemaphoreType.DMA((7,))],
         x, g_s, wt_s, g_e, wt_e, g_t, residue_mask,
         in_hbm=range(7),
     )
@@ -555,7 +577,7 @@
         start_forward_kernel,
         [shape((n_dst, 16, C), BF16), shape(tokens), shape((2 * N, HEADS * N)), shape(tokens, BF16)],
         [(n_dst * 8, C), (HEADS * N, N), (n_dst * 16, C), (8, C)],
-        recv, x, cot, args, qkv, gating, score, wo,
+        recv, x, cot, args, parts, qkv, gating, score, wo,
     )
     recv = swap(send)
     n_dp = lax.axis_size("dp")
@@ -580,29 +602,31 @@
     send, dfirst, dproj = call(
         start_backward_kernel,
         [shape((n_dst, 32, C), BF16), shape(tokens, BF16), shape(hidden, BF16)],
-        [(n_dst * 16, C), tokens, (HEADS * N, N), (C, C), (n_dst * 32, C), half, (8, C), (8, C)],
-        recv, keep, got, small, n, first, qkv, gating, mix, prob, args, wo,
+        [(n_dst * 16, C), tokens, (HEADS * N, N), (C, C), (n_dst * 32, C), half, (16, C)],
+        recv, keep, got, small, n, first, qkv, gating, mix, prob, args, parts, wo,
     )
     recv = swap(send)
     dn, dn_plane, part = call(
         start_plane_kernel,
         [shape(tokens, BF16), shape(tokens, BF16), shape((32, C))],
-        [(8, C), (8, C)],
-        recv, dproj, x, proj_start, args,
+        [(16, C)],
+        recv, dproj, x, proj_start, args, parts,
     )
     others = [lax.ppermute(part, "dp", [(i, i ^ d) for i in range(n_dp)]) for d in range(1, n_dp)]
     grad = call(grad_kernel, shape(tokens, BF16), [], dn, dn_plane, dfirst, x, args)
+    grad, *others = lax.optimization_barrier((grad, *others))
     send = call(spread_kernel, shape((n_dst, 24, C), BF16), [(24, C)], part, *others)
     recv = swap(send)
     other = lax.ppermute(recv, "dp", to_core)
     factor = 1.0 / (n_dp * N)
+    vector, bias, square, tall = (1, C), (HEADS, C), (C, C), (4 * C, C)
+    sizes = [vector, wide, bias, square, vector, wide, bias, square, vector, wide, tall]
     gs, ps, bs, os, ge, pe, be, oe, gt, up, down = call(
         functools.partial(finish_kernel, factor),
-        [shape((1, C)), shape(wide), shape((HEADS, C)), shape((C, C)),
-         shape((1, C)), shape(wide), shape((HEADS, C)), shape((C, C)),
-         shape((1, C)), shape(wide), shape((4 * C, C))],
-        [(n_dst * 48, C), (C, C)],
+        [shape(size) for size in sizes],
+        [*sizes, (n_dst * 48, C), square, pltpu.SemaphoreType.DMA((len(sizes),))],
         recv, other,
+        out=pltpu.HBM,
     )
     return (
         grad.reshape(1, 2, N, C), gs.reshape(C), ps, bs.T, os, ge.reshape(C), pe, be.T, oe, gt.reshape(C), up, down,

time: 118 us -> 118 us (level)
  no operation moved by 1% of the time
where the time goes in v3:
time: 118 us; the launch traced here: 117 us
  blocking collectives  52.4 us (44%)
  starting transfers between devices  31.4 us (27%)
  waiting for transfers between devices  19.5 us (17%)
  Pallas kernels  13.2 us (11%)
    all_to_all x3, blocking collectives, swap(): lax.all_to_all(buffer, 'dap', split_axis=0, concat_axis=0, tiled=True)  52.4 us
    all_to_all x2, starting transfers between devices, swap(): lax.all_to_all(buffer, 'dap', split_axis=0, concat_axis=0, tiled=True)  18.5 us
    all_to_all x2, waiting for transfers between devices, swap(): lax.all_to_all(buffer, 'dap', split_axis=0, concat_axis=0, tiled=True)  14.1 us
    pallas_call x10, Pallas kernels, call(): pl.pallas_call(body, out_shape=out_shape, in_specs=[pl.BlockSpec(memory_s...  13.2 us
    ppermute x3, starting transfers between devices, local(): lax.ppermute(part, 'dp', [(i, i ^ d) for i in range(n_dp)])  9.39 us
    ppermute x1, starting transfers between devices, local(): got = lax.ppermute(give, 'dp', to_core)  3.56 us
    ppermute x3, waiting for transfers between devices, local(): lax.ppermute(part, 'dp', [(i, i ^ d) for i in range(n_dp)])  2.65 us
  transfers between devices with their start and end apart: 7, of which 6 were waited for; matrix products, arithmetic and copies ran while one was open for 0% of the time, Pallas kernels for 2%

profile of v3, /device:TPU:1, one launch (start us, length us, event | category | flops | bytes accessed | tf_op | source)
XLA Modules:
  0.0 117.4 jit_solution(5376952571324971077)
XLA Ops:
  0.6 0.0 copy-start.1
  0.7 2.0 %shard_map.229 = (bf16[64,8,128]{2,1,0:T(8,128)(2,1)}, f32[8,128]{1,0:T(8,128)S(1)}, bf16[32,128]{1,0:T(8,128)(2,1)S(1)}) custom-call(bf16[256,128]{1,0:T(8,128)(2,1)} %bitcast.13, f32[1,128]{1,0:T(1,128)} %bitcast.22, f32[4,128]{1,0:T(4,128)} %bitcast.20, f32[1,128]{1,0:T(1,128)} %bitcast.23, f32[4,128]{1,0:T(4,128)} %bitcast.21, f32[1,128]{1,0:T(1,128)} %bitcast.24, ...), custom_call_target="tpu_custom_call" | custom-call | tf_op jit(solution)/shard_map/pallas_call | solution.py:532
  2.6 0.0 copy-start
  2.6 13.6 %all-to-all-start = ((bf16[64,8,128]{2,1,0:T(8,128)(2,1)}), bf16[64,8,128]{2,1,0:T(8,128)(2,1)S(1)}, u32[]{:S(2)}, u32[]{:S(2)}) async-start(bf16[64,8,128]{2,1,0:T(8,128)(2,1)} %get-tuple-element.58), calls=%async_computation | async-start | bytes 262144 | tf_op jit(solution)/shard_map/all_to_all | solution.py:543
  16.3 0.0 copy-done.1
  16.3 0.0 copy-done
  16.3 1.3 %shard_map.230 = (bf16[256,384]{1,0:T(8,128)(2,1)S(1)}, f32[256,128]{1,0:T(8,128)S(1)}, f32[256,512]{1,0:T(8,128)S(1)}, bf16[256,128]{1,0:T(8,128)(2,1)S(1)}, bf...) custom-call(bf16[256,128]{1,0:T(8,128)(2,1)S(1)} %bitcast.14, bf16[256,128]{1,0:T(8,128)(2,1)} %bitcast.18, ...), custom_call_target="tpu_custom_call" | custom-call | tf_op jit(solution)/shard_map/pallas_call | solution.py:532
  17.6 8.6 %all-to-all-done.recv_ref = bf16[64,8,128]{2,1,0:T(8,128)(2,1)S(1)} async-done(((bf16[64,8,128]{2,1,0:T(8,128)(2,1)}), bf16[64,8,128]{2,1,0:T(8,128)(2,1)S(1)}, u32[]{:S(2)}, u32[]{:S(2)}) %all-to-all-start) | async-done | bytes 131104 | tf_op jit(solution)/shard_map/all_to_all | solution.py:543
  26.2 0.0 copy-start.4
  26.2 0.0 copy-start.5
  26.2 1.0 shard_map.231
  27.2 0.0 copy-start.2
  27.2 0.0 copy-start.3
  27.2 14.7 %all_to_all.25.recv_ref = bf16[64,16,128]{2,1,0:T(8,128)(2,1)S(1)} all-to-all(bf16[64,16,128]{2,1,0:T(8,128)(2,1)S(1)} %get-tuple-element.66), channel_id=1, replica_groups=mesh['dp'=4,'dap'=64] {'dap'}, dimensions={0} | all-to-all | bytes 524288 | tf_op jit(solution)/shard_map/all_to_all | solution.py:543
  41.9 0.0 copy-done.4
  41.9 0.0 copy-done.5
  41.9 0.0 copy-done.2
  41.9 0.0 copy-done.3
  42.0 3.7 %shard_map.232 = (bf16[64,16,128]{2,1,0:T(8,128)(2,1)}, f32[8,128]{1,0:T(8,128)S(1)}, bf16[256,512]{1,0:T(8,128)(2,1)S(1)}, bf16[256,512]{1,0:T(8,128)(2,1)S(1)}...) custom-call(bf16[64,16,128]{2,1,0:T(8,128)(2,1)S(1)} %all_to_all.25., ...), custom_call_target="tpu_custom_call" | custom-call | tf_op jit(solution)/shard_map/pallas_call | solution.py:532
  45.6 4.8 %all-to-all-start.2 = ((bf16[64,16,128]{2,1,0:T(8,128)(2,1)}), bf16[64,16,128]{2,1,0:T(8,128)(2,1)S(1)}, u32[]{:S(2)}, u32[]{:S(2)}) async-start(bf16[64,16,128]{2,1,0:T(8,128)(2,1)} %get-tuple-element.67), calls=%async_computation.2 | async-start | bytes 524288 | tf_op jit(solution)/shard_map/all_to_all | solution.py:543
  50.5 0.5 shard_map.233
  51.0 3.6 %collective-permute-start = (bf16[832,128]{1,0:T(8,128)(2,1)S(1)}, bf16[832,128]{1,0:T(8,128)(2,1)S(1)}, u32[]{:S(2)}, u32[]{:S(2)}) collective-permute-start(bf16[832,128]{1,0:T(8,128)(2,1)S(1)} %get-tuple-element.77), channel_id=1, source_target_pairs={{0,64},{64,0},{128,192},{192,128},{1,65},{65,1},{129,193},{193,129... | collective-permute-start | bytes 638984 | tf_op jit(solution)/shard_map/ppermute | solution.py:601
  54.5 1.1 collective-permute-done.got_ref
  55.6 5.5 %all-to-all-done.2.recv_ref = bf16[64,16,128]{2,1,0:T(8,128)(2,1)S(1)} async-done(((bf16[64,16,128]{2,1,0:T(8,128)(2,1)}), bf16[64,16,128]{2,1,0:T(8,128)(2,1)S(1)}, u32[]{:S(2)}, u32[]{:S(2)}) %all-to-all-start.2) | async-done | bytes 262176 | tf_op jit(solution)/shard_map/all_to_all | solution.py:543
  61.1 2.1 %shard_map.234 = (bf16[64,32,128]{2,1,0:T(8,128)(2,1)S(1)}, bf16[256,128]{1,0:T(8,128)(2,1)S(1)}, bf16[256,512]{1,0:T(8,128)(2,1)S(1)}) custom-call(bf16[64,16,128]{2,1,0:T(8,128)(2,1)S(1)} %all-to-all-done.2.recv_ref, f32[832,128]{1,0:T(8,128)S(1)} %get-tuple-element.76.keep_ref, bf16[832,128]{1,0:T(8,128)(2,1)S(1)} %collective-permute-done.got_ref, ...), custom_call_target="tpu_custom_call" | custom-call | tf_op jit(solution)/shard_map/pallas_call | solution.py:532
  63.3 17.9 %all_to_all.26.recv_ref = bf16[64,32,128]{2,1,0:T(8,128)(2,1)S(1)} all-to-all(bf16[64,32,128]{2,1,0:T(8,128)(2,1)S(1)} %get-tuple-element.83), channel_id=1, replica_groups=mesh['dp'=4,'dap'=64] {'dap'}, dimensions={0} | all-to-all | bytes 1048576 | tf_op jit(solution)/shard_map/all_to_all | solution.py:543
  81.2 0.4 shard_map.235
  81.6 8.9 %collective-permute-start.3 = (f32[32,128]{1,0:T(8,128)S(1)}, f32[32,128]{1,0:T(8,128)S(1)}, u32[]{:S(2)}, u32[]{:S(2)}) collective-permute-start(f32[32,128]{1,0:T(8,128)S(1)} %get-tuple-element.88.a_ref), channel_id=1, source_target_pairs={{0,192},{64,128},{128,64},{192,0},{1,193},{65,129},{129,65},{193,1... | collective-permute-start | bytes 49160 | tf_op jit(solution)/shard_map/ppermute | solution.py:615
  90.5 0.3 collective-permute-start.2
  90.8 0.1 collective-permute-start.1
  91.0 1.0 shard_map.236
  91.9 0.4 collective-permute-done.3.d_ref
  92.3 2.2 %collective-permute-done.2.c_ref = f32[32,128]{1,0:T(8,128)S(1)} collective-permute-done((f32[32,128]{1,0:T(8,128)S(1)}, f32[32,128]{1,0:T(8,128)S(1)}, u32[]{:S(2)}, u32[]{:S(2)}) %collective-permute-start.2) | collective-permute-done | bytes 16416 | tf_op jit(solution)/shard_map/ppermute | solution.py:615
  94.6 0.0 collective-permute-done.1.b_ref
  94.6 19.8 %all_to_all.27.recv_ref = bf16[64,24,128]{2,1,0:T(8,128)(2,1)S(1)} all-to-all(bf16[64,24,128]{2,1,0:T(8,128)(2,1)S(1)} %shard_map.237), channel_id=1, replica_groups=mesh['dp'=4,'dap'=64] {'dap'}, dimensions={0} | all-to-all | bytes 786432 | tf_op jit(solution)/shard_map/all_to_all | solution.py:543
  114.4 0.0 collective-permute-start.4
  114.4 1.7 %collective-permute-done.4.other_ref = bf16[64,24,128]{2,1,0:T(8,128)(2,1)S(1)} collective-permute-done((bf16[64,24,128]{2,1,0:T(8,128)(2,1)S(1)}, bf16[64,24,128]{2,1,0:T(8,128)(2,1)S(1)}, u32[]{:S(2)}, u32[]{:S(2)}) %collective-permute-start.4) | collective-permute-done | bytes 393248 | tf_op jit(solution)/shard_map/ppermute | solution.py:620
  116.1 1.3 %shard_map.238 = (f32[1,128]{1,0:T(1,128)}, f32[128,512]{1,0:T(8,128)}, f32[4,128]{1,0:T(4,128)}, f32[128,128]{1,0:T(8,128)}, f32[1,128]{1,0:T(1,128)}, /*index=...) custom-call(bf16[64,24,128]{2,1,0:T(8,128)(2,1)S(1)} %all_to_all.27., ...), custom_call_target="tpu_custom_call" | custom-call | tf_op jit(solution)/shard_map/pallas_call | solution.py:532
  (1 shorter events, 0.0 us)
Async XLA Ops:
  0.6 15.7 %copy-start.1 = (f32[128,512]{1,0:T(8,128)S(1)}, f32[128,512]{1,0:T(8,128)}, u32[]{:S(2)}) copy-start(f32[128,512]{1,0:T(8,128)} %w_ref.5) | copy-start | bytes 786436
  2.6 13.7 %copy-start = (bf16[1,2,128,128]{3,2,1,0:T(8,128)(2,1)S(1)}, bf16[1,2,128,128]{3,2,1,0:T(8,128)(2,1)}, u32[]{:S(2)}) copy-start(bf16[1,2,128,128]{3,2,1,0:T(8,128)(2,1)} %param.14) | copy-start | bytes 196612
  2.6 23.5 %all-to-all-start = ((bf16[64,8,128]{2,1,0:T(8,128)(2,1)}), bf16[64,8,128]{2,1,0:T(8,128)(2,1)S(1)}, u32[]{:S(2)}, u32[]{:S(2)}) async-start(bf16[64,8,128]{2,1,0:T(8,128)(2,1)} %get-tuple-element.58), calls=%async_computation | async-start | bytes 262144 | tf_op jit(solution)/shard_map/all_to_all | solution.py:543
  26.2 15.7 %copy-start.4 = (f32[512,128]{1,0:T(8,128)S(1)}, f32[512,128]{1,0:T(8,128)}, u32[]{:S(2)}) copy-start(f32[512,128]{1,0:T(8,128)} %wd_ref.1) | copy-start | bytes 786436
  26.2 15.7 %copy-start.5 = (f32[128,128]{1,0:T(8,128)S(1)}, f32[128,128]{1,0:T(8,128)}, u32[]{:S(2)}) copy-start(f32[128,128]{1,0:T(8,128)} %wo_ref.1) | copy-start | bytes 196612
  27.2 14.7 %copy-start.2 = (f32[128,512]{1,0:T(8,128)S(1)}, f32[128,512]{1,0:T(8,128)}, u32[]{:S(2)}) copy-start(f32[128,512]{1,0:T(8,128)} %w_ref.4) | copy-start | bytes 786436
  27.2 14.7 %copy-start.3 = (f32[128,512]{1,0:T(8,128)S(1)}, f32[128,512]{1,0:T(8,128)}, u32[]{:S(2)}) copy-start(f32[128,512]{1,0:T(8,128)} %wu_ref.1) | copy-start | bytes 786436
  45.6 15.5 %all-to-all-start.2 = ((bf16[64,16,128]{2,1,0:T(8,128)(2,1)}), bf16[64,16,128]{2,1,0:T(8,128)(2,1)S(1)}, u32[]{:S(2)}, u32[]{:S(2)}) async-start(bf16[64,16,128]{2,1,0:T(8,128)(2,1)} %get-tuple-element.67), calls=%async_computation.2 | async-start | bytes 524288 | tf_op jit(solution)/shard_map/all_to_all | solution.py:543
  51.0 4.7 %collective-permute-start = (bf16[832,128]{1,0:T(8,128)(2,1)S(1)}, bf16[832,128]{1,0:T(8,128)(2,1)S(1)}, u32[]{:S(2)}, u32[]{:S(2)}) collective-permute-start(bf16[832,128]{1,0:T(8,128)(2,1)S(1)} %get-tuple-element.77), channel_id=1, source_target_pairs={{0,64},{64,0},{128,192},{192,128},{1,65},{65,1},{129,193},{193,129... | collective-permute-start | bytes 638984 | tf_op jit(solution)/shard_map/ppermute | solution.py:601
  81.6 10.7 %collective-permute-start.3 = (f32[32,128]{1,0:T(8,128)S(1)}, f32[32,128]{1,0:T(8,128)S(1)}, u32[]{:S(2)}, u32[]{:S(2)}) collective-permute-start(f32[32,128]{1,0:T(8,128)S(1)} %get-tuple-element.88.a_ref), channel_id=1, source_target_pairs={{0,192},{64,128},{128,64},{192,0},{1,193},{65,129},{129,65},{193,1... | collective-permute-start | bytes 49160 | tf_op jit(solution)/shard_map/ppermute | solution.py:615
  90.5 4.1 %collective-permute-start.2 = (f32[32,128]{1,0:T(8,128)S(1)}, f32[32,128]{1,0:T(8,128)S(1)}, u32[]{:S(2)}, u32[]{:S(2)}) collective-permute-start(f32[32,128]{1,0:T(8,128)S(1)} %get-tuple-element.88.a_ref), channel_id=1, source_target_pairs={{0,128},{64,192},{128,0},{192,64},{1,129},{65,193},{129,1},{193,65... | collective-permute-start | bytes 49160 | tf_op jit(solution)/shard_map/ppermute | solution.py:615
  90.8 3.7 %collective-permute-start.1 = (f32[32,128]{1,0:T(8,128)S(1)}, f32[32,128]{1,0:T(8,128)S(1)}, u32[]{:S(2)}, u32[]{:S(2)}) collective-permute-start(f32[32,128]{1,0:T(8,128)S(1)} %get-tuple-element.88.a_ref), channel_id=1, source_target_pairs={{0,64},{64,0},{128,192},{192,128},{1,65},{65,1},{129,193},{193,129... | collective-permute-start | bytes 49160 | tf_op jit(solution)/shard_map/ppermute | solution.py:615
  114.4 1.7 %collective-permute-start.4 = (bf16[64,24,128]{2,1,0:T(8,128)(2,1)S(1)}, bf16[64,24,128]{2,1,0:T(8,128)(2,1)S(1)}, u32[]{:S(2)}, u32[]{:S(2)}) collective-permute-start(bf16[64,24,128]{2,1,0:T(8,128)(2,1)S(1)} %all_to_all.27.recv_ref), channel_id=1, source_target_pairs={{0,64},{64,0},{128,192},{192,128},{1,65},{65,1},{129,193},{193,129... | collective-permute-start | bytes 1179656 | tf_op jit(solution)/shard_map/ppermute | solution.py:620

commit v4 on v3

--- a/solution.py
+++ b/solution.py
@@ -58,8 +58,14 @@
     return total
 
 
-def project(n, w_ref):
-    proj = dot(n, w_ref[...].astype(BF16))
+def interleave(chains):
+    done = object()
+    while chains:
+        chains = [chain for chain in chains if next(chain, done) is not done]
+
+
+def project(n, w):
+    proj = dot(n, w)
     scale = (C // HEADS) ** (-0.5)
     q = (proj[:, :C] * scale).astype(BF16)
     k = proj[:, C : 2 * C].astype(BF16)
@@ -133,7 +139,7 @@
     xhat, _ = ln_stats(x_ref[...].astype(F32))
     n = (xhat * args_ref[G_S, :]).astype(BF16)
     n_ref[...] = n
-    q, k, v, gating = project(n, w_ref)
+    q, k, v, gating = project(n, w_ref[...].astype(BF16))
     qkv_ref[:, :C] = q
     qkv_ref[:, C : 2 * C] = k
     qkv_ref[:, 2 * C :] = v
@@ -162,30 +168,34 @@
     x = x_ref[...].astype(F32)
     v = qkv_ref[:, 2 * C :]
     gating = gating_ref[...]
-    mixes = []
-    for r in range(2):
+    wo = wo_ref[...].astype(BF16)
+    parts = parts_ref[WT_E, :]
+
+    def chain(r):
         part = slice(r * N, (r + 1) * N)
         probs = []
         for h in range(HEADS):
             w = jnp.exp(score_ref[part, h * N : (h + 1) * N] + plane[h * N : (h + 1) * N, :]) * kept
-            probs.append(w / jnp.sum(w, -1, keepdims=True))
+            probs.append(w * (1.0 / jnp.sum(w, -1, keepdims=True)))
         prob = jnp.concatenate(probs, 1)
         prob_ref[part, :] = prob
-        mixes.append(dot(prob.astype(BF16), stack_heads(v[part], masks)))
-    mix = jnp.concatenate(mixes, 0)
-    mix_ref[...] = mix
-    update = dot((gating * mix).astype(BF16), wo_ref[...].astype(BF16))
-    first = (x + update).astype(BF16)
-    first_ref[...] = first
-    first = first.astype(F32)
-    xhat_e, _ = ln_stats(first)
-    plane_e = plane_of((xhat_e * args_ref[G_E, :]).astype(BF16), parts_ref[WT_E, :])
-    small[0:HEADS, :] = plane_e[:, :N]
-    small[HEADS : 2 * HEADS, :] = plane_e[:, N:]
-    fscr[0 : 2 * N, :] = first
-    for r in range(2):
+        yield
+        mix = dot(prob.astype(BF16), stack_heads(v[part], masks))
+        mix_ref[part, :] = mix
+        yield
+        first = (x[part] + dot((gating[part] * mix).astype(BF16), wo)).astype(BF16)
+        first_ref[part, :] = first
+        yield
+        first = first.astype(F32)
+        fscr[part, :] = first
+        xhat, _ = ln_stats(first)
+        yield
+        small[r * HEADS : (r + 1) * HEADS, :] = plane_of((xhat * args_ref[G_E, :]).astype(BF16), parts)
+        yield
         for a in range(2):
             sscr[pl.ds(r * 2 + a, n_dst, stride=rows), :] = rows_of(fscr, r * N + a, n_dst, 2)
+
+    interleave([chain(r) for r in range(2)])
     fscr[0 : 2 * N, :] = cot_ref[...].astype(F32)
     for r in range(2):
         for a in range(2):
@@ -197,9 +207,9 @@
 
 def put_wide(scr, src, value, starts, n_dst, rows):
     for t in range(4):
-        src[...] = value[:, t * C : (t + 1) * C]
+        src[t * C : (t + 1) * C, :] = value[:, t * C : (t + 1) * C]
         for i in range(2):
-            scr[pl.ds(starts[i] + t, n_dst, stride=rows), :] = rows_of(src, i, n_dst, 2)
+            scr[pl.ds(starts[i] + t, n_dst, stride=rows), :] = rows_of(src, t * C + i, n_dst, 2)
 
 
 def put_narrow(scr, src, row, n_dst, rows, each):
@@ -233,103 +243,112 @@
     gain, gain_t = args_ref[G_E, :], args_ref[G_T, :]
     length = jnp.sum(args_ref[KEPT, :], -1, keepdims=True)
     kept = (lax.broadcasted_iota(jnp.int32, (N, 1), 0).astype(F32) < length).astype(F32)
-    x = zscr[...]
-    cot = cscr[...]
-    xhat, rstd = ln_stats(x)
-    n = (xhat * gain).astype(BF16)
-    q, k, v, gating = project(n, w_ref)
-    saved = []
-    mixes = []
-    for a in range(2):
+    w = w_ref[...].astype(BF16)
+    wo = wo_ref[...].astype(BF16)
+    wu = wu_ref[...].astype(BF16)
+    wd = wd_ref[...].astype(BF16)
+    results = {}
+
+    def chain(a):
         part = slice(a * N, (a + 1) * N)
-        ks = stack_heads(k[part], masks)
-        vs = stack_heads(v[part], masks)
-        s = dot(ks, q[part], NT) + plane[...]
+        x = zscr[part, :]
+        cot = cscr[part, :]
+        cot_b = cot.astype(BF16)
+        cot_ref[part, :] = cot_b
+        xhat, rstd = ln_stats(x)
+        n = (xhat * gain).astype(BF16)
+        n_ref[part, :] = n
+        yield
+        q, k, v, gating = project(n, w)
+        yield
+        ks = stack_heads(k, masks)
+        vs = stack_heads(v, masks)
+        s = dot(ks, q, NT) + plane[...]
+        yield
         probs = []
         for h in range(HEADS):
-            w = jnp.exp(s[h * N : (h + 1) * N]) * kept
-            probs.append(w / jnp.sum(w, 0, keepdims=True))
+            e = jnp.exp(s[h * N : (h + 1) * N]) * kept
+            probs.append(e * (1.0 / jnp.sum(e, 0, keepdims=True)))
         prob = jnp.concatenate(probs, 0)
         prob_b = prob.astype(BF16)
-        mixes.append(dot(prob_b, vs, TN))
-        saved.append((ks, vs, prob, prob_b))
-    mix = jnp.concatenate(mixes, 0)
-    gated = (gating * mix).astype(BF16)
-    wo = wo_ref[...].astype(BF16)
-    second = (x + dot(gated, wo)).astype(BF16).astype(F32)
-    xhat2, rstd2 = ln_stats(second)
-    n2 = (xhat2 * gain_t).astype(BF16)
-    wu = wu_ref[...].astype(BF16)
-    wd = wd_ref[...].astype(BF16)
-    cot_b = cot.astype(BF16)
-    up = dot(n2, wu)
-    cdf = 0.5 * (1.0 + lax.erf(up * (0.5**0.5)))
-    hidden = (up * cdf).astype(BF16)
-    dhidden = dot(cot_b, wd, NT).astype(BF16).astype(F32)
-    slope = cdf + up * (jnp.exp(-0.5 * up * up) * 0.3989422804014327)
-    dup = (dhidden * slope).astype(BF16)
-    hidden_ref[...] = hidden
-    dup_ref[...] = dup
-    n_ref[...] = n
-    n2_ref[...] = n2
-    cot_ref[...] = cot_b
-    gated_ref[...] = gated
-    dn2 = dot(dup, wu, NT).astype(BF16).astype(F32)
-    dx2, dgain_t = ln_back(dn2, xhat2, rstd2, gain_t)
-    dsecond = (cot + dx2).astype(BF16)
-    dsecond_ref[...] = dsecond
-    dgated = dot(dsecond, wo, NT).astype(BF16).astype(F32)
-    dgating = dgated * mix
-    dmix = (dgated * gating).astype(BF16)
-    dq, dk, dv = [], [], []
-    for a in range(2):
-        part = slice(a * N, (a + 1) * N)
-        ks, vs, prob, prob_b = saved[a]
-        dprob = dot(vs, dmix[part], NT).astype(BF16).astype(F32)
-        dv.append(unstack_heads(dot(prob_b, dmix[part]), masks_f))
+        yield
+        mix = dot(prob_b, vs, TN)
+        yield
+        gated = (gating * mix).astype(BF16)
+        gated_ref[part, :] = gated
+        second = (x + dot(gated, wo)).astype(BF16).astype(F32)
+        yield
+        xhat2, rstd2 = ln_stats(second)
+        n2 = (xhat2 * gain_t).astype(BF16)
+        n2_ref[part, :] = n2
+        dhidden = dot(cot_b, wd, NT).astype(BF16).astype(F32)
+        yield
+        up = dot(n2, wu)
+        yield
+        cdf = 0.5 * (1.0 + lax.erf(up * (0.5**0.5)))
+        slope = cdf + up * (jnp.exp(-0.5 * up * up) * 0.3989422804014327)
+        dup = (dhidden * slope).astype(BF16)
+        hidden_ref[part, :] = (up * cdf).astype(BF16)
+        dup_ref[part, :] = dup
+        yield
+        dn2 = dot(dup, wu, NT).astype(BF16).astype(F32)
+        yield
+        dx2, dgain_t = ln_back(dn2, xhat2, rstd2, gain_t)
+        dsecond = (cot + dx2).astype(BF16)
+        dsecond_ref[part, :] = dsecond
+        yield
+        dgated = dot(dsecond, wo, NT).astype(BF16).astype(F32)
+        yield
+        dmix = (dgated * gating).astype(BF16)
+        dprob = dot(vs, dmix, NT).astype(BF16).astype(F32)
+        yield
         ds = []
         for h in range(HEADS):
             p = prob[h * N : (h + 1) * N]
             d = dprob[h * N : (h + 1) * N]
             ds.append(p * (d - jnp.sum(p * d, 0, keepdims=True)))
         ds = jnp.concatenate(ds, 0)
-        if a == 0:
-            plane[...] = ds
-        else:
-            plane[...] += ds
-        ds = ds.astype(BF16)
-        dq.append(dot(ds, ks, TN))
-        dk.append(unstack_heads(dot(ds, q[part]), masks_f))
+        dv = unstack_heads(dot(prob_b, dmix), masks_f)
+        yield
+        ds_b = ds.astype(BF16)
+        dq = dot(ds_b, ks, TN)
+        dk = unstack_heads(dot(ds_b, q), masks_f)
+        yield
+        dproj = project_cotangent(dq, dk, dv, gating, dgated * mix)
+        dproj_ref[part, :] = dproj
+        dn = dot(dproj, w, NT).astype(BF16).astype(F32)
+        yield
+        dx, dgain = ln_back(dn, xhat, rstd, gain)
+        zscr[part, :] = dsecond.astype(F32) + dx
+        results[a] = ds, dgain_t, dgain
+
+    interleave([chain(a) for a in range(2)])
+    (ds, dgain_t, dgain), (ds_b, dgain_t_b, dgain_b) = results[0], results[1]
+    plane[...] = ds + ds_b
     for r in range(2):
         for h in range(HEADS):
             sscr[pl.ds(r * 4 + h, n_dst, stride=rows), :] = rows_of(plane, h * N + r, n_dst, 2)
-    dproj = project_cotangent(dq, dk, dv, gating, dgating)
-    dproj_ref[...] = dproj
-    dn = dot(dproj, w_ref[...].astype(BF16), NT).astype(BF16).astype(F32)
-    dx, dgain = ln_back(dn, xhat, rstd, gain)
-    zscr[...] = dsecond.astype(F32) + dx
-    for r in range(2):
         for a in range(2):
             sscr[pl.ds(8 + r * 2 + a, n_dst, stride=rows), :] = rows_of(zscr, a * N + r, n_dst, 2)
     for i in range(12, rows):
         sscr[pl.ds(i, n_dst, stride=rows), :] = jnp.zeros((n_dst, C), F32)
     send_ref[...] = sscr[...].reshape(n_dst, rows, C).astype(BF16)
-    small_ref[0:1, :] = dgain_t
-    small_ref[1:2, :] = dgain
+    small_ref[0:1, :] = dgain_t + dgain_t_b
+    small_ref[1:2, :] = dgain + dgain_b
     small_ref[2:8, :] = jnp.zeros((6, C), F32)
 
 
 def end_weights_kernel(
     hidden_ref, dup_ref, n_ref, n2_ref, cot_ref, dproj_ref, gated_ref, dsecond_ref,
     keep_ref, give_ref,
-    down, narrow, wscr,
+    down, up, proj, narrow, wscr,
 ):
     half = keep_ref.shape[0]
     n_dst = half // HALF
     down[...] = dot(hidden_ref[...], cot_ref[...], TN)
     put_narrow(wscr, down, half + 4, n_dst, HALF, 8)
-    put_wide(wscr, narrow, dot(n2_ref[...], dup_ref[...], TN), (8, half), n_dst, HALF)
-    put_wide(wscr, narrow, dot(n_ref[...], dproj_ref[...], TN), (0, 4), n_dst, HALF)
+    put_wide(wscr, up, dot(n2_ref[...], dup_ref[...], TN), (8, half), n_dst, HALF)
+    put_wide(wscr, proj, dot(n_ref[...], dproj_ref[...], TN), (0, 4), n_dst, HALF)
     narrow[...] = dot(gated_ref[...], dsecond_ref[...], TN)
     for i in range(2):
         wscr[pl.ds(i * half + 12, n_dst, stride=HALF), :] = rows_of(narrow, i, n_dst, 2)
@@ -339,32 +358,23 @@
 
 
 def project_cotangent(dq, dk, dv, gating, dgating):
-    scale = (C // HEADS) ** (-0.5)
-    dq = jnp.concatenate(dq, 0).astype(BF16).astype(F32) * scale
-    dk = jnp.concatenate(dk, 0)
-    dv = jnp.concatenate(dv, 0)
+    dq = dq.astype(BF16).astype(F32) * (C // HEADS) ** (-0.5)
     dg = dgating * gating * (1.0 - gating)
     return jnp.concatenate([dq.astype(BF16), dk.astype(BF16), dv.astype(BF16), dg.astype(BF16)], 1)
 
 
-def plane_back(planes, n, p_ref, parts):
-    N = planes.shape[1]
+def plane_back(plane, n, p_ref, parts):
     p_ref[...] = jnp.zeros_like(p_ref)
-    dns = []
-    dbias = 0.0
-    for r in range(2):
-        for i in range(3):
-            p_ref[i * HEADS : (i + 1) * HEADS, :] = planes[r * HEADS : (r + 1) * HEADS]
-        p = p_ref[...].astype(BF16)
-        dns.append(dot(p, parts, TN))
-        dbias = dbias + dot(p, n[r * N : (r + 1) * N])
-    return jnp.concatenate(dns, 0).astype(BF16).astype(F32), dbias[0:HEADS]
+    for i in range(3):
+        p_ref[i * HEADS : (i + 1) * HEADS, :] = plane
+    p = p_ref[...].astype(BF16)
+    return dot(p, parts, TN).astype(BF16).astype(F32), dot(p, n)[0:HEADS]
 
 
 def start_backward_kernel(
     recv_ref, keep_ref, got_ref, small_ref, n_ref, first_ref, qkv_ref, gating_ref, mix_ref, prob_ref, args_ref, parts_ref, wo_ref,
     send_ref, dfirst_ref, dproj_ref,
-    fscr, gscr, plane, narrow, sscr, wscr, p_ref,
+    fscr, gscr, plane, narrow, wide, sscr, wscr, p_ref,
 ):
     n_dst, in_rows, _ = recv_ref.shape
     N = 2 * n_dst
@@ -375,54 +385,61 @@
     for r in range(2):
         for a in range(2):
             gscr[pl.ds(r * N + a, n_dst, stride=2), :] = rows_of(fscr, 8 + r * 2 + a, n_dst, in_rows)
-    first = first_ref[...].astype(F32)
-    xhat_e, rstd_e = ln_stats(first)
-    n_e = (xhat_e * args_ref[G_E, :]).astype(BF16)
-    dn_e, dbias_e = plane_back(total[0:8], n_e, p_ref, parts_ref[WT_E, :])
-    dxe, dgain_e = ln_back(dn_e, xhat_e, rstd_e, args_ref[G_E, :])
-    dfirst = (gscr[...] + dxe).astype(BF16)
-    dfirst_ref[...] = dfirst
     masks = head_masks(BF16)
     masks_f = head_masks(F32)
-    n = n_ref[...]
-    q = qkv_ref[:, :C]
-    k = qkv_ref[:, C : 2 * C]
-    v = qkv_ref[:, 2 * C :]
-    gating = gating_ref[...]
-    mix = mix_ref[...]
-    gated = (gating * mix).astype(BF16)
+    gain_e = args_ref[G_E, :]
+    parts = parts_ref[WT_E, :]
     wo = wo_ref[...].astype(BF16)
-    narrow[...] = dot(gated, dfirst, TN)
-    put_narrow(sscr, narrow, 16, n_dst, rows, 2)
-    dgated = dot(dfirst, wo, NT).astype(BF16).astype(F32)
-    dgating = dgated * mix
-    dmix = (dgated * gating).astype(BF16)
-    dq, dk, dv = [], [], []
-    for r in range(2):
+    results = {}
+
+    def chain(r):
         part = slice(r * N, (r + 1) * N)
-        ks = stack_heads(k[part], masks)
-        vs = stack_heads(v[part], masks)
+        xhat, rstd = ln_stats(first_ref[part, :].astype(F32))
+        n_e = (xhat * gain_e).astype(BF16)
+        yield
+        dn_e, dbias_e = plane_back(total[r * HEADS : (r + 1) * HEADS], n_e, p_ref.at[r], parts)
+        yield
+        dxe, dgain_e = ln_back(dn_e, xhat, rstd, gain_e)
+        dfirst = (gscr[part, :] + dxe).astype(BF16)
+        dfirst_ref[part, :] = dfirst
+        yield
+        q = qkv_ref[part, :C]
+        ks = stack_heads(qkv_ref[part, C : 2 * C], masks)
+        vs = stack_heads(qkv_ref[part, 2 * C :], masks)
+        gating = gating_ref[part, :]
+        mix = mix_ref[part, :]
         prob = prob_ref[part, :]
-        dprob = dot(dmix[part], vs, NT).astype(BF16).astype(F32)
-        dv.append(unstack_heads(dot(prob.astype(BF16), dmix[part], TN), masks_f))
+        dgated = dot(dfirst, wo, NT).astype(BF16).astype(F32)
+        yield
+        dmix = (dgated * gating).astype(BF16)
+        dprob = dot(dmix, vs, NT).astype(BF16).astype(F32)
+        yield
         ds = []
         for h in range(HEADS):
             p = prob[:, h * N : (h + 1) * N]
             d = dprob[:, h * N : (h + 1) * N]
             ds.append(p * (d - jnp.sum(p * d, -1, keepdims=True)))
-            if r == 0:
-                plane[h * N : (h + 1) * N, :] = ds[h]
-            else:
-                plane[h * N : (h + 1) * N, :] += ds[h]
-        ds = jnp.concatenate(ds, 1).astype(BF16)
-        dq.append(dot(ds, ks))
-        dk.append(unstack_heads(dot(ds, q[part], TN), masks_f))
+        dv = unstack_heads(dot(prob.astype(BF16), dmix, TN), masks_f)
+        yield
+        ds_b = jnp.concatenate(ds, 1).astype(BF16)
+        dq = dot(ds_b, ks)
+        dk = unstack_heads(dot(ds_b, q, TN), masks_f)
+        yield
+        dproj_ref[part, :] = project_cotangent(dq, dk, dv, gating, dgated * mix)
+        results[r] = ds, dgain_e, dbias_e
+
+    interleave([chain(r) for r in range(2)])
+    (ds, dgain_e, dbias_e), (ds_b, dgain_b, dbias_b) = results[0], results[1]
+    dgain_e, dbias_e = dgain_e + dgain_b, dbias_e + dbias_b
+    for h in range(HEADS):
+        plane[h * N : (h + 1) * N, :] = ds[h] + ds_b[h]
     for r in range(2):
         for h in range(HEADS):
             sscr[pl.ds(r * 4 + h, n_dst, stride=rows), :] = rows_of(plane, h * N + r, n_dst, 2)
-    dproj = project_cotangent(dq, dk, dv, gating, dgating)
-    put_wide(sscr, narrow, dot(n, dproj, TN), (8, 12), n_dst, rows)
-    dproj_ref[...] = dproj
+    gated = (gating_ref[...] * mix_ref[...]).astype(BF16)
+    narrow[0:C, :] = dot(gated, dfirst_ref[...], TN)
+    put_narrow(sscr, narrow, 16, n_dst, rows, 2)
+    put_wide(sscr, wide, dot(n_ref[...], dproj_ref[...], TN), (8, 12), n_dst, rows)
     smalls = [small_ref[0:1, :], small_ref[1:2, :], dgain_e] + [dbias_e[h : h + 1] for h in range(HEADS)]
     put_small(sscr, 18, smalls, n_dst, rows)
     wscr[...] = keep_ref[...] + got_ref[...].astype(F32)
@@ -437,7 +454,13 @@
     n = (xhat * args_ref[G_S, :]).astype(BF16)
     dn = dot(dproj_ref[...], w_ref[...].astype(BF16), NT).astype(BF16)
     dn_ref[...] = dn
-    dn_plane, dbias = plane_back(total[0:8], n, p_ref, parts_ref[WT_S, :])
+    N = n.shape[0] // 2
+    backs = [
+        plane_back(total[r * HEADS : (r + 1) * HEADS], n[r * N : (r + 1) * N], p_ref.at[r], parts_ref[WT_S, :])
+        for r in range(2)
+    ]
+    dn_plane = jnp.concatenate([back[0] for back in backs], 0)
+    dbias = backs[0][1] + backs[1][1]
     dn_plane_ref[...] = dn_plane.astype(BF16)
     part_ref[0:11, :] = total[8:19]
     part_ref[11:15, :] = dbias
@@ -595,21 +618,21 @@
     keep, give = call(
         end_weights_kernel,
         [shape(half), shape(half, BF16)],
-        [(4 * C, C), (C, C), (n_dst * 2 * HALF, C)],
+        [(4 * C, C), (4 * C, C), (4 * C, C), (C, C), (n_dst * 2 * HALF, C)],
         *saved,
     )
     got = lax.ppermute(give, "dp", to_core)
     send, dfirst, dproj = call(
         start_backward_kernel,
         [shape((n_dst, 32, C), BF16), shape(tokens, BF16), shape(hidden, BF16)],
-        [(n_dst * 16, C), tokens, (HEADS * N, N), (C, C), (n_dst * 32, C), half, (16, C)],
+        [(n_dst * 16, C), tokens, (HEADS * N, N), (C, C), (4 * C, C), (n_dst * 32, C), half, (2, 16, C)],
         recv, keep, got, small, n, first, qkv, gating, mix, prob, args, parts, wo,
     )
     recv = swap(send)
     dn, dn_plane, part = call(
         start_plane_kernel,
         [shape(tokens, BF16), shape(tokens, BF16), shape((32, C))],
-        [(16, C)],
+        [(2, 16, C)],
         recv, dproj, x, proj_start, args, parts,
     )
     others = [lax.ppermute(part, "dp", [(i, i ^ d) for i in range(n_dp)]) for d in range(1, n_dp)]

time: 118 us -> 117 us (level)
  no operation moved by 1% of the time
where the time goes in v4:
time: 117 us
  blocking collectives  52.4 us (45%)
  starting transfers between devices  31.4 us (27%)
  waiting for transfers between devices  19.5 us (17%)
  Pallas kernels  12.7 us (11%)
    all_to_all x3, blocking collectives, swap(): lax.all_to_all(buffer, 'dap', split_axis=0, concat_axis=0, tiled=True)  52.4 us
    all_to_all x2, starting transfers between devices, swap(): lax.all_to_all(buffer, 'dap', split_axis=0, concat_axis=0, tiled=True)  18.5 us
    all_to_all x2, waiting for transfers between devices, swap(): lax.all_to_all(buffer, 'dap', split_axis=0, concat_axis=0, tiled=True)  14.1 us
    pallas_call x10, Pallas kernels, call(): pl.pallas_call(body, out_shape=out_shape, in_specs=[pl.BlockSpec(memory_s...  12.7 us
    ppermute x3, starting transfers between devices, local(): lax.ppermute(part, 'dp', [(i, i ^ d) for i in range(n_dp)])  9.38 us
    ppermute x1, starting transfers between devices, local(): got = lax.ppermute(give, 'dp', to_core)  3.56 us
    ppermute x3, waiting for transfers between devices, local(): lax.ppermute(part, 'dp', [(i, i ^ d) for i in range(n_dp)])  2.65 us
  transfers between devices with their start and end apart: 7, of which 6 were waited for; matrix products, arithmetic and copies ran while one was open for 0% of the time, Pallas kernels for 2%

profile of v4, /device:TPU:1, one launch (start us, length us, event | category | flops | bytes accessed | tf_op | source)
XLA Modules:
  0.0 116.9 jit_solution(1220858263254151891)
XLA Ops:
  0.6 0.0 copy-start.1
  0.7 2.0 %shard_map.229 = (bf16[64,8,128]{2,1,0:T(8,128)(2,1)}, f32[8,128]{1,0:T(8,128)S(1)}, bf16[32,128]{1,0:T(8,128)(2,1)S(1)}) custom-call(bf16[256,128]{1,0:T(8,128)(2,1)} %bitcast.13, f32[1,128]{1,0:T(1,128)} %bitcast.22, f32[4,128]{1,0:T(4,128)} %bitcast.20, f32[1,128]{1,0:T(1,128)} %bitcast.23, f32[4,128]{1,0:T(4,128)} %bitcast.21, f32[1,128]{1,0:T(1,128)} %bitcast.24, ...), custom_call_target="tpu_custom_call" | custom-call | tf_op jit(solution)/shard_map/pallas_call | solution.py:555
  2.6 0.0 copy-start
  2.6 13.6 %all-to-all-start = ((bf16[64,8,128]{2,1,0:T(8,128)(2,1)}), bf16[64,8,128]{2,1,0:T(8,128)(2,1)S(1)}, u32[]{:S(2)}, u32[]{:S(2)}) async-start(bf16[64,8,128]{2,1,0:T(8,128)(2,1)} %get-tuple-element.58), calls=%async_computation | async-start | bytes 262144 | tf_op jit(solution)/shard_map/all_to_all | solution.py:566
  16.3 0.0 copy-done.1
  16.3 0.0 copy-done
  16.3 1.3 %shard_map.230 = (bf16[256,384]{1,0:T(8,128)(2,1)S(1)}, f32[256,128]{1,0:T(8,128)S(1)}, f32[256,512]{1,0:T(8,128)S(1)}, bf16[256,128]{1,0:T(8,128)(2,1)S(1)}, bf...) custom-call(bf16[256,128]{1,0:T(8,128)(2,1)S(1)} %bitcast.14, bf16[256,128]{1,0:T(8,128)(2,1)} %bitcast.18, ...), custom_call_target="tpu_custom_call" | custom-call | tf_op jit(solution)/shard_map/pallas_call | solution.py:555
  17.6 8.6 %all-to-all-done.recv_ref = bf16[64,8,128]{2,1,0:T(8,128)(2,1)S(1)} async-done(((bf16[64,8,128]{2,1,0:T(8,128)(2,1)}), bf16[64,8,128]{2,1,0:T(8,128)(2,1)S(1)}, u32[]{:S(2)}, u32[]{:S(2)}) %all-to-all-start) | async-done | bytes 131104 | tf_op jit(solution)/shard_map/all_to_all | solution.py:566
  26.2 0.0 copy-start.4
  26.2 0.0 copy-start.5
  26.2 1.0 shard_map.231
  27.2 0.0 copy-start.2
  27.2 0.0 copy-start.3
  27.2 14.7 %all_to_all.25.recv_ref = bf16[64,16,128]{2,1,0:T(8,128)(2,1)S(1)} all-to-all(bf16[64,16,128]{2,1,0:T(8,128)(2,1)S(1)} %get-tuple-element.66), channel_id=1, replica_groups=mesh['dp'=4,'dap'=64] {'dap'}, dimensions={0} | all-to-all | bytes 524288 | tf_op jit(solution)/shard_map/all_to_all | solution.py:566
  41.9 0.0 copy-done.4
  41.9 0.0 copy-done.5
  41.9 0.0 copy-done.2
  41.9 0.0 copy-done.3
  42.0 3.4 %shard_map.232 = (bf16[64,16,128]{2,1,0:T(8,128)(2,1)}, f32[8,128]{1,0:T(8,128)S(1)}, bf16[256,512]{1,0:T(8,128)(2,1)S(1)}, bf16[256,512]{1,0:T(8,128)(2,1)S(1)}...) custom-call(bf16[64,16,128]{2,1,0:T(8,128)(2,1)S(1)} %all_to_all.25., ...), custom_call_target="tpu_custom_call" | custom-call | tf_op jit(solution)/shard_map/pallas_call | solution.py:555
  45.3 4.9 %all-to-all-start.2 = ((bf16[64,16,128]{2,1,0:T(8,128)(2,1)}), bf16[64,16,128]{2,1,0:T(8,128)(2,1)S(1)}, u32[]{:S(2)}, u32[]{:S(2)}) async-start(bf16[64,16,128]{2,1,0:T(8,128)(2,1)} %get-tuple-element.67), calls=%async_computation.2 | async-start | bytes 524288 | tf_op jit(solution)/shard_map/all_to_all | solution.py:566
  50.2 0.5 shard_map.233
  50.7 3.6 %collective-permute-start = (bf16[832,128]{1,0:T(8,128)(2,1)S(1)}, bf16[832,128]{1,0:T(8,128)(2,1)S(1)}, u32[]{:S(2)}, u32[]{:S(2)}) collective-permute-start(bf16[832,128]{1,0:T(8,128)(2,1)S(1)} %get-tuple-element.77), channel_id=1, source_target_pairs={{0,64},{64,0},{128,192},{192,128},{1,65},{65,1},{129,193},{193,129... | collective-permute-start | bytes 638984 | tf_op jit(solution)/shard_map/ppermute | solution.py:624
  54.3 1.1 collective-permute-done.got_ref
  55.3 5.5 %all-to-all-done.2.recv_ref = bf16[64,16,128]{2,1,0:T(8,128)(2,1)S(1)} async-done(((bf16[64,16,128]{2,1,0:T(8,128)(2,1)}), bf16[64,16,128]{2,1,0:T(8,128)(2,1)S(1)}, u32[]{:S(2)}, u32[]{:S(2)}) %all-to-all-start.2) | async-done | bytes 262176 | tf_op jit(solution)/shard_map/all_to_all | solution.py:566
  60.8 2.0 %shard_map.234 = (bf16[64,32,128]{2,1,0:T(8,128)(2,1)S(1)}, bf16[256,128]{1,0:T(8,128)(2,1)S(1)}, bf16[256,512]{1,0:T(8,128)(2,1)S(1)}) custom-call(bf16[64,16,128]{2,1,0:T(8,128)(2,1)S(1)} %all-to-all-done.2.recv_ref, f32[832,128]{1,0:T(8,128)S(1)} %get-tuple-element.76.keep_ref, bf16[832,128]{1,0:T(8,128)(2,1)S(1)} %collective-permute-done.got_ref, ...), custom_call_target="tpu_custom_call" | custom-call | tf_op jit(solution)/shard_map/pallas_call | solution.py:555
  62.8 17.9 %all_to_all.26.recv_ref = bf16[64,32,128]{2,1,0:T(8,128)(2,1)S(1)} all-to-all(bf16[64,32,128]{2,1,0:T(8,128)(2,1)S(1)} %get-tuple-element.83), channel_id=1, replica_groups=mesh['dp'=4,'dap'=64] {'dap'}, dimensions={0} | all-to-all | bytes 1048576 | tf_op jit(solution)/shard_map/all_to_all | solution.py:566
  80.7 0.4 shard_map.235
  81.1 8.9 %collective-permute-start.3 = (f32[32,128]{1,0:T(8,128)S(1)}, f32[32,128]{1,0:T(8,128)S(1)}, u32[]{:S(2)}, u32[]{:S(2)}) collective-permute-start(f32[32,128]{1,0:T(8,128)S(1)} %get-tuple-element.88.a_ref), channel_id=1, source_target_pairs={{0,192},{64,128},{128,64},{192,0},{1,193},{65,129},{129,65},{193,1... | collective-permute-start | bytes 49160 | tf_op jit(solution)/shard_map/ppermute | solution.py:638
  90.0 0.3 collective-permute-start.2
  90.3 0.1 collective-permute-start.1
  90.5 1.0 shard_map.236
  91.4 0.4 collective-permute-done.3.d_ref
  91.8 2.3 %collective-permute-done.2.c_ref = f32[32,128]{1,0:T(8,128)S(1)} collective-permute-done((f32[32,128]{1,0:T(8,128)S(1)}, f32[32,128]{1,0:T(8,128)S(1)}, u32[]{:S(2)}, u32[]{:S(2)}) %collective-permute-start.2) | collective-permute-done | bytes 16416 | tf_op jit(solution)/shard_map/ppermute | solution.py:638
  94.1 0.0 collective-permute-done.1.b_ref
  94.1 19.8 %all_to_all.27.recv_ref = bf16[64,24,128]{2,1,0:T(8,128)(2,1)S(1)} all-to-all(bf16[64,24,128]{2,1,0:T(8,128)(2,1)S(1)} %shard_map.237), channel_id=1, replica_groups=mesh['dp'=4,'dap'=64] {'dap'}, dimensions={0} | all-to-all | bytes 786432 | tf_op jit(solution)/shard_map/all_to_all | solution.py:566
  113.9 0.0 collective-permute-start.4
  113.9 1.7 %collective-permute-done.4.other_ref = bf16[64,24,128]{2,1,0:T(8,128)(2,1)S(1)} collective-permute-done((bf16[64,24,128]{2,1,0:T(8,128)(2,1)S(1)}, bf16[64,24,128]{2,1,0:T(8,128)(2,1)S(1)}, u32[]{:S(2)}, u32[]{:S(2)}) %collective-permute-start.4) | collective-permute-done | bytes 393248 | tf_op jit(solution)/shard_map/ppermute | solution.py:643
  115.6 1.3 %shard_map.238 = (f32[1,128]{1,0:T(1,128)}, f32[128,512]{1,0:T(8,128)}, f32[4,128]{1,0:T(4,128)}, f32[128,128]{1,0:T(8,128)}, f32[1,128]{1,0:T(1,128)}, /*index=...) custom-call(bf16[64,24,128]{2,1,0:T(8,128)(2,1)S(1)} %all_to_all.27., ...), custom_call_target="tpu_custom_call" | custom-call | tf_op jit(solution)/shard_map/pallas_call | solution.py:555
  (1 shorter events, 0.0 us)
Async XLA Ops:
  0.6 15.7 %copy-start.1 = (f32[128,512]{1,0:T(8,128)S(1)}, f32[128,512]{1,0:T(8,128)}, u32[]{:S(2)}) copy-start(f32[128,512]{1,0:T(8,128)} %w_ref.5) | copy-start | bytes 786436
  2.6 13.7 %copy-start = (bf16[1,2,128,128]{3,2,1,0:T(8,128)(2,1)S(1)}, bf16[1,2,128,128]{3,2,1,0:T(8,128)(2,1)}, u32[]{:S(2)}) copy-start(bf16[1,2,128,128]{3,2,1,0:T(8,128)(2,1)} %param.14) | copy-start | bytes 196612
  2.6 23.5 %all-to-all-start = ((bf16[64,8,128]{2,1,0:T(8,128)(2,1)}), bf16[64,8,128]{2,1,0:T(8,128)(2,1)S(1)}, u32[]{:S(2)}, u32[]{:S(2)}) async-start(bf16[64,8,128]{2,1,0:T(8,128)(2,1)} %get-tuple-element.58), calls=%async_computation | async-start | bytes 262144 | tf_op jit(solution)/shard_map/all_to_all | solution.py:566
  26.2 15.7 %copy-start.4 = (f32[512,128]{1,0:T(8,128)S(1)}, f32[512,128]{1,0:T(8,128)}, u32[]{:S(2)}) copy-start(f32[512,128]{1,0:T(8,128)} %wd_ref.1) | copy-start | bytes 786436
  26.2 15.7 %copy-start.5 = (f32[128,128]{1,0:T(8,128)S(1)}, f32[128,128]{1,0:T(8,128)}, u32[]{:S(2)}) copy-start(f32[128,128]{1,0:T(8,128)} %wo_ref.1) | copy-start | bytes 196612
  27.2 14.7 %copy-start.2 = (f32[128,512]{1,0:T(8,128)S(1)}, f32[128,512]{1,0:T(8,128)}, u32[]{:S(2)}) copy-start(f32[128,512]{1,0:T(8,128)} %w_ref.4) | copy-start | bytes 786436
  27.2 14.7 %copy-start.3 = (f32[128,512]{1,0:T(8,128)S(1)}, f32[128,512]{1,0:T(8,128)}, u32[]{:S(2)}) copy-start(f32[128,512]{1,0:T(8,128)} %wu_ref.1) | copy-start | bytes 786436
  45.3 15.5 %all-to-all-start.2 = ((bf16[64,16,128]{2,1,0:T(8,128)(2,1)}), bf16[64,16,128]{2,1,0:T(8,128)(2,1)S(1)}, u32[]{:S(2)}, u32[]{:S(2)}) async-start(bf16[64,16,128]{2,1,0:T(8,128)(2,1)} %get-tuple-element.67), calls=%async_computation.2 | async-start | bytes 524288 | tf_op jit(solution)/shard_map/all_to_all | solution.py:566
  50.7 4.7 %collective-permute-start = (bf16[832,128]{1,0:T(8,128)(2,1)S(1)}, bf16[832,128]{1,0:T(8,128)(2,1)S(1)}, u32[]{:S(2)}, u32[]{:S(2)}) collective-permute-start(bf16[832,128]{1,0:T(8,128)(2,1)S(1)} %get-tuple-element.77), channel_id=1, source_target_pairs={{0,64},{64,0},{128,192},{192,128},{1,65},{65,1},{129,193},{193,129... | collective-permute-start | bytes 638984 | tf_op jit(solution)/shard_map/ppermute | solution.py:624
  81.1 10.7 %collective-permute-start.3 = (f32[32,128]{1,0:T(8,128)S(1)}, f32[32,128]{1,0:T(8,128)S(1)}, u32[]{:S(2)}, u32[]{:S(2)}) collective-permute-start(f32[32,128]{1,0:T(8,128)S(1)} %get-tuple-element.88.a_ref), channel_id=1, source_target_pairs={{0,192},{64,128},{128,64},{192,0},{1,193},{65,129},{129,65},{193,1... | collective-permute-start | bytes 49160 | tf_op jit(solution)/shard_map/ppermute | solution.py:638
  90.0 4.1 %collective-permute-start.2 = (f32[32,128]{1,0:T(8,128)S(1)}, f32[32,128]{1,0:T(8,128)S(1)}, u32[]{:S(2)}, u32[]{:S(2)}) collective-permute-start(f32[32,128]{1,0:T(8,128)S(1)} %get-tuple-element.88.a_ref), channel_id=1, source_target_pairs={{0,128},{64,192},{128,0},{192,64},{1,129},{65,193},{129,1},{193,65... | collective-permute-start | bytes 49160 | tf_op jit(solution)/shard_map/ppermute | solution.py:638
  90.3 3.7 %collective-permute-start.1 = (f32[32,128]{1,0:T(8,128)S(1)}, f32[32,128]{1,0:T(8,128)S(1)}, u32[]{:S(2)}, u32[]{:S(2)}) collective-permute-start(f32[32,128]{1,0:T(8,128)S(1)} %get-tuple-element.88.a_ref), channel_id=1, source_target_pairs={{0,64},{64,0},{128,192},{192,128},{1,65},{65,1},{129,193},{193,129... | collective-permute-start | bytes 49160 | tf_op jit(solution)/shard_map/ppermute | solution.py:638
  113.9 1.7 %collective-permute-start.4 = (bf16[64,24,128]{2,1,0:T(8,128)(2,1)S(1)}, bf16[64,24,128]{2,1,0:T(8,128)(2,1)S(1)}, u32[]{:S(2)}, u32[]{:S(2)}) collective-permute-start(bf16[64,24,128]{2,1,0:T(8,128)(2,1)S(1)} %all_to_all.27.recv_ref), channel_id=1, source_target_pairs={{0,64},{64,0},{128,192},{192,128},{1,65},{65,1},{129,193},{193,129... | collective-permute-start | bytes 1179656 | tf_op jit(solution)/shard_map/ppermute | solution.py:643

commit v5 on v4

--- a/solution.py
+++ b/solution.py
@@ -476,11 +476,15 @@
     grad_ref[...] = (dfirst_ref[...].astype(F32) + dx + dx_plane).astype(BF16)
 
 
-def spread_kernel(a_ref, b_ref, c_ref, d_ref, out_ref, scr):
-    near = a_ref[...] + c_ref[...]
-    total = near + (b_ref[...] + d_ref[...])
+def core_sum_kernel(own_ref, other_ref, out_ref):
+    out_ref[0:16, :] = own_ref[0:16, :] + other_ref[0:16, :]
+    out_ref[16:32, :] = own_ref[16:32, :]
+
+
+def spread_kernel(own_ref, far_ref, out_ref, scr):
+    total = own_ref[...] + far_ref[...]
     scr[0:8, :] = jnp.where(core_index() == 0, total[0:8], total[8:16])
-    scr[8:24, :] = near[16:32]
+    scr[8:24, :] = total[16:32]
     out_ref[...] = jnp.broadcast_to(scr[...].astype(BF16)[None], out_ref.shape)
 
 
@@ -635,10 +639,11 @@
         [(2, 16, C)],
         recv, dproj, x, proj_start, args, parts,
     )
-    others = [lax.ppermute(part, "dp", [(i, i ^ d) for i in range(n_dp)]) for d in range(1, n_dp)]
+    part = call(core_sum_kernel, shape((32, C)), [], part, lax.ppermute(part, "dp", to_core))
+    far = lax.ppermute(part, "dp", [(i, i ^ 2) for i in range(n_dp)])
     grad = call(grad_kernel, shape(tokens, BF16), [], dn, dn_plane, dfirst, x, args)
-    grad, *others = lax.optimization_barrier((grad, *others))
-    send = call(spread_kernel, shape((n_dst, 24, C), BF16), [(24, C)], part, *others)
+    grad, far = lax.optimization_barrier((grad, far))
+    send = call(spread_kernel, shape((n_dst, 24, C), BF16), [(24, C)], part, far)
     recv = swap(send)
     other = lax.ppermute(recv, "dp", to_core)
     factor = 1.0 / (n_dp * N)

time: 117 us -> 117 us (level)
  starting transfers between devices: 31.4 us -> 35.5 us
  blocking collectives: 52.4 us -> 49.4 us
  waiting for transfers between devices: 19.5 us -> 17.9 us
    ppermute x1, starting transfers between devices: 0.01 us -> 4.43 us  [local(): other = lax.ppermute(recv, 'dp', to_core)]
    all_to_all x3, blocking collectives: 52.4 us -> 49.4 us  [swap(): lax.all_to_all(buffer, 'dap', split_axis=0, concat_axis=0, tiled=True)]
    ppermute x3 -> x2, waiting for transfers between devices: 2.65 us -> 1.36 us  [the longest x1 0.84 us: local(): lax.ppermute(part, 'dp', to_core)]
    ppermute x3 -> x2, starting transfers between devices: 9.38 us -> 9 us  [the longest x1 6.38 us: local(): lax.ppermute(part, 'dp', to_core)]
    pallas_call x10 -> x11, Pallas kernels: 12.7 us -> 12.8 us  [call(): pl.pallas_call(body, out_shape=out_shape, in_specs=[pl.BlockSpec(memory_s...]
  transfers between devices with their start and end apart: 7 -> 6, of which waited for: 6 -> 6; matrix products, arithmetic and copies ran while one was open for 0% -> 0% of each run, Pallas kernels for 2% -> 2%
where the time goes in v5:
time: 117 us; the launch traced here: 116 us
  blocking collectives  49.4 us (42%)
  starting transfers between devices  35.5 us (30%)
  waiting for transfers between devices  17.9 us (15%)
  Pallas kernels  12.8 us (11%)
    all_to_all x3, blocking collectives, swap(): lax.all_to_all(buffer, 'dap', split_axis=0, concat_axis=0, tiled=True)  49.4 us
    all_to_all x2, starting transfers between devices, swap(): lax.all_to_all(buffer, 'dap', split_axis=0, concat_axis=0, tiled=True)  18.5 us
    all_to_all x2, waiting for transfers between devices, swap(): lax.all_to_all(buffer, 'dap', split_axis=0, concat_axis=0, tiled=True)  14.1 us
    pallas_call x11, Pallas kernels, call(): pl.pallas_call(body, out_shape=out_shape, in_specs=[pl.BlockSpec(memory_s...  12.8 us
    ppermute x1, starting transfers between devices, local(): lax.ppermute(part, 'dp', to_core)  6.38 us
    ppermute x1, starting transfers between devices, local(): other = lax.ppermute(recv, 'dp', to_core)  4.43 us
    ppermute x1, starting transfers between devices, local(): got = lax.ppermute(give, 'dp', to_core)  3.56 us
    ppermute x1, starting transfers between devices, local(): far = lax.ppermute(part, 'dp', [(i, i ^ 2) for i in range(n_dp)])  2.62 us
  transfers between devices with their start and end apart: 6, of which 6 were waited for; matrix products, arithmetic and copies ran while one was open for 0% of the time, Pallas kernels for 2%

profile of v5, /device:TPU:1, one launch (start us, length us, event | category | flops | bytes accessed | tf_op | source)
XLA Modules:
  0.0 116.3 jit_solution(8112344175814340972)
XLA Ops:
  0.6 0.0 copy-start.1
  0.7 2.0 %shard_map.229 = (bf16[64,8,128]{2,1,0:T(8,128)(2,1)}, f32[8,128]{1,0:T(8,128)S(1)}, bf16[32,128]{1,0:T(8,128)(2,1)S(1)}) custom-call(bf16[256,128]{1,0:T(8,128)(2,1)} %bitcast.13, f32[1,128]{1,0:T(1,128)} %bitcast.22, f32[4,128]{1,0:T(4,128)} %bitcast.20, f32[1,128]{1,0:T(1,128)} %bitcast.23, f32[4,128]{1,0:T(4,128)} %bitcast.21, f32[1,128]{1,0:T(1,128)} %bitcast.24, ...), custom_call_target="tpu_custom_call" | custom-call | tf_op jit(solution)/shard_map/pallas_call | solution.py:559
  2.6 0.0 copy-start
  2.6 13.6 %all-to-all-start = ((bf16[64,8,128]{2,1,0:T(8,128)(2,1)}), bf16[64,8,128]{2,1,0:T(8,128)(2,1)S(1)}, u32[]{:S(2)}, u32[]{:S(2)}) async-start(bf16[64,8,128]{2,1,0:T(8,128)(2,1)} %get-tuple-element.56), calls=%async_computation | async-start | bytes 262144 | tf_op jit(solution)/shard_map/all_to_all | solution.py:570
  16.3 0.0 copy-done.1
  16.3 0.0 copy-done
  16.3 1.3 %shard_map.230 = (bf16[256,384]{1,0:T(8,128)(2,1)S(1)}, f32[256,128]{1,0:T(8,128)S(1)}, f32[256,512]{1,0:T(8,128)S(1)}, bf16[256,128]{1,0:T(8,128)(2,1)S(1)}, bf...) custom-call(bf16[256,128]{1,0:T(8,128)(2,1)S(1)} %bitcast.14, bf16[256,128]{1,0:T(8,128)(2,1)} %bitcast.18, ...), custom_call_target="tpu_custom_call" | custom-call | tf_op jit(solution)/shard_map/pallas_call | solution.py:559
  17.6 8.6 %all-to-all-done.recv_ref = bf16[64,8,128]{2,1,0:T(8,128)(2,1)S(1)} async-done(((bf16[64,8,128]{2,1,0:T(8,128)(2,1)}), bf16[64,8,128]{2,1,0:T(8,128)(2,1)S(1)}, u32[]{:S(2)}, u32[]{:S(2)}) %all-to-all-start) | async-done | bytes 131104 | tf_op jit(solution)/shard_map/all_to_all | solution.py:570
  26.2 0.0 copy-start.4
  26.2 0.0 copy-start.5
  26.2 1.0 shard_map.231
  27.2 0.0 copy-start.2
  27.2 0.0 copy-start.3
  27.2 14.7 %all_to_all.25.recv_ref = bf16[64,16,128]{2,1,0:T(8,128)(2,1)S(1)} all-to-all(bf16[64,16,128]{2,1,0:T(8,128)(2,1)S(1)} %get-tuple-element.64), channel_id=1, replica_groups=mesh['dp'=4,'dap'=64] {'dap'}, dimensions={0} | all-to-all | bytes 524288 | tf_op jit(solution)/shard_map/all_to_all | solution.py:570
  41.9 0.0 copy-done.4
  41.9 0.0 copy-done.5
  41.9 0.0 copy-done.2
  41.9 0.0 copy-done.3
  42.0 3.4 %shard_map.232 = (bf16[64,16,128]{2,1,0:T(8,128)(2,1)}, f32[8,128]{1,0:T(8,128)S(1)}, bf16[256,512]{1,0:T(8,128)(2,1)S(1)}, bf16[256,512]{1,0:T(8,128)(2,1)S(1)}...) custom-call(bf16[64,16,128]{2,1,0:T(8,128)(2,1)S(1)} %all_to_all.25., ...), custom_call_target="tpu_custom_call" | custom-call | tf_op jit(solution)/shard_map/pallas_call | solution.py:559
  45.3 4.9 %all-to-all-start.2 = ((bf16[64,16,128]{2,1,0:T(8,128)(2,1)}), bf16[64,16,128]{2,1,0:T(8,128)(2,1)S(1)}, u32[]{:S(2)}, u32[]{:S(2)}) async-start(bf16[64,16,128]{2,1,0:T(8,128)(2,1)} %get-tuple-element.65), calls=%async_computation.2 | async-start | bytes 524288 | tf_op jit(solution)/shard_map/all_to_all | solution.py:570
  50.2 0.5 shard_map.233
  50.7 3.6 %collective-permute-start = (bf16[832,128]{1,0:T(8,128)(2,1)S(1)}, bf16[832,128]{1,0:T(8,128)(2,1)S(1)}, u32[]{:S(2)}, u32[]{:S(2)}) collective-permute-start(bf16[832,128]{1,0:T(8,128)(2,1)S(1)} %get-tuple-element.75), channel_id=1, source_target_pairs={{0,64},{64,0},{128,192},{192,128},{1,65},{65,1},{129,193},{193,129... | collective-permute-start | bytes 638984 | tf_op jit(solution)/shard_map/ppermute | solution.py:628
  54.3 1.1 collective-permute-done.got_ref
  55.3 5.5 %all-to-all-done.2.recv_ref = bf16[64,16,128]{2,1,0:T(8,128)(2,1)S(1)} async-done(((bf16[64,16,128]{2,1,0:T(8,128)(2,1)}), bf16[64,16,128]{2,1,0:T(8,128)(2,1)S(1)}, u32[]{:S(2)}, u32[]{:S(2)}) %all-to-all-start.2) | async-done | bytes 262176 | tf_op jit(solution)/shard_map/all_to_all | solution.py:570
  60.8 2.0 %shard_map.234 = (bf16[64,32,128]{2,1,0:T(8,128)(2,1)S(1)}, bf16[256,128]{1,0:T(8,128)(2,1)S(1)}, bf16[256,512]{1,0:T(8,128)(2,1)S(1)}) custom-call(bf16[64,16,128]{2,1,0:T(8,128)(2,1)S(1)} %all-to-all-done.2.recv_ref, f32[832,128]{1,0:T(8,128)S(1)} %get-tuple-element.74.keep_ref, bf16[832,128]{1,0:T(8,128)(2,1)S(1)} %collective-permute-done.got_ref, ...), custom_call_target="tpu_custom_call" | custom-call | tf_op jit(solution)/shard_map/pallas_call | solution.py:559
  62.8 17.9 %all_to_all.26.recv_ref = bf16[64,32,128]{2,1,0:T(8,128)(2,1)S(1)} all-to-all(bf16[64,32,128]{2,1,0:T(8,128)(2,1)S(1)} %get-tuple-element.81), channel_id=1, replica_groups=mesh['dp'=4,'dap'=64] {'dap'}, dimensions={0} | all-to-all | bytes 1048576 | tf_op jit(solution)/shard_map/all_to_all | solution.py:570
  80.7 0.4 shard_map.235
  81.1 6.4 %collective-permute-start.1 = (f32[32,128]{1,0:T(8,128)S(1)}, f32[32,128]{1,0:T(8,128)S(1)}, u32[]{:S(2)}, u32[]{:S(2)}) collective-permute-start(f32[32,128]{1,0:T(8,128)S(1)} %get-tuple-element.86.own_ref), channel_id=1, source_target_pairs={{0,64},{64,0},{128,192},{192,128},{1,65},{65,1},{129,193},{193,129... | collective-permute-start | bytes 49160 | tf_op jit(solution)/shard_map/ppermute | solution.py:642
  87.5 0.8 collective-permute-done.1.other_ref
  88.3 2.6 %collective-permute-start.2 = (f32[32,128]{1,0:T(8,128)S(1)}, f32[32,128]{1,0:T(8,128)S(1)}, u32[]{:S(2)}, u32[]{:S(2)}) collective-permute-start(f32[32,128]{1,0:T(8,128)S(1)} %shard_map.237.own_ref), channel_id=1, source_target_pairs={{0,128},{64,192},{128,0},{192,64},{1,129},{65,193},{129,1},{193,65... | collective-permute-start | bytes 49160 | tf_op jit(solution)/shard_map/ppermute | solution.py:643
  90.9 1.0 shard_map.236
  91.9 0.5 collective-permute-done.2.far_ref
  92.4 16.7 %all_to_all.27.recv_ref = bf16[64,24,128]{2,1,0:T(8,128)(2,1)S(1)} all-to-all(bf16[64,24,128]{2,1,0:T(8,128)(2,1)S(1)} %shard_map.238), channel_id=1, replica_groups=mesh['dp'=4,'dap'=64] {'dap'}, dimensions={0} | all-to-all | bytes 786432 | tf_op jit(solution)/shard_map/all_to_all | solution.py:570
  109.2 4.4 %collective-permute-start.3 = (bf16[64,24,128]{2,1,0:T(8,128)(2,1)S(1)}, bf16[64,24,128]{2,1,0:T(8,128)(2,1)S(1)}, u32[]{:S(2)}, u32[]{:S(2)}) collective-permute-start(bf16[64,24,128]{2,1,0:T(8,128)(2,1)S(1)} %all_to_all.27.recv_ref), channel_id=1, source_target_pairs={{0,64},{64,0},{128,192},{192,128},{1,65},{65,1},{129,193},{193,129... | collective-permute-start | bytes 1179656 | tf_op jit(solution)/shard_map/ppermute | solution.py:648
  113.6 1.3 %collective-permute-done.3.other_ref = bf16[64,24,128]{2,1,0:T(8,128)(2,1)S(1)} collective-permute-done((bf16[64,24,128]{2,1,0:T(8,128)(2,1)S(1)}, bf16[64,24,128]{2,1,0:T(8,128)(2,1)S(1)}, u32[]{:S(2)}, u32[]{:S(2)}) %collective-permute-start.3) | collective-permute-done | bytes 393248 | tf_op jit(solution)/shard_map/ppermute | solution.py:648
  114.9 1.3 %shard_map.239 = (f32[1,128]{1,0:T(1,128)}, f32[128,512]{1,0:T(8,128)}, f32[4,128]{1,0:T(4,128)}, f32[128,128]{1,0:T(8,128)}, f32[1,128]{1,0:T(1,128)}, /*index=...) custom-call(bf16[64,24,128]{2,1,0:T(8,128)(2,1)S(1)} %all_to_all.27., ...), custom_call_target="tpu_custom_call" | custom-call | tf_op jit(solution)/shard_map/pallas_call | solution.py:559
  (2 shorter events, 0.0 us)
Async XLA Ops:
  0.6 15.7 %copy-start.1 = (f32[128,512]{1,0:T(8,128)S(1)}, f32[128,512]{1,0:T(8,128)}, u32[]{:S(2)}) copy-start(f32[128,512]{1,0:T(8,128)} %w_ref.5) | copy-start | bytes 786436
  2.6 13.7 %copy-start = (bf16[1,2,128,128]{3,2,1,0:T(8,128)(2,1)S(1)}, bf16[1,2,128,128]{3,2,1,0:T(8,128)(2,1)}, u32[]{:S(2)}) copy-start(bf16[1,2,128,128]{3,2,1,0:T(8,128)(2,1)} %param.14) | copy-start | bytes 196612
  2.6 23.5 %all-to-all-start = ((bf16[64,8,128]{2,1,0:T(8,128)(2,1)}), bf16[64,8,128]{2,1,0:T(8,128)(2,1)S(1)}, u32[]{:S(2)}, u32[]{:S(2)}) async-start(bf16[64,8,128]{2,1,0:T(8,128)(2,1)} %get-tuple-element.56), calls=%async_computation | async-start | bytes 262144 | tf_op jit(solution)/shard_map/all_to_all | solution.py:570
  26.2 15.7 %copy-start.4 = (f32[512,128]{1,0:T(8,128)S(1)}, f32[512,128]{1,0:T(8,128)}, u32[]{:S(2)}) copy-start(f32[512,128]{1,0:T(8,128)} %wd_ref.1) | copy-start | bytes 786436
  26.2 15.7 %copy-start.5 = (f32[128,128]{1,0:T(8,128)S(1)}, f32[128,128]{1,0:T(8,128)}, u32[]{:S(2)}) copy-start(f32[128,128]{1,0:T(8,128)} %wo_ref.1) | copy-start | bytes 196612
  27.2 14.7 %copy-start.2 = (f32[128,512]{1,0:T(8,128)S(1)}, f32[128,512]{1,0:T(8,128)}, u32[]{:S(2)}) copy-start(f32[128,512]{1,0:T(8,128)} %w_ref.4) | copy-start | bytes 786436
  27.2 14.7 %copy-start.3 = (f32[128,512]{1,0:T(8,128)S(1)}, f32[128,512]{1,0:T(8,128)}, u32[]{:S(2)}) copy-start(f32[128,512]{1,0:T(8,128)} %wu_ref.1) | copy-start | bytes 786436
  45.3 15.5 %all-to-all-start.2 = ((bf16[64,16,128]{2,1,0:T(8,128)(2,1)}), bf16[64,16,128]{2,1,0:T(8,128)(2,1)S(1)}, u32[]{:S(2)}, u32[]{:S(2)}) async-start(bf16[64,16,128]{2,1,0:T(8,128)(2,1)} %get-tuple-element.65), calls=%async_computation.2 | async-start | bytes 524288 | tf_op jit(solution)/shard_map/all_to_all | solution.py:570
  50.7 4.7 %collective-permute-start = (bf16[832,128]{1,0:T(8,128)(2,1)S(1)}, bf16[832,128]{1,0:T(8,128)(2,1)S(1)}, u32[]{:S(2)}, u32[]{:S(2)}) collective-permute-start(bf16[832,128]{1,0:T(8,128)(2,1)S(1)} %get-tuple-element.75), channel_id=1, source_target_pairs={{0,64},{64,0},{128,192},{192,128},{1,65},{65,1},{129,193},{193,129... | collective-permute-start | bytes 638984 | tf_op jit(solution)/shard_map/ppermute | solution.py:628
  81.1 7.2 %collective-permute-start.1 = (f32[32,128]{1,0:T(8,128)S(1)}, f32[32,128]{1,0:T(8,128)S(1)}, u32[]{:S(2)}, u32[]{:S(2)}) collective-permute-start(f32[32,128]{1,0:T(8,128)S(1)} %get-tuple-element.86.own_ref), channel_id=1, source_target_pairs={{0,64},{64,0},{128,192},{192,128},{1,65},{65,1},{129,193},{193,129... | collective-permute-start | bytes 49160 | tf_op jit(solution)/shard_map/ppermute | solution.py:642
  88.3 4.1 %collective-permute-start.2 = (f32[32,128]{1,0:T(8,128)S(1)}, f32[32,128]{1,0:T(8,128)S(1)}, u32[]{:S(2)}, u32[]{:S(2)}) collective-permute-start(f32[32,128]{1,0:T(8,128)S(1)} %shard_map.237.own_ref), channel_id=1, source_target_pairs={{0,128},{64,192},{128,0},{192,64},{1,129},{65,193},{129,1},{193,65... | collective-permute-start | bytes 49160 | tf_op jit(solution)/shard_map/ppermute | solution.py:643
  109.2 5.8 %collective-permute-start.3 = (bf16[64,24,128]{2,1,0:T(8,128)(2,1)S(1)}, bf16[64,24,128]{2,1,0:T(8,128)(2,1)S(1)}, u32[]{:S(2)}, u32[]{:S(2)}) collective-permute-start(bf16[64,24,128]{2,1,0:T(8,128)(2,1)S(1)} %all_to_all.27.recv_ref), channel_id=1, source_target_pairs={{0,64},{64,0},{128,192},{192,128},{1,65},{65,1},{129,193},{193,129... | collective-permute-start | bytes 1179656 | tf_op jit(solution)/shard_map/ppermute | solution.py:648

commit v6 on v5

--- a/solution.py
+++ b/solution.py
@@ -100,16 +100,19 @@
 
 
 def plane_local_kernel(
-    x_hbm, gs_hbm, wts_hbm, ge_hbm, wte_hbm, gt_hbm, mask_hbm,
-    out_ref, args_ref, parts_ref,
-    x_ref, gs, wts, ge, wte, gt, mask, small, scr, sems,
+    x_hbm, gs_hbm, wts_hbm, ge_hbm, wte_hbm, gt_hbm, mask_hbm, w_hbm, cot_hbm, wo_hbm,
+    out_ref, args_ref, parts_ref, x_ref, qkv_ref, gating_ref, score_ref, n_ref, cot_ref, wo_ref,
+    gs, wts, ge, wte, gt, mask, w_ref, small, scr, sems,
 ):
     n_dst, rows, _ = out_ref.shape
-    moves = [(gs_hbm, gs), (wts_hbm, wts), (x_hbm, x_ref), (ge_hbm, ge), (wte_hbm, wte), (gt_hbm, gt), (mask_hbm, mask)]
+    moves = [
+        (x_hbm, x_ref), (gs_hbm, gs), (wts_hbm, wts), (ge_hbm, ge), (wte_hbm, wte), (gt_hbm, gt), (mask_hbm, mask),
+        (w_hbm, w_ref), (cot_hbm, cot_ref), (wo_hbm, wo_ref),
+    ]
     copies = [pltpu.make_async_copy(src, dst, sems.at[i]) for i, (src, dst) in enumerate(moves)]
     for copy in copies:
         copy.start()
-    for copy in copies:
+    for copy in copies[:-3]:
         copy.wait()
     parts_ref[WT_S, :] = split(scr, wts[...])
     parts_ref[WT_E, :] = split(scr, wte[...])
@@ -124,30 +127,24 @@
     small[0:HEADS, :] = plane[:, :C]
     small[HEADS : 2 * HEADS, :] = plane[:, C:]
     out_ref[...] = jnp.broadcast_to(small[...].astype(BF16)[None], (n_dst, rows, C))
-
-
-def start_scores_kernel(
-    x_ref, cot_hbm, args_ref, w_ref, wo_hbm,
-    qkv_ref, gating_ref, score_ref, n_ref, cot_ref, wo_ref,
-    sems,
-):
-    copies = [pltpu.make_async_copy(cot_hbm, cot_ref, sems.at[0]), pltpu.make_async_copy(wo_hbm, wo_ref, sems.at[1])]
-    for copy in copies:
-        copy.start()
-    N = score_ref.shape[1] // HEADS
+    n_ref[...] = n
+    copies[-3].wait()
+    w = w_ref[...].astype(BF16)
     masks = head_masks(BF16)
-    xhat, _ = ln_stats(x_ref[...].astype(F32))
-    n = (xhat * args_ref[G_S, :]).astype(BF16)
-    n_ref[...] = n
-    q, k, v, gating = project(n, w_ref[...].astype(BF16))
-    qkv_ref[:, :C] = q
-    qkv_ref[:, C : 2 * C] = k
-    qkv_ref[:, 2 * C :] = v
-    gating_ref[...] = gating
-    for r in range(2):
+    N = 2 * n_dst
+
+    def chain(r):
         part = slice(r * N, (r + 1) * N)
-        score_ref[part, :] = dot(q[part], stack_heads(k[part], masks), NT)
-    for copy in copies:
+        q, k, v, gating = project(n[part], w)
+        yield
+        qkv_ref[part, :C] = q
+        qkv_ref[part, C : 2 * C] = k
+        qkv_ref[part, 2 * C :] = v
+        gating_ref[part, :] = gating
+        score_ref[part, :] = dot(q, stack_heads(k, masks), NT)
+
+    interleave([chain(r) for r in range(2)])
+    for copy in copies[-2:]:
         copy.wait()
 
 
@@ -230,7 +227,6 @@
 ):
     n_dst, in_rows, _ = recv_ref.shape
     N = 2 * n_dst
-    rows = send_ref.shape[1]
     fscr[...] = recv_ref[...].astype(F32).reshape(n_dst * in_rows, C)
     for r in range(2):
         for a in range(2):
@@ -327,12 +323,10 @@
     plane[...] = ds + ds_b
     for r in range(2):
         for h in range(HEADS):
-            sscr[pl.ds(r * 4 + h, n_dst, stride=rows), :] = rows_of(plane, h * N + r, n_dst, 2)
+            sscr[pl.ds(r * 8 + h, n_dst, stride=24), :] = rows_of(plane, h * N + r, n_dst, 2)
         for a in range(2):
-            sscr[pl.ds(8 + r * 2 + a, n_dst, stride=rows), :] = rows_of(zscr, a * N + r, n_dst, 2)
-    for i in range(12, rows):
-        sscr[pl.ds(i, n_dst, stride=rows), :] = jnp.zeros((n_dst, C), F32)
-    send_ref[...] = sscr[...].reshape(n_dst, rows, C).astype(BF16)
+            sscr[pl.ds(16 + r * 2 + a, n_dst, stride=24), :] = rows_of(zscr, a * N + r, n_dst, 2)
+    send_ref[...] = sscr[...].reshape(n_dst, 3, 8, C)[:, :, 0:4, :].astype(BF16)
     small_ref[0:1, :] = dgain_t + dgain_t_b
     small_ref[1:2, :] = dgain + dgain_b
     small_ref[2:8, :] = jnp.zeros((6, C), F32)
@@ -376,15 +370,15 @@
     send_ref, dfirst_ref, dproj_ref,
     fscr, gscr, plane, narrow, wide, sscr, wscr, p_ref,
 ):
-    n_dst, in_rows, _ = recv_ref.shape
+    n_dst = recv_ref.shape[0]
     N = 2 * n_dst
     rows = send_ref.shape[1]
-    recv = recv_ref[...].astype(F32)
-    total = jnp.sum(recv, 0)
-    fscr[...] = recv.reshape(n_dst * in_rows, C)
+    total = jnp.sum(recv_ref[:, 0:2].astype(F32), 0)
+    fscr[:, 0:4, :] = recv_ref[:, 2].astype(F32)
+    grads = fscr.reshape(n_dst * 8, C)
     for r in range(2):
         for a in range(2):
-            gscr[pl.ds(r * N + a, n_dst, stride=2), :] = rows_of(fscr, 8 + r * 2 + a, n_dst, in_rows)
+            gscr[pl.ds(r * N + a, n_dst, stride=2), :] = rows_of(grads, r * 2 + a, n_dst, 8)
     masks = head_masks(BF16)
     masks_f = head_masks(F32)
     gain_e = args_ref[G_E, :]
@@ -397,7 +391,7 @@
         xhat, rstd = ln_stats(first_ref[part, :].astype(F32))
         n_e = (xhat * gain_e).astype(BF16)
         yield
-        dn_e, dbias_e = plane_back(total[r * HEADS : (r + 1) * HEADS], n_e, p_ref.at[r], parts)
+        dn_e, dbias_e = plane_back(total[r], n_e, p_ref.at[r], parts)
         yield
         dxe, dgain_e = ln_back(dn_e, xhat, rstd, gain_e)
         dfirst = (gscr[part, :] + dxe).astype(BF16)
@@ -583,28 +577,21 @@
     tokens = (2 * N, C)
     wide = (C, 4 * C)
 
-    send, args, parts = call(
+    send, args, parts, x_in, qkv, gating, score, n, cot, wo = call(
         plane_local_kernel,
-        [shape((n_dst, 8, C), BF16), shape((8, C)), shape((32, C), BF16)],
-        [pltpu.VMEM(tokens, BF16), (1, C), (HEADS, C), (1, C), (HEADS, C), (1, C),
-         pltpu.VMEM((1, C), jnp.int32), (8, C), (16, C), pltpu.SemaphoreType.DMA((7,))],
-        x, g_s, wt_s, g_e, wt_e, g_t, residue_mask,
-        in_hbm=range(7),
+        [shape((n_dst, 8, C), BF16), shape((8, C)), shape((32, C), BF16), shape(tokens, BF16), shape((2 * N, 3 * C), BF16),
+         shape(tokens), shape((2 * N, HEADS * N)), shape(tokens, BF16), shape(tokens, BF16), shape((C, C))],
+        [(1, C), (HEADS, C), (1, C), (HEADS, C), (1, C), pltpu.VMEM((1, C), jnp.int32), wide,
+         (8, C), (16, C), pltpu.SemaphoreType.DMA((10,))],
+        x, g_s, wt_s, g_e, wt_e, g_t, residue_mask, proj_start, cot, output_start,
+        in_hbm=range(10),
     )
     recv = swap(send)
-    qkv, gating, score, n, cot, wo = call(
-        start_scores_kernel,
-        [shape((2 * N, 3 * C), BF16), shape(tokens), shape((2 * N, HEADS * N)), shape(tokens, BF16),
-         shape(tokens, BF16), shape((C, C))],
-        [pltpu.SemaphoreType.DMA((2,))],
-        x, cot, args, proj_start, output_start,
-        in_hbm=(1, 4),
-    )
     send, mix, prob, first = call(
         start_forward_kernel,
         [shape((n_dst, 16, C), BF16), shape(tokens), shape((2 * N, HEADS * N)), shape(tokens, BF16)],
         [(n_dst * 8, C), (HEADS * N, N), (n_dst * 16, C), (8, C)],
-        recv, x, cot, args, parts, qkv, gating, score, wo,
+        recv, x_in, cot, args, parts, qkv, gating, score, wo,
     )
     recv = swap(send)
     n_dp = lax.axis_size("dp")
@@ -613,9 +600,9 @@
     hidden = (2 * N, 4 * C)
     send, small, *saved = call(
         end_kernel,
-        [shape((n_dst, 16, C), BF16), shape((8, C)), shape(hidden, BF16), shape(hidden, BF16), shape(tokens, BF16),
+        [shape((n_dst, 3, 4, C), BF16), shape((8, C)), shape(hidden, BF16), shape(hidden, BF16), shape(tokens, BF16),
          shape(tokens, BF16), shape(tokens, BF16), shape(hidden, BF16), shape(tokens, BF16), shape(tokens, BF16)],
-        [(n_dst * 16, C), tokens, tokens, (HEADS * N, N), (n_dst * 16, C)],
+        [(n_dst * 16, C), tokens, tokens, (HEADS * N, N), (n_dst * 24, C)],
         recv, args, proj_end, output_end, transition_up, transition_down,
     )
     recv = swap(send)
@@ -629,7 +616,7 @@
     send, dfirst, dproj = call(
         start_backward_kernel,
         [shape((n_dst, 32, C), BF16), shape(tokens, BF16), shape(hidden, BF16)],
-        [(n_dst * 16, C), tokens, (HEADS * N, N), (C, C), (4 * C, C), (n_dst * 32, C), half, (2, 16, C)],
+        [(n_dst, 8, C), tokens, (HEADS * N, N), (C, C), (4 * C, C), (n_dst * 32, C), half, (2, 16, C)],
         recv, keep, got, small, n, first, qkv, gating, mix, prob, args, parts, wo,
     )
     recv = swap(send)

time: 117 us -> 116 us (level)
  blocking collectives: 49.4 us -> 73.7 us
  starting transfers between devices: 35.5 us -> 21.4 us
  waiting for transfers between devices: 17.9 us -> 8.79 us
  Pallas kernels: 12.8 us -> 11.1 us
    all_to_all x3 -> x4, blocking collectives: 49.4 us -> 73.7 us  [swap(): lax.all_to_all(buffer, 'dap', split_axis=0, concat_axis=0, tiled=True)]
    all_to_all x2 -> x1, starting transfers between devices: 18.5 us -> 4.86 us  [swap(): lax.all_to_all(buffer, 'dap', split_axis=0, concat_axis=0, tiled=True)]
    all_to_all x2 -> x1, waiting for transfers between devices: 14.1 us -> 4.99 us  [swap(): lax.all_to_all(buffer, 'dap', split_axis=0, concat_axis=0, tiled=True)]
    pallas_call x11 -> x10, Pallas kernels: 12.8 us -> 11.1 us  [call(): pl.pallas_call(body, out_shape=out_shape, in_specs=[pl.BlockSpec(memory_s...]
  transfers between devices with their start and end apart: 6 -> 5, of which waited for: 6 -> 5; matrix products, arithmetic and copies ran while one was open for 0% -> 0% of each run, Pallas kernels for 2% -> 1%
where the time goes in v6:
time: 116 us
  blocking collectives  73.7 us (64%)
  starting transfers between devices  21.4 us (18%)
  Pallas kernels  11.1 us (10%)
  waiting for transfers between devices  8.79 us (8%)
    all_to_all x4, blocking collectives, swap(): lax.all_to_all(buffer, 'dap', split_axis=0, concat_axis=0, tiled=True)  73.7 us
    pallas_call x10, Pallas kernels, call(): pl.pallas_call(body, out_shape=out_shape, in_specs=[pl.BlockSpec(memory_s...  11.1 us
    ppermute x1, starting transfers between devices, local(): lax.ppermute(part, 'dp', to_core)  5.91 us
    all_to_all x1, waiting for transfers between devices, swap(): lax.all_to_all(buffer, 'dap', split_axis=0, concat_axis=0, tiled=True)  4.99 us
    all_to_all x1, starting transfers between devices, swap(): lax.all_to_all(buffer, 'dap', split_axis=0, concat_axis=0, tiled=True)  4.86 us
    ppermute x1, starting transfers between devices, local(): other = lax.ppermute(recv, 'dp', to_core)  4.43 us
    ppermute x1, starting transfers between devices, local(): got = lax.ppermute(give, 'dp', to_core)  3.56 us
    ppermute x1, starting transfers between devices, local(): far = lax.ppermute(part, 'dp', [(i, i ^ 2) for i in range(n_dp)])  2.62 us
  transfers between devices with their start and end apart: 5, of which 5 were waited for; matrix products, arithmetic and copies ran while one was open for 0% of the time, Pallas kernels for 1%

profile of v6, /device:TPU:1, one launch (start us, length us, event | category | flops | bytes accessed | tf_op | source)
XLA Modules:
  0.0 115.7 jit_solution(6260239339099129945)
XLA Ops:
  0.6 1.7 %shard_map.229 = (bf16[64,8,128]{2,1,0:T(8,128)(2,1)S(1)}, f32[8,128]{1,0:T(8,128)S(1)}, bf16[32,128]{1,0:T(8,128)(2,1)S(1)}, bf16[256,128]{1,0:T(8,128)(2,1)S(1...) custom-call(bf16[256,128]{1,0:T(8,128)(2,1)} %bitcast.13, ...), custom_call_target="tpu_custom_call" | custom-call | tf_op jit(solution)/shard_map/pallas_call | solution.py:553
  2.4 23.2 %all_to_all.25.recv_ref = bf16[64,8,128]{2,1,0:T(8,128)(2,1)S(1)} all-to-all(bf16[64,8,128]{2,1,0:T(8,128)(2,1)S(1)} %get-tuple-element.57), channel_id=1, replica_groups=mesh['dp'=4,'dap'=64] {'dap'}, dimensions={0} | all-to-all | bytes 262144 | tf_op jit(solution)/shard_map/all_to_all | solution.py:564
  25.6 0.0 copy-start.4
  25.6 0.0 copy-start.5
  25.6 1.0 shard_map.230
  26.6 0.0 copy-start.2
  26.6 0.0 copy-start.3
  26.6 14.7 %all_to_all.26.recv_ref = bf16[64,16,128]{2,1,0:T(8,128)(2,1)S(1)} all-to-all(bf16[64,16,128]{2,1,0:T(8,128)(2,1)S(1)} %get-tuple-element.66), channel_id=1, replica_groups=mesh['dp'=4,'dap'=64] {'dap'}, dimensions={0} | all-to-all | bytes 524288 | tf_op jit(solution)/shard_map/all_to_all | solution.py:564
  41.3 0.0 copy-done.4
  41.3 0.0 copy-done.5
  41.3 0.0 copy-done.2
  41.3 0.0 copy-done.3
  41.3 3.3 %shard_map.231 = (bf16[64,3,4,128]{3,2,1,0:T(4,128)(2,1)}, f32[8,128]{1,0:T(8,128)S(1)}, bf16[256,512]{1,0:T(8,128)(2,1)S(1)}, bf16[256,512]{1,0:T(8,128)(2,1)S(...) custom-call(bf16[64,16,128]{2,1,0:T(8,128)(2,1)S(1)} %all_to_all.26., ...), custom_call_target="tpu_custom_call" | custom-call | tf_op jit(solution)/shard_map/pallas_call | solution.py:553
  44.7 4.9 %all-to-all-start.2 = ((bf16[64,3,4,128]{3,2,1,0:T(4,128)(2,1)}), bf16[64,3,4,128]{3,2,1,0:T(4,128)(2,1)S(1)}, u32[]{:S(2)}, u32[]{:S(2)}) async-start(bf16[64,3,4,128]{3,2,1,0:T(4,128)(2,1)} %get-tuple-element.67), calls=%async_computation.2 | async-start | bytes 393216 | tf_op jit(solution)/shard_map/all_to_all | solution.py:564
  49.5 0.5 shard_map.232
  50.0 3.6 %collective-permute-start = (bf16[832,128]{1,0:T(8,128)(2,1)S(1)}, bf16[832,128]{1,0:T(8,128)(2,1)S(1)}, u32[]{:S(2)}, u32[]{:S(2)}) collective-permute-start(bf16[832,128]{1,0:T(8,128)(2,1)S(1)} %get-tuple-element.77), channel_id=1, source_target_pairs={{0,64},{64,0},{128,192},{192,128},{1,65},{65,1},{129,193},{193,129... | collective-permute-start | bytes 638984 | tf_op jit(solution)/shard_map/ppermute | solution.py:615
  53.6 1.1 collective-permute-done.got_ref
  54.7 5.0 %all-to-all-done.2.recv_ref = bf16[64,3,4,128]{3,2,1,0:T(4,128)(2,1)S(1)} async-done(((bf16[64,3,4,128]{3,2,1,0:T(4,128)(2,1)}), bf16[64,3,4,128]{3,2,1,0:T(4,128)(2,1)S(1)}, u32[]{:S(2)}, u32[]{:S(2)}) %all-to-all-start.2) | async-done | bytes 196640 | tf_op jit(solution)/shard_map/all_to_all | solution.py:564
  59.7 1.9 %shard_map.233 = (bf16[64,32,128]{2,1,0:T(8,128)(2,1)S(1)}, bf16[256,128]{1,0:T(8,128)(2,1)S(1)}, bf16[256,512]{1,0:T(8,128)(2,1)S(1)}) custom-call(bf16[64,3,4,128]{3,2,1,0:T(4,128)(2,1)S(1)} %all-to-all-done.2.recv_ref, f32[832,128]{1,0:T(8,128)S(1)} %get-tuple-element.76.keep_ref, bf16[832,128]{1,0:T(8,128)(2,1)S(1)} %collective-permute-done.got_ref, ...), custom_call_target="tpu_custom_call" | custom-call | tf_op jit(solution)/shard_map/pallas_call | solution.py:553
  61.6 0.0 copy-start
  61.6 0.0 copy-start.1
  61.6 19.0 %all_to_all.27.recv_ref = bf16[64,32,128]{2,1,0:T(8,128)(2,1)S(1)} all-to-all(bf16[64,32,128]{2,1,0:T(8,128)(2,1)S(1)} %get-tuple-element.83), channel_id=1, replica_groups=mesh['dp'=4,'dap'=64] {'dap'}, dimensions={0} | all-to-all | bytes 1048576 | tf_op jit(solution)/shard_map/all_to_all | solution.py:564
  80.6 0.0 copy-done
  80.6 0.0 copy-done.1
  80.6 0.4 shard_map.234
  80.9 5.9 %collective-permute-start.1 = (f32[32,128]{1,0:T(8,128)S(1)}, f32[32,128]{1,0:T(8,128)S(1)}, u32[]{:S(2)}, u32[]{:S(2)}) collective-permute-start(f32[32,128]{1,0:T(8,128)S(1)} %get-tuple-element.88.own_ref), channel_id=1, source_target_pairs={{0,64},{64,0},{128,192},{192,128},{1,65},{65,1},{129,193},{193,129... | collective-permute-start | bytes 49160 | tf_op jit(solution)/shard_map/ppermute | solution.py:629
  86.9 0.8 collective-permute-done.1.other_ref
  87.7 2.6 %collective-permute-start.2 = (f32[32,128]{1,0:T(8,128)S(1)}, f32[32,128]{1,0:T(8,128)S(1)}, u32[]{:S(2)}, u32[]{:S(2)}) collective-permute-start(f32[32,128]{1,0:T(8,128)S(1)} %shard_map.236.own_ref), channel_id=1, source_target_pairs={{0,128},{64,192},{128,0},{192,64},{1,129},{65,193},{129,1},{193,65... | collective-permute-start | bytes 49160 | tf_op jit(solution)/shard_map/ppermute | solution.py:630
  90.3 1.0 shard_map.235
  91.3 0.5 collective-permute-done.2.far_ref
  91.8 16.8 %all_to_all.28.recv_ref = bf16[64,24,128]{2,1,0:T(8,128)(2,1)S(1)} all-to-all(bf16[64,24,128]{2,1,0:T(8,128)(2,1)S(1)} %shard_map.237), channel_id=1, replica_groups=mesh['dp'=4,'dap'=64] {'dap'}, dimensions={0} | all-to-all | bytes 786432 | tf_op jit(solution)/shard_map/all_to_all | solution.py:564
  108.6 4.4 %collective-permute-start.3 = (bf16[64,24,128]{2,1,0:T(8,128)(2,1)S(1)}, bf16[64,24,128]{2,1,0:T(8,128)(2,1)S(1)}, u32[]{:S(2)}, u32[]{:S(2)}) collective-permute-start(bf16[64,24,128]{2,1,0:T(8,128)(2,1)S(1)} %all_to_all.28.recv_ref), channel_id=1, source_target_pairs={{0,64},{64,0},{128,192},{192,128},{1,65},{65,1},{129,193},{193,129... | collective-permute-start | bytes 1179656 | tf_op jit(solution)/shard_map/ppermute | solution.py:635
  113.1 1.3 %collective-permute-done.3.other_ref = bf16[64,24,128]{2,1,0:T(8,128)(2,1)S(1)} collective-permute-done((bf16[64,24,128]{2,1,0:T(8,128)(2,1)S(1)}, bf16[64,24,128]{2,1,0:T(8,128)(2,1)S(1)}, u32[]{:S(2)}, u32[]{:S(2)}) %collective-permute-start.3) | collective-permute-done | bytes 393248 | tf_op jit(solution)/shard_map/ppermute | solution.py:635
  114.4 1.3 %shard_map.238 = (f32[1,128]{1,0:T(1,128)}, f32[128,512]{1,0:T(8,128)}, f32[4,128]{1,0:T(4,128)}, f32[128,128]{1,0:T(8,128)}, f32[1,128]{1,0:T(1,128)}, /*index=...) custom-call(bf16[64,24,128]{2,1,0:T(8,128)(2,1)S(1)} %all_to_all.28., ...), custom_call_target="tpu_custom_call" | custom-call | tf_op jit(solution)/shard_map/pallas_call | solution.py:553
  (2 shorter events, 0.0 us)
Async XLA Ops:
  25.6 15.8 %copy-start.4 = (f32[512,128]{1,0:T(8,128)S(1)}, f32[512,128]{1,0:T(8,128)}, u32[]{:S(2)}) copy-start(f32[512,128]{1,0:T(8,128)} %wd_ref.1) | copy-start | bytes 786436
  25.6 15.8 %copy-start.5 = (f32[128,128]{1,0:T(8,128)S(1)}, f32[128,128]{1,0:T(8,128)}, u32[]{:S(2)}) copy-start(f32[128,128]{1,0:T(8,128)} %wo_ref.1) | copy-start | bytes 196612
  26.6 14.7 %copy-start.2 = (f32[128,512]{1,0:T(8,128)S(1)}, f32[128,512]{1,0:T(8,128)}, u32[]{:S(2)}) copy-start(f32[128,512]{1,0:T(8,128)} %w_ref.2) | copy-start | bytes 786436
  26.6 14.7 %copy-start.3 = (f32[128,512]{1,0:T(8,128)S(1)}, f32[128,512]{1,0:T(8,128)}, u32[]{:S(2)}) copy-start(f32[128,512]{1,0:T(8,128)} %wu_ref.1) | copy-start | bytes 786436
  44.7 15.0 %all-to-all-start.2 = ((bf16[64,3,4,128]{3,2,1,0:T(4,128)(2,1)}), bf16[64,3,4,128]{3,2,1,0:T(4,128)(2,1)S(1)}, u32[]{:S(2)}, u32[]{:S(2)}) async-start(bf16[64,3,4,128]{3,2,1,0:T(4,128)(2,1)} %get-tuple-element.67), calls=%async_computation.2 | async-start | bytes 393216 | tf_op jit(solution)/shard_map/all_to_all | solution.py:564
  50.0 4.7 %collective-permute-start = (bf16[832,128]{1,0:T(8,128)(2,1)S(1)}, bf16[832,128]{1,0:T(8,128)(2,1)S(1)}, u32[]{:S(2)}, u32[]{:S(2)}) collective-permute-start(bf16[832,128]{1,0:T(8,128)(2,1)S(1)} %get-tuple-element.77), channel_id=1, source_target_pairs={{0,64},{64,0},{128,192},{192,128},{1,65},{65,1},{129,193},{193,129... | collective-permute-start | bytes 638984 | tf_op jit(solution)/shard_map/ppermute | solution.py:615
  61.6 19.0 %copy-start = (f32[128,512]{1,0:T(8,128)S(1)}, f32[128,512]{1,0:T(8,128)}, u32[]{:S(2)}) copy-start(f32[128,512]{1,0:T(8,128)} %w_ref.3) | copy-start | bytes 786436
  61.6 19.0 %copy-start.1 = (bf16[1,2,128,128]{3,2,1,0:T(8,128)(2,1)S(1)}, bf16[1,2,128,128]{3,2,1,0:T(8,128)(2,1)}, u32[]{:S(2)}) copy-start(bf16[1,2,128,128]{3,2,1,0:T(8,128)(2,1)} %param.14) | copy-start | bytes 196612
  80.9 6.7 %collective-permute-start.1 = (f32[32,128]{1,0:T(8,128)S(1)}, f32[32,128]{1,0:T(8,128)S(1)}, u32[]{:S(2)}, u32[]{:S(2)}) collective-permute-start(f32[32,128]{1,0:T(8,128)S(1)} %get-tuple-element.88.own_ref), channel_id=1, source_target_pairs={{0,64},{64,0},{128,192},{192,128},{1,65},{65,1},{129,193},{193,129... | collective-permute-start | bytes 49160 | tf_op jit(solution)/shard_map/ppermute | solution.py:629
  87.7 4.1 %collective-permute-start.2 = (f32[32,128]{1,0:T(8,128)S(1)}, f32[32,128]{1,0:T(8,128)S(1)}, u32[]{:S(2)}, u32[]{:S(2)}) collective-permute-start(f32[32,128]{1,0:T(8,128)S(1)} %shard_map.236.own_ref), channel_id=1, source_target_pairs={{0,128},{64,192},{128,0},{192,64},{1,129},{65,193},{129,1},{193,65... | collective-permute-start | bytes 49160 | tf_op jit(solution)/shard_map/ppermute | solution.py:630
  108.6 5.8 %collective-permute-start.3 = (bf16[64,24,128]{2,1,0:T(8,128)(2,1)S(1)}, bf16[64,24,128]{2,1,0:T(8,128)(2,1)S(1)}, u32[]{:S(2)}, u32[]{:S(2)}) collective-permute-start(bf16[64,24,128]{2,1,0:T(8,128)(2,1)S(1)} %all_to_all.28.recv_ref), channel_id=1, source_target_pairs={{0,64},{64,0},{128,192},{192,128},{1,65},{65,1},{129,193},{193,129... | collective-permute-start | bytes 1179656 | tf_op jit(solution)/shard_map/ppermute | solution.py:635

commit v7 on v6

--- a/solution.py
+++ b/solution.py
@@ -365,8 +365,16 @@
     return dot(p, parts, TN).astype(BF16).astype(F32), dot(p, n)[0:HEADS]
 
 
+def first_norm_kernel(first_ref, gating_ref, mix_ref, args_ref, after_ref, xhat_ref, rstd_ref, n_ref, gated_ref):
+    xhat, rstd = ln_stats(first_ref[...].astype(F32))
+    xhat_ref[...] = xhat
+    rstd_ref[...] = jnp.broadcast_to(rstd, rstd_ref.shape)
+    n_ref[...] = (xhat * args_ref[G_E, :]).astype(BF16)
+    gated_ref[...] = (gating_ref[...] * mix_ref[...]).astype(BF16)
+
+
 def start_backward_kernel(
-    recv_ref, keep_ref, got_ref, small_ref, n_ref, first_ref, qkv_ref, gating_ref, mix_ref, prob_ref, args_ref, parts_ref, wo_ref,
+    recv_ref, keep_ref, got_ref, small_ref, n_ref, xhat_ref, rstd_ref, ne_ref, gated_ref, qkv_ref, gating_ref, mix_ref, prob_ref, args_ref, parts_ref, wo_ref,
     send_ref, dfirst_ref, dproj_ref,
     fscr, gscr, plane, narrow, wide, sscr, wscr, p_ref,
 ):
@@ -388,9 +396,8 @@
 
     def chain(r):
         part = slice(r * N, (r + 1) * N)
-        xhat, rstd = ln_stats(first_ref[part, :].astype(F32))
-        n_e = (xhat * gain_e).astype(BF16)
-        yield
+        xhat, rstd = xhat_ref[part, :], rstd_ref[part, :]
+        n_e = ne_ref[part, :]
         dn_e, dbias_e = plane_back(total[r], n_e, p_ref.at[r], parts)
         yield
         dxe, dgain_e = ln_back(dn_e, xhat, rstd, gain_e)
@@ -430,8 +437,7 @@
     for r in range(2):
         for h in range(HEADS):
             sscr[pl.ds(r * 4 + h, n_dst, stride=rows), :] = rows_of(plane, h * N + r, n_dst, 2)
-    gated = (gating_ref[...] * mix_ref[...]).astype(BF16)
-    narrow[0:C, :] = dot(gated, dfirst_ref[...], TN)
+    narrow[0:C, :] = dot(gated_ref[...], dfirst_ref[...], TN)
     put_narrow(sscr, narrow, 16, n_dst, rows, 2)
     put_wide(sscr, wide, dot(n_ref[...], dproj_ref[...], TN), (8, 12), n_dst, rows)
     smalls = [small_ref[0:1, :], small_ref[1:2, :], dgain_e] + [dbias_e[h : h + 1] for h in range(HEADS)]
@@ -613,11 +619,17 @@
         *saved,
     )
     got = lax.ppermute(give, "dp", to_core)
+    normed = call(
+        first_norm_kernel,
+        [shape(tokens), shape(tokens), shape(tokens, BF16), shape(tokens, BF16)],
+        [],
+        first, gating, mix, args, small,
+    )
     send, dfirst, dproj = call(
         start_backward_kernel,
         [shape((n_dst, 32, C), BF16), shape(tokens, BF16), shape(hidden, BF16)],
         [(n_dst, 8, C), tokens, (HEADS * N, N), (C, C), (4 * C, C), (n_dst * 32, C), half, (2, 16, C)],
-        recv, keep, got, small, n, first, qkv, gating, mix, prob, args, parts, wo,
+        recv, keep, got, small, n, *normed, qkv, gating, mix, prob, args, parts, wo,
     )
     recv = swap(send)
     dn, dn_plane, part = call(

time: 116 us -> 116 us (level)
    pallas_call x10 -> x11, Pallas kernels: 11.1 us -> 11.3 us  [call(): pl.pallas_call(body, out_shape=out_shape, in_specs=[pl.BlockSpec(memory_s...]
where the time goes in v7:
time: 116 us
  blocking collectives  73.6 us (63%)
  starting transfers between devices  21.4 us (18%)
  Pallas kernels  11.3 us (10%)
  waiting for transfers between devices  8.59 us (7%)
    all_to_all x4, blocking collectives, swap(): lax.all_to_all(buffer, 'dap', split_axis=0, concat_axis=0, tiled=True)  73.6 us
    pallas_call x11, Pallas kernels, call(): pl.pallas_call(body, out_shape=out_shape, in_specs=[pl.BlockSpec(memory_s...  11.3 us
    ppermute x1, starting transfers between devices, local(): lax.ppermute(part, 'dp', to_core)  5.91 us
    all_to_all x1, waiting for transfers between devices, swap(): lax.all_to_all(buffer, 'dap', split_axis=0, concat_axis=0, tiled=True)  4.99 us
    all_to_all x1, starting transfers between devices, swap(): lax.all_to_all(buffer, 'dap', split_axis=0, concat_axis=0, tiled=True)  4.86 us
    ppermute x1, starting transfers between devices, local(): other = lax.ppermute(recv, 'dp', to_core)  4.43 us
    ppermute x1, starting transfers between devices, local(): got = lax.ppermute(give, 'dp', to_core)  3.56 us
    ppermute x1, starting transfers between devices, local(): far = lax.ppermute(part, 'dp', [(i, i ^ 2) for i in range(n_dp)])  2.62 us
  transfers between devices with their start and end apart: 5, of which 5 were waited for; matrix products, arithmetic and copies ran while one was open for 0% of the time, Pallas kernels for 1%

profile of v7, /device:TPU:1, one launch (start us, length us, event | category | flops | bytes accessed | tf_op | source)
XLA Modules:
  0.0 115.7 jit_solution(17611856937750717212)
XLA Ops:
  0.6 1.7 %shard_map.229 = (bf16[64,8,128]{2,1,0:T(8,128)(2,1)S(1)}, f32[8,128]{1,0:T(8,128)S(1)}, bf16[32,128]{1,0:T(8,128)(2,1)S(1)}, bf16[256,128]{1,0:T(8,128)(2,1)S(1...) custom-call(bf16[256,128]{1,0:T(8,128)(2,1)} %bitcast.13, ...), custom_call_target="tpu_custom_call" | custom-call | tf_op jit(solution)/shard_map/pallas_call | solution.py:559
  2.4 23.2 %all_to_all.25.recv_ref = bf16[64,8,128]{2,1,0:T(8,128)(2,1)S(1)} all-to-all(bf16[64,8,128]{2,1,0:T(8,128)(2,1)S(1)} %get-tuple-element.61), channel_id=1, replica_groups=mesh['dp'=4,'dap'=64] {'dap'}, dimensions={0} | all-to-all | bytes 262144 | tf_op jit(solution)/shard_map/all_to_all | solution.py:570
  25.6 0.0 copy-start.4
  25.6 0.0 copy-start.5
  25.6 1.0 shard_map.230
  26.6 0.0 copy-start.2
  26.6 0.0 copy-start.3
  26.6 14.7 %all_to_all.26.recv_ref = bf16[64,16,128]{2,1,0:T(8,128)(2,1)S(1)} all-to-all(bf16[64,16,128]{2,1,0:T(8,128)(2,1)S(1)} %get-tuple-element.70), channel_id=1, replica_groups=mesh['dp'=4,'dap'=64] {'dap'}, dimensions={0} | all-to-all | bytes 524288 | tf_op jit(solution)/shard_map/all_to_all | solution.py:570
  41.3 0.0 copy-done.4
  41.3 0.0 copy-done.5
  41.3 0.0 copy-done.2
  41.3 0.0 copy-done.3
  41.3 3.3 %shard_map.231 = (bf16[64,3,4,128]{3,2,1,0:T(4,128)(2,1)}, f32[8,128]{1,0:T(8,128)S(1)}, bf16[256,512]{1,0:T(8,128)(2,1)S(1)}, bf16[256,512]{1,0:T(8,128)(2,1)S(...) custom-call(bf16[64,16,128]{2,1,0:T(8,128)(2,1)S(1)} %all_to_all.26., ...), custom_call_target="tpu_custom_call" | custom-call | tf_op jit(solution)/shard_map/pallas_call | solution.py:559
  44.7 4.9 %all-to-all-start.2 = ((bf16[64,3,4,128]{3,2,1,0:T(4,128)(2,1)}), bf16[64,3,4,128]{3,2,1,0:T(4,128)(2,1)S(1)}, u32[]{:S(2)}, u32[]{:S(2)}) async-start(bf16[64,3,4,128]{3,2,1,0:T(4,128)(2,1)} %get-tuple-element.71), calls=%async_computation.2 | async-start | bytes 393216 | tf_op jit(solution)/shard_map/all_to_all | solution.py:570
  49.5 0.5 shard_map.232
  50.0 3.6 %collective-permute-start = (bf16[832,128]{1,0:T(8,128)(2,1)S(1)}, bf16[832,128]{1,0:T(8,128)(2,1)S(1)}, u32[]{:S(2)}, u32[]{:S(2)}) collective-permute-start(bf16[832,128]{1,0:T(8,128)(2,1)S(1)} %get-tuple-element.81), channel_id=1, source_target_pairs={{0,64},{64,0},{128,192},{192,128},{1,65},{65,1},{129,193},{193,129... | collective-permute-start | bytes 638984 | tf_op jit(solution)/shard_map/ppermute | solution.py:621
  53.6 0.2 shard_map.233
  53.8 0.9 collective-permute-done.got_ref
  54.7 5.0 %all-to-all-done.2.recv_ref = bf16[64,3,4,128]{3,2,1,0:T(4,128)(2,1)S(1)} async-done(((bf16[64,3,4,128]{3,2,1,0:T(4,128)(2,1)}), bf16[64,3,4,128]{3,2,1,0:T(4,128)(2,1)S(1)}, u32[]{:S(2)}, u32[]{:S(2)}) %all-to-all-start.2) | async-done | bytes 196640 | tf_op jit(solution)/shard_map/all_to_all | solution.py:570
  59.7 1.9 %shard_map.234 = (bf16[64,32,128]{2,1,0:T(8,128)(2,1)S(1)}, bf16[256,128]{1,0:T(8,128)(2,1)S(1)}, bf16[256,512]{1,0:T(8,128)(2,1)S(1)}) custom-call(bf16[64,3,4,128]{3,2,1,0:T(4,128)(2,1)S(1)} %all-to-all-done.2.recv_ref, f32[832,128]{1,0:T(8,128)S(1)} %get-tuple-element.80.keep_ref, bf16[832,128]{1,0:T(8,128)(2,1)S(1)} %collective-permute-done.got_ref, ...), custom_call_target="tpu_custom_call" | custom-call | tf_op jit(solution)/shard_map/pallas_call | solution.py:559
  61.6 0.0 copy-start
  61.6 0.0 copy-start.1
  61.6 18.9 %all_to_all.27.recv_ref = bf16[64,32,128]{2,1,0:T(8,128)(2,1)S(1)} all-to-all(bf16[64,32,128]{2,1,0:T(8,128)(2,1)S(1)} %get-tuple-element.91), channel_id=1, replica_groups=mesh['dp'=4,'dap'=64] {'dap'}, dimensions={0} | all-to-all | bytes 1048576 | tf_op jit(solution)/shard_map/all_to_all | solution.py:570
  80.6 0.0 copy-done
  80.6 0.0 copy-done.1
  80.6 0.4 shard_map.235
  80.9 5.9 %collective-permute-start.1 = (f32[32,128]{1,0:T(8,128)S(1)}, f32[32,128]{1,0:T(8,128)S(1)}, u32[]{:S(2)}, u32[]{:S(2)}) collective-permute-start(f32[32,128]{1,0:T(8,128)S(1)} %get-tuple-element.96.own_ref), channel_id=1, source_target_pairs={{0,64},{64,0},{128,192},{192,128},{1,65},{65,1},{129,193},{193,129... | collective-permute-start | bytes 49160 | tf_op jit(solution)/shard_map/ppermute | solution.py:641
  86.8 0.8 collective-permute-done.1.other_ref
  87.7 2.6 %collective-permute-start.2 = (f32[32,128]{1,0:T(8,128)S(1)}, f32[32,128]{1,0:T(8,128)S(1)}, u32[]{:S(2)}, u32[]{:S(2)}) collective-permute-start(f32[32,128]{1,0:T(8,128)S(1)} %shard_map.237.own_ref), channel_id=1, source_target_pairs={{0,128},{64,192},{128,0},{192,64},{1,129},{65,193},{129,1},{193,65... | collective-permute-start | bytes 49160 | tf_op jit(solution)/shard_map/ppermute | solution.py:642
  90.3 1.0 shard_map.236
  91.3 0.5 collective-permute-done.2.far_ref
  91.8 16.8 %all_to_all.28.recv_ref = bf16[64,24,128]{2,1,0:T(8,128)(2,1)S(1)} all-to-all(bf16[64,24,128]{2,1,0:T(8,128)(2,1)S(1)} %shard_map.238), channel_id=1, replica_groups=mesh['dp'=4,'dap'=64] {'dap'}, dimensions={0} | all-to-all | bytes 786432 | tf_op jit(solution)/shard_map/all_to_all | solution.py:570
  108.6 4.4 %collective-permute-start.3 = (bf16[64,24,128]{2,1,0:T(8,128)(2,1)S(1)}, bf16[64,24,128]{2,1,0:T(8,128)(2,1)S(1)}, u32[]{:S(2)}, u32[]{:S(2)}) collective-permute-start(bf16[64,24,128]{2,1,0:T(8,128)(2,1)S(1)} %all_to_all.28.recv_ref), channel_id=1, source_target_pairs={{0,64},{64,0},{128,192},{192,128},{1,65},{65,1},{129,193},{193,129... | collective-permute-start | bytes 1179656 | tf_op jit(solution)/shard_map/ppermute | solution.py:647
  113.0 1.3 %collective-permute-done.3.other_ref = bf16[64,24,128]{2,1,0:T(8,128)(2,1)S(1)} collective-permute-done((bf16[64,24,128]{2,1,0:T(8,128)(2,1)S(1)}, bf16[64,24,128]{2,1,0:T(8,128)(2,1)S(1)}, u32[]{:S(2)}, u32[]{:S(2)}) %collective-permute-start.3) | collective-permute-done | bytes 393248 | tf_op jit(solution)/shard_map/ppermute | solution.py:647
  114.4 1.3 %shard_map.239 = (f32[1,128]{1,0:T(1,128)}, f32[128,512]{1,0:T(8,128)}, f32[4,128]{1,0:T(4,128)}, f32[128,128]{1,0:T(8,128)}, f32[1,128]{1,0:T(1,128)}, /*index=...) custom-call(bf16[64,24,128]{2,1,0:T(8,128)(2,1)S(1)} %all_to_all.28., ...), custom_call_target="tpu_custom_call" | custom-call | tf_op jit(solution)/shard_map/pallas_call | solution.py:559
  (2 shorter events, 0.0 us)
Async XLA Ops:
  25.6 15.8 %copy-start.4 = (f32[512,128]{1,0:T(8,128)S(1)}, f32[512,128]{1,0:T(8,128)}, u32[]{:S(2)}) copy-start(f32[512,128]{1,0:T(8,128)} %wd_ref.1) | copy-start | bytes 786436
  25.6 15.8 %copy-start.5 = (f32[128,128]{1,0:T(8,128)S(1)}, f32[128,128]{1,0:T(8,128)}, u32[]{:S(2)}) copy-start(f32[128,128]{1,0:T(8,128)} %wo_ref.1) | copy-start | bytes 196612
  26.6 14.7 %copy-start.2 = (f32[128,512]{1,0:T(8,128)S(1)}, f32[128,512]{1,0:T(8,128)}, u32[]{:S(2)}) copy-start(f32[128,512]{1,0:T(8,128)} %w_ref.2) | copy-start | bytes 786436
  26.6 14.7 %copy-start.3 = (f32[128,512]{1,0:T(8,128)S(1)}, f32[128,512]{1,0:T(8,128)}, u32[]{:S(2)}) copy-start(f32[128,512]{1,0:T(8,128)} %wu_ref.1) | copy-start | bytes 786436
  44.7 15.0 %all-to-all-start.2 = ((bf16[64,3,4,128]{3,2,1,0:T(4,128)(2,1)}), bf16[64,3,4,128]{3,2,1,0:T(4,128)(2,1)S(1)}, u32[]{:S(2)}, u32[]{:S(2)}) async-start(bf16[64,3,4,128]{3,2,1,0:T(4,128)(2,1)} %get-tuple-element.71), calls=%async_computation.2 | async-start | bytes 393216 | tf_op jit(solution)/shard_map/all_to_all | solution.py:570
  50.0 4.7 %collective-permute-start = (bf16[832,128]{1,0:T(8,128)(2,1)S(1)}, bf16[832,128]{1,0:T(8,128)(2,1)S(1)}, u32[]{:S(2)}, u32[]{:S(2)}) collective-permute-start(bf16[832,128]{1,0:T(8,128)(2,1)S(1)} %get-tuple-element.81), channel_id=1, source_target_pairs={{0,64},{64,0},{128,192},{192,128},{1,65},{65,1},{129,193},{193,129... | collective-permute-start | bytes 638984 | tf_op jit(solution)/shard_map/ppermute | solution.py:621
  61.6 19.0 %copy-start = (f32[128,512]{1,0:T(8,128)S(1)}, f32[128,512]{1,0:T(8,128)}, u32[]{:S(2)}) copy-start(f32[128,512]{1,0:T(8,128)} %w_ref.3) | copy-start | bytes 786436
  61.6 19.0 %copy-start.1 = (bf16[1,2,128,128]{3,2,1,0:T(8,128)(2,1)S(1)}, bf16[1,2,128,128]{3,2,1,0:T(8,128)(2,1)}, u32[]{:S(2)}) copy-start(bf16[1,2,128,128]{3,2,1,0:T(8,128)(2,1)} %param.14) | copy-start | bytes 196612
  80.9 6.7 %collective-permute-start.1 = (f32[32,128]{1,0:T(8,128)S(1)}, f32[32,128]{1,0:T(8,128)S(1)}, u32[]{:S(2)}, u32[]{:S(2)}) collective-permute-start(f32[32,128]{1,0:T(8,128)S(1)} %get-tuple-element.96.own_ref), channel_id=1, source_target_pairs={{0,64},{64,0},{128,192},{192,128},{1,65},{65,1},{129,193},{193,129... | collective-permute-start | bytes 49160 | tf_op jit(solution)/shard_map/ppermute | solution.py:641
  87.7 4.1 %collective-permute-start.2 = (f32[32,128]{1,0:T(8,128)S(1)}, f32[32,128]{1,0:T(8,128)S(1)}, u32[]{:S(2)}, u32[]{:S(2)}) collective-permute-start(f32[32,128]{1,0:T(8,128)S(1)} %shard_map.237.own_ref), channel_id=1, source_target_pairs={{0,128},{64,192},{128,0},{192,64},{1,129},{65,193},{129,1},{193,65... | collective-permute-start | bytes 49160 | tf_op jit(solution)/shard_map/ppermute | solution.py:642
  108.6 5.8 %collective-permute-start.3 = (bf16[64,24,128]{2,1,0:T(8,128)(2,1)S(1)}, bf16[64,24,128]{2,1,0:T(8,128)(2,1)S(1)}, u32[]{:S(2)}, u32[]{:S(2)}) collective-permute-start(bf16[64,24,128]{2,1,0:T(8,128)(2,1)S(1)} %all_to_all.28.recv_ref), channel_id=1, source_target_pairs={{0,64},{64,0},{128,192},{192,128},{1,65},{65,1},{129,193},{193,129... | collective-permute-start | bytes 1179656 | tf_op jit(solution)/shard_map/ppermute | solution.py:647

commit v8 on v6

--- a/solution.py
+++ b/solution.py
@@ -442,7 +442,7 @@
     send_ref[...] = sscr[...].reshape(n_dst, rows, C).astype(BF16)
 
 
-def start_plane_kernel(recv_ref, dproj_ref, x_ref, w_ref, args_ref, parts_ref, dn_ref, dn_plane_ref, part_ref, p_ref):
+def start_plane_kernel(recv_ref, dproj_ref, x_ref, w_ref, args_ref, parts_ref, dn_ref, dn_plane_ref, part_ref, half_ref, p_ref):
     total = jnp.sum(recv_ref[...].astype(F32), 0)
     xhat, _ = ln_stats(x_ref[...].astype(F32))
     n = (xhat * args_ref[G_S, :]).astype(BF16)
@@ -459,8 +459,8 @@
     part_ref[0:11, :] = total[8:19]
     part_ref[11:15, :] = dbias
     part_ref[15:16, :] = jnp.sum((dn_plane + dn.astype(F32)) * xhat, 0, keepdims=True)
-    part_ref[16 : 16 + HALF, :] = total[19 : 19 + HALF]
-    part_ref[16 + HALF : 32, :] = jnp.zeros((16 - HALF, C), F32)
+    half_ref[0:HALF, :] = total[19 : 19 + HALF]
+    half_ref[HALF:16, :] = jnp.zeros((16 - HALF, C), F32)
 
 
 def grad_kernel(dn_ref, dn_plane_ref, dfirst_ref, x_ref, args_ref, grad_ref):
@@ -470,9 +470,9 @@
     grad_ref[...] = (dfirst_ref[...].astype(F32) + dx + dx_plane).astype(BF16)
 
 
-def core_sum_kernel(own_ref, other_ref, out_ref):
-    out_ref[0:16, :] = own_ref[0:16, :] + other_ref[0:16, :]
-    out_ref[16:32, :] = own_ref[16:32, :]
+def core_sum_kernel(own_ref, other_ref, half_ref, out_ref):
+    out_ref[0:16, :] = own_ref[...] + other_ref[...]
+    out_ref[16:32, :] = half_ref[...]
 
 
 def spread_kernel(own_ref, far_ref, out_ref, scr):
@@ -620,13 +620,13 @@
         recv, keep, got, small, n, first, qkv, gating, mix, prob, args, parts, wo,
     )
     recv = swap(send)
-    dn, dn_plane, part = call(
+    dn, dn_plane, part, half_part = call(
         start_plane_kernel,
-        [shape(tokens, BF16), shape(tokens, BF16), shape((32, C))],
+        [shape(tokens, BF16), shape(tokens, BF16), shape((16, C)), shape((16, C))],
         [(2, 16, C)],
         recv, dproj, x, proj_start, args, parts,
     )
-    part = call(core_sum_kernel, shape((32, C)), [], part, lax.ppermute(part, "dp", to_core))
+    part = call(core_sum_kernel, shape((32, C)), [], part, lax.ppermute(part, "dp", to_core), half_part)
     far = lax.ppermute(part, "dp", [(i, i ^ 2) for i in range(n_dp)])
     grad = call(grad_kernel, shape(tokens, BF16), [], dn, dn_plane, dfirst, x, args)
     grad, far = lax.optimization_barrier((grad, far))

time: 116 us -> 116 us (level)
  no operation moved by 1% of the time
where the time goes in v8:
time: 116 us
  blocking collectives  73.7 us (64%)
  starting transfers between devices  21.4 us (18%)
  Pallas kernels  11.1 us (10%)
  waiting for transfers between devices  8.78 us (8%)
    all_to_all x4, blocking collectives, swap(): lax.all_to_all(buffer, 'dap', split_axis=0, concat_axis=0, tiled=True)  73.7 us
    pallas_call x10, Pallas kernels, call(): pl.pallas_call(body, out_shape=out_shape, in_specs=[pl.BlockSpec(memory_s...  11.1 us
    ppermute x1, starting transfers between devices, local(): lax.ppermute(part, 'dp', to_core)  5.91 us
    all_to_all x1, waiting for transfers between devices, swap(): lax.all_to_all(buffer, 'dap', split_axis=0, concat_axis=0, tiled=True)  4.99 us
    all_to_all x1, starting transfers between devices, swap(): lax.all_to_all(buffer, 'dap', split_axis=0, concat_axis=0, tiled=True)  4.86 us
    ppermute x1, starting transfers between devices, local(): other = lax.ppermute(recv, 'dp', to_core)  4.43 us
    ppermute x1, starting transfers between devices, local(): got = lax.ppermute(give, 'dp', to_core)  3.56 us
    ppermute x1, starting transfers between devices, local(): far = lax.ppermute(part, 'dp', [(i, i ^ 2) for i in range(n_dp)])  2.62 us
  transfers between devices with their start and end apart: 5, of which 5 were waited for; matrix products, arithmetic and copies ran while one was open for 0% of the time, Pallas kernels for 1%

profile of v8, /device:TPU:1, one launch (start us, length us, event | category | flops | bytes accessed | tf_op | source)
XLA Modules:
  0.0 115.7 jit_solution(7186775537593575935)
XLA Ops:
  0.6 1.7 %shard_map.229 = (bf16[64,8,128]{2,1,0:T(8,128)(2,1)S(1)}, f32[8,128]{1,0:T(8,128)S(1)}, bf16[32,128]{1,0:T(8,128)(2,1)S(1)}, bf16[256,128]{1,0:T(8,128)(2,1)S(1...) custom-call(bf16[256,128]{1,0:T(8,128)(2,1)} %bitcast.13, ...), custom_call_target="tpu_custom_call" | custom-call | tf_op jit(solution)/shard_map/pallas_call | solution.py:553
  2.4 23.2 %all_to_all.25.recv_ref = bf16[64,8,128]{2,1,0:T(8,128)(2,1)S(1)} all-to-all(bf16[64,8,128]{2,1,0:T(8,128)(2,1)S(1)} %get-tuple-element.58), channel_id=1, replica_groups=mesh['dp'=4,'dap'=64] {'dap'}, dimensions={0} | all-to-all | bytes 262144 | tf_op jit(solution)/shard_map/all_to_all | solution.py:564
  25.6 0.0 copy-start.4
  25.6 0.0 copy-start.5
  25.6 1.0 shard_map.230
  26.6 0.0 copy-start.2
  26.6 0.0 copy-start.3
  26.6 14.7 %all_to_all.26.recv_ref = bf16[64,16,128]{2,1,0:T(8,128)(2,1)S(1)} all-to-all(bf16[64,16,128]{2,1,0:T(8,128)(2,1)S(1)} %get-tuple-element.67), channel_id=1, replica_groups=mesh['dp'=4,'dap'=64] {'dap'}, dimensions={0} | all-to-all | bytes 524288 | tf_op jit(solution)/shard_map/all_to_all | solution.py:564
  41.3 0.0 copy-done.4
  41.3 0.0 copy-done.5
  41.3 0.0 copy-done.2
  41.3 0.0 copy-done.3
  41.3 3.3 %shard_map.231 = (bf16[64,3,4,128]{3,2,1,0:T(4,128)(2,1)}, f32[8,128]{1,0:T(8,128)S(1)}, bf16[256,512]{1,0:T(8,128)(2,1)S(1)}, bf16[256,512]{1,0:T(8,128)(2,1)S(...) custom-call(bf16[64,16,128]{2,1,0:T(8,128)(2,1)S(1)} %all_to_all.26., ...), custom_call_target="tpu_custom_call" | custom-call | tf_op jit(solution)/shard_map/pallas_call | solution.py:553
  44.7 4.9 %all-to-all-start.2 = ((bf16[64,3,4,128]{3,2,1,0:T(4,128)(2,1)}), bf16[64,3,4,128]{3,2,1,0:T(4,128)(2,1)S(1)}, u32[]{:S(2)}, u32[]{:S(2)}) async-start(bf16[64,3,4,128]{3,2,1,0:T(4,128)(2,1)} %get-tuple-element.68), calls=%async_computation.2 | async-start | bytes 393216 | tf_op jit(solution)/shard_map/all_to_all | solution.py:564
  49.5 0.5 shard_map.232
  50.0 3.6 %collective-permute-start = (bf16[832,128]{1,0:T(8,128)(2,1)S(1)}, bf16[832,128]{1,0:T(8,128)(2,1)S(1)}, u32[]{:S(2)}, u32[]{:S(2)}) collective-permute-start(bf16[832,128]{1,0:T(8,128)(2,1)S(1)} %get-tuple-element.78), channel_id=1, source_target_pairs={{0,64},{64,0},{128,192},{192,128},{1,65},{65,1},{129,193},{193,129... | collective-permute-start | bytes 638984 | tf_op jit(solution)/shard_map/ppermute | solution.py:615
  53.6 1.1 collective-permute-done.got_ref
  54.7 5.0 %all-to-all-done.2.recv_ref = bf16[64,3,4,128]{3,2,1,0:T(4,128)(2,1)S(1)} async-done(((bf16[64,3,4,128]{3,2,1,0:T(4,128)(2,1)}), bf16[64,3,4,128]{3,2,1,0:T(4,128)(2,1)S(1)}, u32[]{:S(2)}, u32[]{:S(2)}) %all-to-all-start.2) | async-done | bytes 196640 | tf_op jit(solution)/shard_map/all_to_all | solution.py:564
  59.7 1.9 %shard_map.233 = (bf16[64,32,128]{2,1,0:T(8,128)(2,1)S(1)}, bf16[256,128]{1,0:T(8,128)(2,1)S(1)}, bf16[256,512]{1,0:T(8,128)(2,1)S(1)}) custom-call(bf16[64,3,4,128]{3,2,1,0:T(4,128)(2,1)S(1)} %all-to-all-done.2.recv_ref, f32[832,128]{1,0:T(8,128)S(1)} %get-tuple-element.77.keep_ref, bf16[832,128]{1,0:T(8,128)(2,1)S(1)} %collective-permute-done.got_ref, ...), custom_call_target="tpu_custom_call" | custom-call | tf_op jit(solution)/shard_map/pallas_call | solution.py:553
  61.6 0.0 copy-start
  61.6 0.0 copy-start.1
  61.6 19.0 %all_to_all.27.recv_ref = bf16[64,32,128]{2,1,0:T(8,128)(2,1)S(1)} all-to-all(bf16[64,32,128]{2,1,0:T(8,128)(2,1)S(1)} %get-tuple-element.84), channel_id=1, replica_groups=mesh['dp'=4,'dap'=64] {'dap'}, dimensions={0} | all-to-all | bytes 1048576 | tf_op jit(solution)/shard_map/all_to_all | solution.py:564
  80.6 0.0 copy-done
  80.6 0.0 copy-done.1
  80.6 0.4 shard_map.234
  80.9 5.9 %collective-permute-start.1 = (f32[16,128]{1,0:T(8,128)S(1)}, f32[16,128]{1,0:T(8,128)S(1)}, u32[]{:S(2)}, u32[]{:S(2)}) collective-permute-start(f32[16,128]{1,0:T(8,128)S(1)} %get-tuple-element.89.own_ref), channel_id=1, source_target_pairs={{0,64},{64,0},{128,192},{192,128},{1,65},{65,1},{129,193},{193,129... | collective-permute-start | bytes 24584 | tf_op jit(solution)/shard_map/ppermute | solution.py:629
  86.9 0.8 collective-permute-done.1.other_ref
  87.7 2.6 %collective-permute-start.2 = (f32[32,128]{1,0:T(8,128)S(1)}, f32[32,128]{1,0:T(8,128)S(1)}, u32[]{:S(2)}, u32[]{:S(2)}) collective-permute-start(f32[32,128]{1,0:T(8,128)S(1)} %shard_map.236.own_ref), channel_id=1, source_target_pairs={{0,128},{64,192},{128,0},{192,64},{1,129},{65,193},{129,1},{193,65... | collective-permute-start | bytes 49160 | tf_op jit(solution)/shard_map/ppermute | solution.py:630
  90.3 1.0 shard_map.235
  91.3 0.5 collective-permute-done.2.far_ref
  91.8 16.8 %all_to_all.28.recv_ref = bf16[64,24,128]{2,1,0:T(8,128)(2,1)S(1)} all-to-all(bf16[64,24,128]{2,1,0:T(8,128)(2,1)S(1)} %shard_map.237), channel_id=1, replica_groups=mesh['dp'=4,'dap'=64] {'dap'}, dimensions={0} | all-to-all | bytes 786432 | tf_op jit(solution)/shard_map/all_to_all | solution.py:564
  108.6 4.4 %collective-permute-start.3 = (bf16[64,24,128]{2,1,0:T(8,128)(2,1)S(1)}, bf16[64,24,128]{2,1,0:T(8,128)(2,1)S(1)}, u32[]{:S(2)}, u32[]{:S(2)}) collective-permute-start(bf16[64,24,128]{2,1,0:T(8,128)(2,1)S(1)} %all_to_all.28.recv_ref), channel_id=1, source_target_pairs={{0,64},{64,0},{128,192},{192,128},{1,65},{65,1},{129,193},{193,129... | collective-permute-start | bytes 1179656 | tf_op jit(solution)/shard_map/ppermute | solution.py:635
  113.0 1.3 %collective-permute-done.3.other_ref = bf16[64,24,128]{2,1,0:T(8,128)(2,1)S(1)} collective-permute-done((bf16[64,24,128]{2,1,0:T(8,128)(2,1)S(1)}, bf16[64,24,128]{2,1,0:T(8,128)(2,1)S(1)}, u32[]{:S(2)}, u32[]{:S(2)}) %collective-permute-start.3) | collective-permute-done | bytes 393248 | tf_op jit(solution)/shard_map/ppermute | solution.py:635
  114.4 1.3 %shard_map.238 = (f32[1,128]{1,0:T(1,128)}, f32[128,512]{1,0:T(8,128)}, f32[4,128]{1,0:T(4,128)}, f32[128,128]{1,0:T(8,128)}, f32[1,128]{1,0:T(1,128)}, /*index=...) custom-call(bf16[64,24,128]{2,1,0:T(8,128)(2,1)S(1)} %all_to_all.28., ...), custom_call_target="tpu_custom_call" | custom-call | tf_op jit(solution)/shard_map/pallas_call | solution.py:553
  (2 shorter events, 0.0 us)
Async XLA Ops:
  25.6 15.8 %copy-start.4 = (f32[512,128]{1,0:T(8,128)S(1)}, f32[512,128]{1,0:T(8,128)}, u32[]{:S(2)}) copy-start(f32[512,128]{1,0:T(8,128)} %wd_ref.1) | copy-start | bytes 786436
  25.6 15.8 %copy-start.5 = (f32[128,128]{1,0:T(8,128)S(1)}, f32[128,128]{1,0:T(8,128)}, u32[]{:S(2)}) copy-start(f32[128,128]{1,0:T(8,128)} %wo_ref.1) | copy-start | bytes 196612
  26.6 14.7 %copy-start.2 = (f32[128,512]{1,0:T(8,128)S(1)}, f32[128,512]{1,0:T(8,128)}, u32[]{:S(2)}) copy-start(f32[128,512]{1,0:T(8,128)} %w_ref.2) | copy-start | bytes 786436
  26.6 14.7 %copy-start.3 = (f32[128,512]{1,0:T(8,128)S(1)}, f32[128,512]{1,0:T(8,128)}, u32[]{:S(2)}) copy-start(f32[128,512]{1,0:T(8,128)} %wu_ref.1) | copy-start | bytes 786436
  44.7 15.0 %all-to-all-start.2 = ((bf16[64,3,4,128]{3,2,1,0:T(4,128)(2,1)}), bf16[64,3,4,128]{3,2,1,0:T(4,128)(2,1)S(1)}, u32[]{:S(2)}, u32[]{:S(2)}) async-start(bf16[64,3,4,128]{3,2,1,0:T(4,128)(2,1)} %get-tuple-element.68), calls=%async_computation.2 | async-start | bytes 393216 | tf_op jit(solution)/shard_map/all_to_all | solution.py:564
  50.0 4.7 %collective-permute-start = (bf16[832,128]{1,0:T(8,128)(2,1)S(1)}, bf16[832,128]{1,0:T(8,128)(2,1)S(1)}, u32[]{:S(2)}, u32[]{:S(2)}) collective-permute-start(bf16[832,128]{1,0:T(8,128)(2,1)S(1)} %get-tuple-element.78), channel_id=1, source_target_pairs={{0,64},{64,0},{128,192},{192,128},{1,65},{65,1},{129,193},{193,129... | collective-permute-start | bytes 638984 | tf_op jit(solution)/shard_map/ppermute | solution.py:615
  61.6 19.0 %copy-start = (f32[128,512]{1,0:T(8,128)S(1)}, f32[128,512]{1,0:T(8,128)}, u32[]{:S(2)}) copy-start(f32[128,512]{1,0:T(8,128)} %w_ref.3) | copy-start | bytes 786436
  61.6 19.0 %copy-start.1 = (bf16[1,2,128,128]{3,2,1,0:T(8,128)(2,1)S(1)}, bf16[1,2,128,128]{3,2,1,0:T(8,128)(2,1)}, u32[]{:S(2)}) copy-start(bf16[1,2,128,128]{3,2,1,0:T(8,128)(2,1)} %param.14) | copy-start | bytes 196612
  80.9 6.7 %collective-permute-start.1 = (f32[16,128]{1,0:T(8,128)S(1)}, f32[16,128]{1,0:T(8,128)S(1)}, u32[]{:S(2)}, u32[]{:S(2)}) collective-permute-start(f32[16,128]{1,0:T(8,128)S(1)} %get-tuple-element.89.own_ref), channel_id=1, source_target_pairs={{0,64},{64,0},{128,192},{192,128},{1,65},{65,1},{129,193},{193,129... | collective-permute-start | bytes 24584 | tf_op jit(solution)/shard_map/ppermute | solution.py:629
  87.7 4.1 %collective-permute-start.2 = (f32[32,128]{1,0:T(8,128)S(1)}, f32[32,128]{1,0:T(8,128)S(1)}, u32[]{:S(2)}, u32[]{:S(2)}) collective-permute-start(f32[32,128]{1,0:T(8,128)S(1)} %shard_map.236.own_ref), channel_id=1, source_target_pairs={{0,128},{64,192},{128,0},{192,64},{1,129},{65,193},{129,1},{193,65... | collective-permute-start | bytes 49160 | tf_op jit(solution)/shard_map/ppermute | solution.py:630
  108.6 5.8 %collective-permute-start.3 = (bf16[64,24,128]{2,1,0:T(8,128)(2,1)S(1)}, bf16[64,24,128]{2,1,0:T(8,128)(2,1)S(1)}, u32[]{:S(2)}, u32[]{:S(2)}) collective-permute-start(bf16[64,24,128]{2,1,0:T(8,128)(2,1)S(1)} %all_to_all.28.recv_ref), channel_id=1, source_target_pairs={{0,64},{64,0},{128,192},{192,128},{1,65},{65,1},{129,193},{193,129... | collective-permute-start | bytes 1179656 | tf_op jit(solution)/shard_map/ppermute | solution.py:635
